TPU v7x, 512 devices: a whole 4x8x8 slice. The times are simulated.
512 devices in a mesh: space: 8 (over z), vel: 64 (over x, y, core).
Axes of the slice: x: 4, y: 8, z: 8, core: 2. Of those that a mesh axis runs over, the one named last changes fastest.
Arguments:
- distribution: float32 [32768, 2048], P('vel', 'space'), may hold values from 0.1 to 32, as said below
- normals: float32 [4, 3, 2048], P(None, None, 'space'), may hold values from -0.3 to 0.3
- adjacency: int32 [4, 2048], P(None, 'space'), may hold values from 0 to 2047, as said below
- send_list: int32 [8, 8, 256], P('space'), may hold values from 0 to 255
- block_counts: int32 [8, 8], P(None, 'space'), may hold values from 0 to 2, as said below
Outputs:
- relaxed: float32 [32768, 2048], P('vel', 'space')
- fields: float32 [13, 2048], P(None, 'space')
Inputs may be any that keep to these rules, and one draw needn't show every extreme that they name: `adjacency`: every entry of 256 or more names a position below 128 times the sum of block_counts over the senders to its group. `block_counts`: no group sends to itself; every other pair has at least one block; one receiving group gets 2 blocks from every other group. `distribution`: Positive.
All inputs are finite; a program needn't handle non-finite values.
Results may differ from a plain program's by a relative error of at most 0.00011.
Values sent between devices are 32-bit elements; how exact they have to be, the bound alone decides.
No kernel may reach another device: no remote copies, remote signals or barrier semaphores. Data moves between devices by JAX's collectives and lax.ppermute only.
A program may use at most 64 MiB of HBM per device.

v0:
```python
import jax
import jax.numpy as jnp
from jax import lax
from jax.sharding import PartitionSpec as P

VXY = 32
TILE = 128
BND = 256
ITERS = 2


spacing = 0.3
ellipsoid_mix = -0.25
prandtl = 0.8
visc_power = 0.26
time_step = 0.025


def sent_to_all(x, axis):
    copies = jnp.broadcast_to(x, (lax.axis_size(axis), *x.shape))
    return lax.all_to_all(copies, axis, split_axis=0, concat_axis=0, tiled=True)


def laid_out(pieces, dim):
    pieces = jnp.moveaxis(pieces, 0, dim)
    shape = pieces.shape
    return pieces.reshape(*shape[:dim], shape[dim] * shape[dim + 1], *shape[dim + 2 :])


def gather_directly(x, axis, dim):
    pieces = sent_to_all(x, axis)
    return laid_out(pieces, dim)


def of_everyone(x, axis):
    return sent_to_all(x, axis).sum(axis=0)


def velocity_nodes(vel_index, z_count):
    comp_x = (vel_index % VXY).astype(jnp.float32)
    comp_y = (vel_index // VXY % VXY).astype(jnp.float32)
    comp_z = (vel_index // (VXY * VXY)).astype(jnp.float32)
    centre = (VXY - 1) / 2.0
    return jnp.stack(
        [
            (comp_x - centre) * spacing,
            (comp_y - centre) * spacing,
            (comp_z - (z_count - 1) / 2.0) * spacing,
        ]
    )


def moment_rows(velocity):
    comp_x, comp_y, comp_z = (velocity[0], velocity[1], velocity[2])
    squared = comp_x * comp_x + comp_y * comp_y + comp_z * comp_z
    return jnp.stack(
        [
            jnp.ones_like(comp_x),
            comp_x,
            comp_y,
            comp_z,
            comp_x * comp_x,
            comp_y * comp_y,
            comp_z * comp_z,
            comp_x * comp_y,
            comp_x * comp_z,
            comp_y * comp_z,
            comp_x * squared,
            comp_y * squared,
            comp_z * squared,
        ]
    )


def quad_rows(velocity):
    comp_x, comp_y, comp_z = (velocity[0], velocity[1], velocity[2])
    return jnp.stack(
        [
            comp_x * comp_x,
            comp_y * comp_y,
            comp_z * comp_z,
            comp_x * comp_y,
            comp_x * comp_z,
            comp_y * comp_z,
            comp_x,
            comp_y,
            comp_z,
            jnp.ones_like(comp_x),
        ]
    )


def macroscopic(moments):
    density = moments[0]
    mean_x = moments[1] / density
    mean_y = moments[2] / density
    mean_z = moments[3] / density
    second = moments[4:10] / density[None, :]
    third = moments[10:13] / density[None, :]
    theta_xx = second[0] - mean_x * mean_x
    theta_yy = second[1] - mean_y * mean_y
    theta_zz = second[2] - mean_z * mean_z
    theta_xy = second[3] - mean_x * mean_y
    theta_xz = second[4] - mean_x * mean_z
    theta_yz = second[5] - mean_y * mean_z
    temper = (theta_xx + theta_yy + theta_zz) / 3.0
    trace_b = second[0] + second[1] + second[2]
    bu_x = second[0] * mean_x + second[3] * mean_y + second[4] * mean_z
    bu_y = second[3] * mean_x + second[1] * mean_y + second[5] * mean_z
    bu_z = second[4] * mean_x + second[5] * mean_y + second[2] * mean_z
    mean_sq = mean_x * mean_x + mean_y * mean_y + mean_z * mean_z
    flux_x = 0.5 * (third[0] - 2.0 * bu_x - mean_x * trace_b + 2.0 * mean_x * mean_sq)
    flux_y = 0.5 * (third[1] - 2.0 * bu_y - mean_y * trace_b + 2.0 * mean_y * mean_sq)
    flux_z = 0.5 * (third[2] - 2.0 * bu_z - mean_z * trace_b + 2.0 * mean_z * mean_sq)
    iso_part = (1.0 - ellipsoid_mix) * temper
    lam_xx = iso_part + ellipsoid_mix * theta_xx
    lam_yy = iso_part + ellipsoid_mix * theta_yy
    lam_zz = iso_part + ellipsoid_mix * theta_zz
    lam_xy = ellipsoid_mix * theta_xy
    lam_xz = ellipsoid_mix * theta_xz
    lam_yz = ellipsoid_mix * theta_yz
    cof_xx = lam_yy * lam_zz - lam_yz * lam_yz
    cof_xy = lam_yz * lam_xz - lam_xy * lam_zz
    cof_xz = lam_xy * lam_yz - lam_yy * lam_xz
    cof_yy = lam_xx * lam_zz - lam_xz * lam_xz
    cof_yz = lam_xy * lam_xz - lam_xx * lam_yz
    cof_zz = lam_xx * lam_yy - lam_xy * lam_xy
    determinant = lam_xx * cof_xx + lam_xy * cof_xy + lam_xz * cof_xz
    inv_xx = cof_xx / determinant
    inv_yy = cof_yy / determinant
    inv_zz = cof_zz / determinant
    inv_xy = cof_xy / determinant
    inv_xz = cof_xz / determinant
    inv_yz = cof_yz / determinant
    lin_x = inv_xx * mean_x + inv_xy * mean_y + inv_xz * mean_z
    lin_y = inv_xy * mean_x + inv_yy * mean_y + inv_yz * mean_z
    lin_z = inv_xz * mean_x + inv_yz * mean_y + inv_zz * mean_z
    offset = mean_x * lin_x + mean_y * lin_y + mean_z * lin_z
    collide = prandtl * density * jnp.exp(visc_power * jnp.log(temper))
    return jnp.stack(
        [
            density,
            mean_x,
            mean_y,
            mean_z,
            theta_xx,
            theta_yy,
            theta_zz,
            theta_xy,
            theta_xz,
            theta_yz,
            flux_x,
            flux_y,
            flux_z,
            inv_xx,
            inv_yy,
            inv_zz,
            2.0 * inv_xy,
            2.0 * inv_xz,
            2.0 * inv_yz,
            -2.0 * lin_x,
            -2.0 * lin_y,
            -2.0 * lin_z,
            offset,
            collide,
        ]
    )


def ghost_slots(adjacency, counts, cells, groups, slot_count):
    ends = jnp.cumsum(counts) * TILE
    starts = ends - counts * TILE
    is_local = adjacency < cells
    position = jnp.maximum(adjacency - cells, 0)
    source = jnp.sum((ends[:, None, None] <= position[None]).astype(jnp.int32), axis=0)
    source = jnp.minimum(source, groups - 1)
    group_ids = jnp.arange(groups, dtype=jnp.int32)[:, None, None]
    chosen = jnp.sum(jnp.where(group_ids == source[None], starts[:, None, None], 0), axis=0)
    slot_pos = jnp.clip(position - chosen, 0, slot_count - 1)
    return (is_local, source, slot_pos)


def relax(current, neighbours, velocity, normals, params, norm_z, equilibrium):
    gauss = params[0][None, :] * equilibrium / norm_z[None, :]
    outflow = jnp.zeros(current.shape, jnp.float32)
    inflow = jnp.zeros(current.shape, jnp.float32)
    for side in range(normals.shape[0]):
        normal_speed = (
            velocity[0][:, None] * normals[side, 0][None, :]
            + velocity[1][:, None] * normals[side, 1][None, :]
            + velocity[2][:, None] * normals[side, 2][None, :]
        )
        outflow = outflow + jnp.maximum(normal_speed, 0.0)
        inflow = inflow + jnp.minimum(normal_speed, 0.0) * neighbours[side]
    return current + time_step * (
        params[23][None, :] * (gauss - current) - outflow * current - inflow
    )


def per_device(distribution, normals, adjacency, send_list, block_counts):
    vel_local = distribution.shape[0]
    cells = distribution.shape[1]
    total_vel = vel_local * lax.axis_size("vel")
    z_count = total_vel // (VXY * VXY)
    groups = send_list.shape[1]
    slot_count = send_list.shape[2]
    vel_index = lax.axis_index("vel") * vel_local + jnp.arange(vel_local, dtype=jnp.int32)
    velocity = velocity_nodes(vel_index, z_count)
    moment_table = moment_rows(velocity)
    quad_table = quad_rows(velocity).T
    is_local, source, slot_pos = ghost_slots(
        adjacency, block_counts[:, 0], cells, groups, slot_count
    )
    ghost_index = source * slot_count + slot_pos
    local_index = jnp.where(is_local, adjacency, 0)
    list_all = gather_directly(send_list, "space", 0)
    column = lax.dynamic_index_in_dim(list_all, lax.axis_index("space"), 1, keepdims=False)
    pull_index = (jnp.arange(groups, dtype=jnp.int32)[:, None] * BND + column).reshape(-1)

    def reduce_moments(current):
        partial_value = (
            jnp.dot(
                moment_table,
                current,
                precision=lax.Precision.HIGHEST,
                preferred_element_type=jnp.float32,
            )
            / total_vel
        )
        return macroscopic(of_everyone(partial_value, "vel"))

    current = distribution
    for iteration in range(ITERS):
        params = reduce_moments(current)
        border = lax.all_gather(current, "space", axis=1, tiled=True)
        ghosts = jnp.take(border, pull_index, axis=1)
        exponent = jnp.dot(
            quad_table,
            params[13:23],
            precision=lax.Precision.HIGHEST,
            preferred_element_type=jnp.float32,
        )
        equilibrium = jnp.exp(-0.5 * exponent)
        norm_z = of_everyone(jnp.sum(equilibrium, axis=0) / total_vel, "vel")
        neighbours = [
            jnp.where(
                is_local[side][None, :],
                jnp.take(current, local_index[side], axis=1),
                jnp.take(ghosts, ghost_index[side], axis=1),
            )
            for side in range(normals.shape[0])
        ]
        current = relax(current, neighbours, velocity, normals, params, norm_z, equilibrium)
    final = reduce_moments(current)
    return (current, final[:13])


def solution(mesh):
    placed = (
        P("vel", "space"),
        P(None, None, "space"),
        P(None, "space"),
        P("space", None, None),
        P(None, "space"),
    )
    return jax.shard_map(
        per_device,
        mesh=mesh,
        in_specs=placed,
        out_specs=(P("vel", "space"), P(None, "space")),
        check_vma=False,
    )
```

profile of v0, /device:TPU:1, one launch (start us, length us, event | category | flops | bytes accessed | tf_op | source)
XLA Modules:
  0.0 278.8 jit_solution(2723023578636813399)
XLA Ops:
  7.2 2.0 copy.61
  10.7 10.9 %all-to-all-start.2 = ((s32[8,1,8,256]{3,2,1,0:T(8,128)}), s32[8,1,8,256]{3,2,1,0:T(8,128)S(1)}, u32[]{:S(2)}, u32[]{:S(2)}) async-start(s32[8,1,8,256]{3,2,1,0:T(8,128)} %broadcast_in_dim.117), calls=%async_computation.2 | async-start | bytes 131072 | tf_op jit(solution)/shard_map/all_to_all | solution.py:21
  33.4 11.1 %all-to-all-start = ((f32[64,13,256]{2,1,0:T(8,128)}), f32[64,13,256]{2,1,0:T(8,128)S(1)}, u32[]{:S(2)}, u32[]{:S(2)}) async-start(f32[64,13,256]{2,1,0:T(8,128)} %broadcast_in_dim.112), calls=%async_computation | async-start | bytes 2097152 | tf_op jit(solution)/shard_map/all_to_all | solution.py:21
  44.6 28.4 %all-to-all-done = f32[64,13,256]{2,1,0:T(8,128)S(1)} async-done(((f32[64,13,256]{2,1,0:T(8,128)}), f32[64,13,256]{2,1,0:T(8,128)S(1)}, u32[]{:S(2)}, u32[]{:S(2)}) %all-to-all-start) | async-done | bytes 852000 | tf_op jit(solution)/shard_map/all_to_all | solution.py:21
  74.6 6.2 %all-to-all-start.1 = ((f32[64,1,256]{2,1,0:T(1,128)}), f32[64,1,256]{2,1,0:T(1,128)S(1)}, u32[]{:S(2)}, u32[]{:S(2)}) async-start(f32[64,1,256]{2,1,0:T(1,128)} %broadcast_in_dim.113), calls=%async_computation.1 | async-start | bytes 131072 | tf_op jit(solution)/shard_map/all_to_all | solution.py:21
  81.1 9.5 %all-to-all-done.1 = f32[64,1,256]{2,1,0:T(1,128)S(1)} async-done(((f32[64,1,256]{2,1,0:T(1,128)}), f32[64,1,256]{2,1,0:T(1,128)S(1)}, u32[]{:S(2)}, u32[]{:S(2)}) %all-to-all-start.1) | async-done | bytes 65568 | tf_op jit(solution)/shard_map/all_to_all | solution.py:21
  90.8 11.7 %gather_fusion.1 = f32[2048,512]{1,0:T(8,128)} fusion(f32[512,2048]{0,1:T(8,128)} %all-gather.3.cloned.1.call-done, s32[2048]{0:T(1024)S(1)} %broadcast_clamp_fusion), kind=kCustom, calls=%fused_computation.1.clone | custom fusion | bytes 8396800 | tf_op jit(solution)/shard_map/jit(_take)/gather | solution.py:236
  102.5 3.8 %select_bitcast_fusion.1 = f32[512,2048]{0,1:T(8,128)} fusion(f32[2048,512]{1,0:T(8,128)} %gather_fusion.1, pred[2048]{0:T(1024)(128)(4,1)S(1)} %compare_and_fusion), kind=kLoop, calls=%fused_computation.19 | loop fusion | flops 1048576 | bytes 8390656 | tf_op jit(solution)/shard_map/jit(_take)/select_n | solution.py:236
  106.3 3.4 %gather_fusion.8 = f32[256,512]{1,0:T(8,128)S(1)} fusion(f32[512,2048]{0,1:T(8,128)} %select_bitcast_fusion.1, s32[1024]{0:T(1024)S(1)} %pad_clamp_fusion), kind=kCustom, calls=%fused_computation.13.clone | custom fusion | bytes 1049600 | tf_op jit(solution)/shard_map/jit(_take)/gather | solution.py:249
  110.7 3.4 %gather_fusion.6 = f32[256,512]{1,0:T(8,128)S(1)} fusion(f32[512,2048]{0,1:T(8,128)} %select_bitcast_fusion.1, s32[1024]{0:T(1024)S(1)} %pad_clamp_fusion.2), kind=kCustom, calls=%fused_computation.12.clone | custom fusion | bytes 1049600 | tf_op jit(solution)/shard_map/jit(_take)/gather | solution.py:249
  115.1 4.2 %gather_fusion.4 = f32[256,512]{1,0:T(8,128)} fusion(f32[512,2048]{0,1:T(8,128)} %select_bitcast_fusion.1, s32[1024]{0:T(1024)S(1)} %pad_clamp_fusion.4), kind=kCustom, calls=%fused_computation.11.clone | custom fusion | bytes 1049600 | tf_op jit(solution)/shard_map/jit(_take)/gather | solution.py:249
  119.3 2.1 copy.67
  121.4 4.2 %gather_fusion.2 = f32[256,512]{1,0:T(8,128)} fusion(f32[512,2048]{0,1:T(8,128)} %select_bitcast_fusion.1, s32[1024]{0:T(1024)S(1)} %pad_clamp_fusion.6), kind=kCustom, calls=%fused_computation.2.clone | custom fusion | bytes 1049600 | tf_op jit(solution)/shard_map/jit(_take)/gather | solution.py:249
  125.6 2.1 copy.64
  127.6 3.6 %fusion.16 = f32[512,256]{1,0:T(8,128)} fusion(f32[512,256]{1,0:T(8,128)S(1)} %copy-done.2, f32[256,512]{0,1:T(8,128)} %copy.73, f32[256,512]{0,1:T(8,128)S(1)} %copy.72, f32[256,512]{0,1:T(8,128)} %copy.70, f32[256,512]{0,1:T(8,128)S(1)} %copy.69, f32[256,512]{0,1:T(8,128)} %copy.67, f32[256,512]{0,1:T(8,128)S(1)} %copy.66, f32[256,512]{0,1:T(8,128)} %copy.64, ...), kind=kLoop, calls=%fused_computation.46 | loop fusion | flops 7733248 | bytes 5791744 | tf_op jit(solution)/shard_map/add | solution.py:195
  132.8 32.4 %all_to_all.32 = f32[64,13,256]{2,1,0:T(8,128)S(1)} all-to-all(f32[64,13,256]{2,1,0:T(8,128)S(1)} %broadcast_in_dim.126), channel_id=1, replica_groups=mesh['space'=8,'vel'=64] {'vel'}, dimensions={0} | all-to-all | bytes 1703936 | tf_op jit(solution)/shard_map/all_to_all | solution.py:21
  166.8 6.2 %all-to-all-start.4 = ((f32[64,1,256]{2,1,0:T(1,128)}), f32[64,1,256]{2,1,0:T(1,128)S(1)}, u32[]{:S(2)}, u32[]{:S(2)}) async-start(f32[64,1,256]{2,1,0:T(1,128)} %broadcast_in_dim.127), calls=%async_computation.4 | async-start | bytes 131072 | tf_op jit(solution)/shard_map/all_to_all | solution.py:21
  175.2 1.8 gather_fusion.12
  177.0 1.8 gather_fusion.9
  180.4 2.1 copy.77
  184.5 5.3 %copy.78 = f32[512,2048]{0,1:T(8,128)} copy(f32[512,2048]{1,0:T(8,128)} %all-gather.5.cloned.1.call-done) | data formatting | bytes 8388608 | tf_op jit(solution)/shard_map/all_gather | solution.py:235
  189.8 11.7 %gather_fusion.10 = f32[2048,512]{1,0:T(8,128)} fusion(f32[512,2048]{0,1:T(8,128)} %copy.78, s32[2048]{0:T(1024)S(1)} %broadcast_clamp_fusion), kind=kCustom, calls=%fused_computation.10.clone | custom fusion | bytes 8396800 | tf_op jit(solution)/shard_map/jit(_take)/gather | solution.py:236
  201.5 3.7 %select_bitcast_fusion = f32[512,2048]{0,1:T(8,128)} fusion(f32[2048,512]{1,0:T(8,128)} %gather_fusion.10, pred[2048]{0:T(1024)(128)(4,1)S(1)} %compare_and_fusion), kind=kLoop, calls=%fused_computation.18 | loop fusion | flops 1048576 | bytes 8390656 | tf_op jit(solution)/shard_map/jit(_take)/select_n | solution.py:236
  205.3 3.4 %gather_fusion.17 = f32[256,512]{1,0:T(8,128)S(1)} fusion(f32[512,2048]{0,1:T(8,128)} %select_bitcast_fusion, s32[1024]{0:T(1024)S(1)} %pad_clamp_fusion), kind=kCustom, calls=%fused_computation.17.clone | custom fusion | bytes 1049600 | tf_op jit(solution)/shard_map/jit(_take)/gather | solution.py:249
  208.7 4.2 %gather_fusion.15 = f32[256,512]{1,0:T(8,128)} fusion(f32[512,2048]{0,1:T(8,128)} %select_bitcast_fusion, s32[1024]{0:T(1024)S(1)} %pad_clamp_fusion.2), kind=kCustom, calls=%fused_computation.16.clone | custom fusion | bytes 1049600 | tf_op jit(solution)/shard_map/jit(_take)/gather | solution.py:249
  212.9 4.2 %gather_fusion.13 = f32[256,512]{1,0:T(8,128)} fusion(f32[512,2048]{0,1:T(8,128)} %select_bitcast_fusion, s32[1024]{0:T(1024)S(1)} %pad_clamp_fusion.4), kind=kCustom, calls=%fused_computation.15.clone | custom fusion | bytes 1049600 | tf_op jit(solution)/shard_map/jit(_take)/gather | solution.py:249
  217.1 4.2 %gather_fusion.11 = f32[256,512]{1,0:T(8,128)} fusion(f32[512,2048]{0,1:T(8,128)} %select_bitcast_fusion, s32[1024]{0:T(1024)S(1)} %pad_clamp_fusion.6), kind=kCustom, calls=%fused_computation.14.clone | custom fusion | bytes 1049600 | tf_op jit(solution)/shard_map/jit(_take)/gather | solution.py:249
  222.3 2.0 copy.85
  224.3 2.0 copy.82
  226.3 2.1 copy.79
  228.4 2.9 %fusion.6 = f32[512,256]{1,0:T(8,128)S(1)} fusion(f32[512,256]{1,0:T(8,128)S(1)} %copy-done.1, f32[256,512]{0,1:T(8,128)} %copy.88, f32[256,512]{0,1:T(8,128)S(1)} %copy.87, f32[256,512]{0,1:T(8,128)} %copy.85, f32[256,512]{0,1:T(8,128)S(1)} %copy.84, f32[256,512]{0,1:T(8,128)} %copy.82, f32[256,512]{0,1:T(8,128)S(1)} %copy.81, f32[256,512]{0,1:T(8,128)} %copy.79, ...), kind=kLoop, calls=%fused_computation.32 | loop fusion | flops 7733248 | bytes 5791744 | tf_op jit(solution)/shard_map/add | solution.py:195
  231.8 38.7 %all_to_all.33 = f32[64,13,256]{2,1,0:T(8,128)S(1)} all-to-all(f32[64,13,256]{2,1,0:T(8,128)S(1)} %broadcast_in_dim.128), channel_id=1, replica_groups=mesh['space'=8,'vel'=64] {'vel'}, dimensions={0} | all-to-all | bytes 1703936 | tf_op jit(solution)/shard_map/all_to_all | solution.py:21
  (136 shorter events, 28.6 us)
Async XLA Ops:
  7.2 83.6 %all-gather.3.cloned.1.call-start = ((), (), s32[]{:S(2)}) async-start(), calls=%async_computation.6 | async-start | bytes 4718592 | tf_op jit(solution)/shard_map/all_gather | solution.py:235
  9.2 18.2 %copy-start = (f32[512,256]{0,1:T(8,128)S(1)}, f32[512,256]{0,1:T(8,128)}, u32[]{:S(2)}) copy-start(f32[512,256]{0,1:T(8,128)} %copy.61) | copy-start | bytes 1572868
  10.7 21.6 %all-to-all-start.2 = ((s32[8,1,8,256]{3,2,1,0:T(8,128)}), s32[8,1,8,256]{3,2,1,0:T(8,128)S(1)}, u32[]{:S(2)}, u32[]{:S(2)}) async-start(s32[8,1,8,256]{3,2,1,0:T(8,128)} %broadcast_in_dim.117), calls=%async_computation.2 | async-start | bytes 131072 | tf_op jit(solution)/shard_map/all_to_all | solution.py:21
  31.0 13.5 %copy-start.4 = (f32[4,3,256]{2,0,1:T(4,128)S(1)}, f32[4,3,256]{2,0,1:T(4,128)}, u32[]{:S(2)}) copy-start(f32[4,3,256]{2,0,1:T(4,128)} %param.12) | copy-start | bytes 36868
  33.4 39.6 %all-to-all-start = ((f32[64,13,256]{2,1,0:T(8,128)}), f32[64,13,256]{2,1,0:T(8,128)S(1)}, u32[]{:S(2)}, u32[]{:S(2)}) async-start(f32[64,13,256]{2,1,0:T(8,128)} %broadcast_in_dim.112), calls=%async_computation | async-start | bytes 2097152 | tf_op jit(solution)/shard_map/all_to_all | solution.py:21
  74.6 16.0 %all-to-all-start.1 = ((f32[64,1,256]{2,1,0:T(1,128)}), f32[64,1,256]{2,1,0:T(1,128)S(1)}, u32[]{:S(2)}, u32[]{:S(2)}) async-start(f32[64,1,256]{2,1,0:T(1,128)} %broadcast_in_dim.113), calls=%async_computation.1 | async-start | bytes 131072 | tf_op jit(solution)/shard_map/all_to_all | solution.py:21
  80.8 103.6 %all-gather.5.cloned.1.call-start = ((), (), s32[]{:S(2)}) async-start(), calls=%async_computation.7 | async-start | bytes 4718592 | tf_op jit(solution)/shard_map/all_gather | solution.py:235
  119.3 8.4 %copy-start.2 = (f32[512,256]{1,0:T(8,128)S(1)}, f32[512,256]{1,0:T(8,128)}, u32[]{:S(2)}) copy-start(f32[512,256]{1,0:T(8,128)} %param.11) | copy-start | bytes 1572868
  131.2 41.8 %copy-start.1 = (f32[512,256]{1,0:T(8,128)S(1)}, f32[512,256]{1,0:T(8,128)}, u32[]{:S(2)}) copy-start(f32[512,256]{1,0:T(8,128)} %fusion.16) | copy-start | bytes 1572868
  166.8 16.0 %all-to-all-start.4 = ((f32[64,1,256]{2,1,0:T(1,128)}), f32[64,1,256]{2,1,0:T(1,128)S(1)}, u32[]{:S(2)}, u32[]{:S(2)}) async-start(f32[64,1,256]{2,1,0:T(1,128)} %broadcast_in_dim.127), calls=%async_computation.4 | async-start | bytes 131072 | tf_op jit(solution)/shard_map/all_to_all | solution.py:21
  231.3 40.6 %copy-start.3 = (f32[512,256]{1,0:T(8,128)}, f32[512,256]{1,0:T(8,128)S(1)}, u32[]{:S(2)}) copy-start(f32[512,256]{1,0:T(8,128)S(1)} %fusion.6) | copy-start | bytes 1572868
Sparse Core Ops, SparseCore 0:
  10.7 63.7 all-gather.2
  131.4 53.0 all-gather.4
where the time goes:
time: 280 us; the launch traced here: 279 us
  local copies, waits for them, and re-layouts  95.1 us (34%)
  blocking collectives  71.1 us (25%)
  waiting for transfers between devices  39.9 us (14%)
  starting transfers between devices  34.6 us (12%)
  other arithmetic  19 us (7%)
  between operations  14.8 us (5%)
  matrix products  4.28 us (2%)
    all_to_all x2, blocking collectives, sent_to_all(): return lax.all_to_all(copies, axis, split_axis=0, concat_axis=0, tiled=True)  71.1 us
    gather x16, local copies, waits for them, and re-layouts, per_device(): jnp.take(ghosts, ghost_index[side], axis=1)  44.5 us
    all_to_all x4, waiting for transfers between devices, sent_to_all(): return lax.all_to_all(copies, axis, split_axis=0, concat_axis=0, tiled=True)  38.3 us
    all_to_all x4, starting transfers between devices, sent_to_all(): return lax.all_to_all(copies, axis, split_axis=0, concat_axis=0, tiled=True)  34.3 us
    gather x2, local copies, waits for them, and re-layouts, per_device(): ghosts = jnp.take(border, pull_index, axis=1)  23.5 us
    gather x16, local copies, waits for them, and re-layouts, per_device(): jnp.take(current, local_index[side], axis=1)  13.9 us
    select_n x2, other arithmetic, per_device(): ghosts = jnp.take(border, pull_index, axis=1)  7.53 us
    add x2, other arithmetic, relax(): current + time_step * (params[23][None, :] * (gauss - current) - outflow...  6.51 us
  transfers between devices with their start and end apart: 6, of which 4 were waited for; matrix products, arithmetic and copies ran while one was open for 10% of the time, Pallas kernels for 0%

commit v1 on v0

v1 whole, which is shorter than its diff:
```python
import functools

import jax
import jax.numpy as jnp
from jax import lax
from jax.experimental import pallas as pl
from jax.experimental.pallas import tpu as pltpu
from jax.sharding import Mesh, PartitionSpec as P

VXY = 32
TILE = 128
CELLS = 256
GROUPS = 8
NODES = 64
LANES = 128
TILES = 16
LEVELS = 32
FACES = 4
TOTAL = 32768

spacing = 0.3
ellipsoid_mix = -0.25
prandtl = 0.8
visc_power = 0.26
time_step = 0.025

ROW_ADJ = NODES
ROW_NORMAL = ROW_ADJ + FACES
ROW_SEND = ROW_NORMAL + 3 * FACES
ROW_COUNT = ROW_SEND + GROUPS
ROWS = ROW_COUNT + GROUPS

HIGHEST = lax.Precision.HIGHEST
PARAMS = pltpu.CompilerParams(vmem_limit_bytes=48 * 1024 * 1024)


def level(i):
    return (i - (VXY - 1) / 2.0) * spacing


def take_lanes(values, lanes):
    return jnp.take_along_axis(values, lanes, axis=1, mode="promise_in_bounds")


def node_x(rows, lanes):
    row = lax.broadcasted_iota(jnp.int32, (rows, lanes), 0)
    return ((row & (VXY - 1)).astype(jnp.float32) - (VXY - 1) / 2.0) * spacing


def neighbour_tiles(block_ref, g):
    adj = block_ref[g, ROW_ADJ : ROW_ADJ + FACES, :]
    adj = jnp.concatenate([adj[:, :LANES], adj[:, LANES:]], axis=0)
    place = adj - CELLS
    end = jnp.zeros((1, LANES), jnp.float32)
    source = jnp.zeros(adj.shape, jnp.float32)
    start = jnp.zeros(adj.shape, jnp.float32)
    for s in range(GROUPS):
        end = end + TILE * block_ref[g, ROW_COUNT + s : ROW_COUNT + s + 1, :LANES]
        past = end <= place
        source = source + jnp.where(past, 1.0, 0.0)
        if s < GROUPS - 1:
            start = jnp.where(past, jnp.broadcast_to(end, adj.shape), start)
    source = jnp.minimum(source, GROUPS - 1.0)
    slot = jnp.clip(place - start, 0.0, CELLS - 1.0).astype(jnp.int32)
    table = source.astype(jnp.int32) * 2 + (slot >> 7)
    lane = slot & (LANES - 1)
    mine = lax.broadcasted_iota(jnp.int32, adj.shape, 0) == g
    listed = jnp.zeros(adj.shape, jnp.float32)
    for s in range(GROUPS):
        for half in range(2):
            rows = block_ref[s, ROW_SEND : ROW_SEND + GROUPS, half * LANES : (half + 1) * LANES]
            row = column_sum(jnp.where(mine, rows, 0.0))
            found = take_lanes(jnp.broadcast_to(row, adj.shape), lane)
            listed = jnp.where(table == s * 2 + half, found, listed)
    far = source * CELLS + listed
    own = adj + jnp.float32(CELLS) * lax.convert_element_type(g, jnp.float32)
    return jnp.where(adj < CELLS, own, far).astype(jnp.int32)


def transport(value_ref, normal_ref, near, node_ref, g, half):
    at = slice(half * LANES, (half + 1) * LANES)
    lanes, tiles = [], []
    for face in range(FACES):
        row = jnp.broadcast_to(near[half * FACES + face : half * FACES + face + 1, :], (8, LANES))
        lanes.append(row & (LANES - 1))
        tiles.append(row >> 7)
    blocks = NODES // 8
    found = [[None] * blocks for _ in range(FACES)]
    for t in range(TILES):
        hit = [tiles[face] == t for face in range(FACES)]
        for b in range(blocks):
            source = value_ref[t // 2, b * 8 : b * 8 + 8, (t % 2) * LANES : (t % 2 + 1) * LANES]
            for face in range(FACES):
                got = take_lanes(source, lanes[face])
                found[face][b] = got if t == 0 else jnp.where(hit[face], got, found[face][b])
    out = []
    speeds = []
    for face in range(FACES):
        normal = [
            normal_ref[g, ROW_NORMAL + 3 * face + d : ROW_NORMAL + 3 * face + d + 1, at] for d in range(3)
        ]
        fixed = [normal[1] * node_ref[0, y] + normal[2] * node_ref[0, 2] for y in range(2)]
        speeds.append((jnp.broadcast_to(normal[0], (8, LANES)), [jnp.broadcast_to(f, (8, LANES)) for f in fixed]))
    comp_x = node_x(VXY, LANES)
    for b in range(blocks):
        own = value_ref[g, b * 8 : b * 8 + 8, at]
        vx = comp_x[(b % 4) * 8 : (b % 4) * 8 + 8, :]
        total = jnp.zeros((8, LANES), jnp.float32)
        for face in range(FACES):
            speed = speeds[face][0] * vx + speeds[face][1][b // 4]
            total = total + speed * jnp.where(speed > 0.0, own, found[face][b])
        out.append(total)
    return jnp.concatenate(out, axis=0)


def moment_table(node_ref, third):
    row = lax.broadcasted_iota(jnp.int32, (8, NODES), 0)
    col = lax.broadcasted_iota(jnp.int32, (8, NODES), 1)
    x = ((col & (VXY - 1)).astype(jnp.float32) - (VXY - 1) / 2.0) * spacing
    y = jnp.where(col >= VXY, node_ref[0, 1], node_ref[0, 0])
    flat = x * x + y * y
    table = jnp.zeros((8, NODES), jnp.float32)
    picks = [jnp.ones_like(x), x, y, x * x, y * y, x * y]
    if third:
        picks += [x * flat, y * flat]
    for i, pick in enumerate(picks):
        table = jnp.where(row == i, pick, table)
    return table


def first_kernel(node_ref, block_ref, near_ref, flux_ref, sums_ref):
    table = moment_table(node_ref, False)

    def group(g, carry):
        near = neighbour_tiles(block_ref, g)
        near_ref[g] = near
        for half in range(2):
            at = slice(half * LANES, (half + 1) * LANES)
            flux = transport(block_ref, block_ref, near, node_ref, g, half)
            flux_ref[g, :, at] = flux
            own = block_ref[g, :NODES, at]
            sums_ref[g * 2 + half, :8, :] = jnp.dot(
                table, own, precision=HIGHEST, preferred_element_type=jnp.float32
            )
            sums_ref[g * 2 + half, 8:, :] = jnp.dot(
                table, flux, precision=HIGHEST, preferred_element_type=jnp.float32
            )
        return carry

    lax.fori_loop(0, GROUPS, group, 0)


def macroscopic(m):
    density = m[0]
    scale = 1.0 / density
    ux, uy, uz = m[1] * scale, m[2] * scale, m[3] * scale
    second = [m[4 + i] * scale for i in range(6)]
    txx = second[0] - ux * ux
    tyy = second[1] - uy * uy
    tzz = second[2] - uz * uz
    txy = second[3] - ux * uy
    txz = second[4] - ux * uz
    tyz = second[5] - uy * uz
    temper = (txx + tyy + tzz) / 3.0
    return density, (ux, uy, uz), second, (txx, tyy, tzz, txy, txz, tyz), temper


def coefficients(m):
    density, (ux, uy, uz), _, (txx, tyy, tzz, txy, txz, tyz), temper = macroscopic(m)
    iso = (1.0 - ellipsoid_mix) * temper
    lxx = iso + ellipsoid_mix * txx
    lyy = iso + ellipsoid_mix * tyy
    lzz = iso + ellipsoid_mix * tzz
    lxy = ellipsoid_mix * txy
    lxz = ellipsoid_mix * txz
    lyz = ellipsoid_mix * tyz
    cxx = lyy * lzz - lyz * lyz
    cxy = lyz * lxz - lxy * lzz
    cxz = lxy * lyz - lyy * lxz
    cyy = lxx * lzz - lxz * lxz
    cyz = lxy * lxz - lxx * lyz
    czz = lxx * lyy - lxy * lxy
    det = 1.0 / (lxx * cxx + lxy * cxy + lxz * cxz)
    inverse = (cxx * det, cyy * det, czz * det, cxy * det, cxz * det, cyz * det)
    collide = prandtl * density * jnp.exp(visc_power * jnp.log(temper))
    return density, (ux, uy, uz), inverse, collide


def factor_tables(mean, inverse, pair_ref, row_ref, col_ref):
    grid = level(lax.broadcasted_iota(jnp.int32, (VXY, LANES), 0).astype(jnp.float32))
    ixx, iyy, izz, ixy, ixz, iyz = inverse
    cx, cy, cz = grid - mean[0], grid - mean[1], grid - mean[2]
    own_x, own_y, own_z = -0.25 * ixx * cx * cx, -0.25 * iyy * cy * cy, -0.25 * izz * cz * cz
    cross_y = -ixy * cy
    cross_z = -ixz * cz
    cross_yz = -iyz * cy
    for i in range(VXY):
        x_own, x_c = own_x[i : i + 1, :], cx[i : i + 1, :]
        z_own, z_c = own_z[i : i + 1, :], cz[i : i + 1, :]
        pair_ref[i] = jnp.exp(x_own + own_y + x_c * cross_y)
        row_ref[i] = jnp.exp(x_own + own_z + x_c * cross_z)
        col_ref[i] = jnp.exp(z_own + own_y + z_c * cross_yz)


def column_sum(a):
    return jnp.sum(a, axis=0, keepdims=True)


def equilibrium_moments(mean, inverse, pair_ref, row_ref, col_ref):
    factor_tables(mean, inverse, pair_ref, row_ref, col_ref)
    zero = jnp.zeros((VXY, LANES), jnp.float32)

    def step(i, carry):
        s0, sx, sxx, s1, s1x, s2 = carry
        u0, u1, u2 = zero, zero, zero
        for k in range(VXY // 2):
            z = -level(k)
            low = row_ref[i, k : k + 1, :] * col_ref[k]
            high = row_ref[i, VXY - 1 - k : VXY - k, :] * col_ref[VXY - 1 - k]
            both = low + high
            u0 = u0 + both
            u1 = u1 + z * (high - low)
            u2 = u2 + (z * z) * both
        pair = pair_ref[i]
        x = level(lax.convert_element_type(i, jnp.float32))
        w0, w1 = pair * u0, pair * u1
        s0 = s0 + w0
        sx = sx + x * w0
        sxx = sxx + (x * x) * w0
        s1 = s1 + w1
        s1x = s1x + x * w1
        s2 = s2 + pair * u2
        return s0, sx, sxx, s1, s1x, s2

    s0, sx, sxx, s1, s1x, s2 = lax.fori_loop(0, VXY, step, (zero,) * 6)
    y = level(lax.broadcasted_iota(jnp.int32, (VXY, LANES), 0).astype(jnp.float32))
    return [
        column_sum(a)
        for a in (s0, sx, y * s0, s1, sxx, y * y * s0, s2, y * sx, s1x, y * s1)
    ]


def equilibrium_total(mean, inverse, pair_ref, row_ref, col_ref):
    factor_tables(mean, inverse, pair_ref, row_ref, col_ref)
    zero = jnp.zeros((VXY, LANES), jnp.float32)

    def step(i, total):
        u = zero
        for k in range(VXY):
            u = u + row_ref[i, k : k + 1, :] * col_ref[k]
        return total + pair_ref[i] * u

    return column_sum(lax.fori_loop(0, VXY, step, zero))


def put_rows(out_ref, base, mean, inverse, alpha, beta):
    ixx, iyy, izz, ixy, ixz, iyz = inverse
    lx = ixx * mean[0] + ixy * mean[1] + ixz * mean[2]
    ly = ixy * mean[0] + iyy * mean[1] + iyz * mean[2]
    lz = ixz * mean[0] + iyz * mean[1] + izz * mean[2]
    offset = mean[0] * lx + mean[1] * ly + mean[2] * lz
    rows = [ixx, iyy, izz, 2.0 * ixy, 2.0 * ixz, 2.0 * iyz, -2.0 * lx, -2.0 * ly, -2.0 * lz, offset, alpha, beta]
    for i, row in enumerate(rows):
        out_ref[base + i : base + i + 1, :] = row


def level_sums(parts_ref, rows):
    zero = jnp.zeros((rows, LANES), jnp.float32)
    s0, s1, s2, s3 = zero, zero, zero, zero
    for i in range(LEVELS):
        part = parts_ref[i]
        z = level(i)
        s0 = s0 + part
        s1 = s1 + z * part
        s2 = s2 + (z * z) * part
        if rows == 8:
            s3 = s3 + (z * z * z) * part
    return s0, s1, s2, s3


def ten(s0, s1, s2, base):
    def row(a, i):
        return a[base + i : base + i + 1, :] / TOTAL

    return [
        row(s0, 0), row(s0, 1), row(s0, 2), row(s1, 0), row(s0, 3), row(s0, 4), row(s2, 0),
        row(s0, 5), row(s1, 1), row(s1, 2),
    ]


def fields_kernel(parts_ref, out_ref, pair_ref, row_ref, col_ref):
    s0, s1, s2, _ = level_sums(parts_ref, 16)
    now = ten(s0, s1, s2, 0)
    moved = ten(s0, s1, s2, 8)
    density, mean, inverse, collide = coefficients(now)
    gauss = equilibrium_moments(mean, inverse, pair_ref, row_ref, col_ref)
    beta = time_step * collide * density * TOTAL / gauss[0]
    alpha = 1.0 - time_step * collide
    put_rows(out_ref, 0, mean, inverse, alpha, beta)
    later = [alpha * a + beta * (e / TOTAL) - time_step * b for a, e, b in zip(now, gauss, moved)]
    density, mean, inverse, collide = coefficients(later)
    total = equilibrium_total(mean, inverse, pair_ref, row_ref, col_ref)
    beta = time_step * collide * density * TOTAL / total
    put_rows(out_ref, 12, mean, inverse, 1.0 - time_step * collide, beta)


def relaxed_tile(value, flux, params_ref, base, tile, node_ref):
    rows = [params_ref[tile, base + i : base + i + 1, :] for i in range(12)]
    ixx, iyy, izz, ixy, ixz, iyz, lx, ly, lz, offset, alpha, beta = rows
    vz = node_ref[0, 2]
    x = node_x(VXY, LANES)
    parts = []
    for y in range(2):
        vy = node_ref[0, y]
        slope = ixy * vy + ixz * vz + lx
        rest = (iyy * vy + iyz * vz + ly) * vy + (izz * vz + lz) * vz + offset
        energy = jnp.exp(-0.5 * ((ixx * x + slope) * x + rest))
        at = slice(y * VXY, (y + 1) * VXY)
        parts.append(alpha * value[at, :] + beta * energy - time_step * flux[at, :])
    return jnp.concatenate(parts, axis=0)


def second_kernel(node_ref, block_ref, near_ref, flux_ref, params_ref, out_ref, sums_ref, value_ref):
    table = moment_table(node_ref, True)

    def first_step(g, carry):
        for half in range(2):
            at = slice(half * LANES, (half + 1) * LANES)
            value_ref[g, :, at] = relaxed_tile(
                block_ref[g, :NODES, at], flux_ref[g, :, at], params_ref, 0, g * 2 + half, node_ref
            )
        return carry

    lax.fori_loop(0, GROUPS, first_step, 0)

    def second_step(g, carry):
        near = near_ref[g]
        for half in range(2):
            at = slice(half * LANES, (half + 1) * LANES)
            flux = transport(value_ref, block_ref, near, node_ref, g, half)
            value = relaxed_tile(value_ref[g, :, at], flux, params_ref, 12, g * 2 + half, node_ref)
            out_ref[g, :, at] = value
            sums_ref[g * 2 + half] = jnp.dot(
                table, value, precision=HIGHEST, preferred_element_type=jnp.float32
            )
        return carry

    lax.fori_loop(0, GROUPS, second_step, 0)


def final_kernel(parts_ref, out_ref):
    s0, s1, s2, s3 = level_sums(parts_ref, 8)

    def row(a, i):
        return a[i : i + 1, :] / TOTAL

    density, (ux, uy, uz), b, theta, _ = macroscopic(ten(s0, s1, s2, 0))
    third = [
        row(s0, 6) + row(s2, 1),
        row(s0, 7) + row(s2, 2),
        row(s1, 3) + row(s1, 4) + row(s3, 0),
    ]
    trace = b[0] + b[1] + b[2]
    square = ux * ux + uy * uy + uz * uz
    stress = (
        b[0] * ux + b[3] * uy + b[4] * uz,
        b[3] * ux + b[1] * uy + b[5] * uz,
        b[4] * ux + b[5] * uy + b[2] * uz,
    )
    flux = [
        0.5 * (t / density - 2.0 * s - u * trace + 2.0 * u * square)
        for t, s, u in zip(third, stress, (ux, uy, uz))
    ]
    for i, value in enumerate((density, ux, uy, uz, *theta, *flux)):
        out_ref[i : i + 1, :] = value
    out_ref[13:16, :] = jnp.zeros((3, LANES), jnp.float32)


def shape(*dims, dtype=jnp.float32):
    return jax.ShapeDtypeStruct(dims, dtype)


VMEM = pl.BlockSpec(memory_space=pltpu.VMEM)
SMEM = pl.BlockSpec(memory_space=pltpu.SMEM)
TABLES = [pltpu.VMEM((VXY, VXY, LANES), jnp.float32)] * 3


def spread(x, axes, count):
    copies = jnp.broadcast_to(x, (count, *x.shape))
    return lax.all_to_all(copies, axes, 0, 0, tiled=True)


def per_device(distribution, normals, adjacency, send_list, block_counts):
    z, x, y, c = (lax.axis_index(a) for a in ("z", "x", "y", "c"))
    vel = (x * 8 + y) * 2 + c
    row = (vel * 16 + z * 2) & (VXY - 1)
    node = jnp.stack([row, row + 1, vel // 2, vel // 2]).astype(jnp.float32)
    node = ((node - (VXY - 1) / 2.0) * spacing).reshape(1, 4)

    extra = jnp.concatenate(
        [
            adjacency.astype(jnp.float32),
            normals.reshape(3 * FACES, CELLS),
            send_list[0].astype(jnp.float32),
            jnp.broadcast_to(block_counts.astype(jnp.float32), (GROUPS, CELLS)),
        ],
        axis=0,
    )
    block = jnp.concatenate(
        [distribution.reshape(GROUPS, NODES, CELLS), jnp.broadcast_to(extra, (GROUPS, *extra.shape))], axis=1
    )
    block = lax.all_to_all(block, "z", 0, 0, tiled=True)

    near, flux, sums = pl.pallas_call(
        first_kernel,
        out_shape=(
            shape(GROUPS, 8, LANES, dtype=jnp.int32),
            shape(GROUPS, NODES, CELLS),
            shape(TILES, 16, LANES),
        ),
        in_specs=[SMEM, VMEM],
        out_specs=(VMEM, VMEM, VMEM),
        compiler_params=PARAMS,
    )(node, block)

    mine = jnp.sum(lax.all_to_all(sums, ("z", "c"), 0, 0, tiled=True), axis=0)
    params = pl.pallas_call(
        fields_kernel,
        out_shape=shape(24, LANES),
        in_specs=[VMEM],
        out_specs=VMEM,
        scratch_shapes=TABLES,
        compiler_params=PARAMS,
    )(spread(mine, ("x", "y"), LEVELS))
    params = spread(params, ("z", "c"), TILES)

    value, sums = pl.pallas_call(
        second_kernel,
        out_shape=(shape(GROUPS, NODES, CELLS), shape(TILES, 8, LANES)),
        in_specs=[SMEM, VMEM, VMEM, VMEM, VMEM],
        out_specs=(VMEM, VMEM),
        scratch_shapes=[pltpu.VMEM((GROUPS, NODES, CELLS), jnp.float32)],
        compiler_params=PARAMS,
    )(node, block, near, flux, params)

    relaxed = lax.all_to_all(value, "z", 0, 0, tiled=True).reshape(GROUPS * NODES, CELLS)
    mine = jnp.sum(lax.all_to_all(sums, ("z", "c"), 0, 0, tiled=True), axis=0)
    fields = pl.pallas_call(
        final_kernel,
        out_shape=shape(16, LANES),
        in_specs=[VMEM],
        out_specs=VMEM,
        compiler_params=PARAMS,
    )(spread(mine, ("x", "y"), LEVELS))
    both = spread(fields, "c", 2)
    return relaxed, jnp.concatenate([both[0], both[1]], axis=1)[:13]


def solution(mesh):
    split = Mesh(mesh.devices.reshape(8, 4, 8, 2), ("z", "x", "y", "c"))
    vel = ("x", "y", "c")
    placed = (P(vel, "z"), P(None, None, "z"), P(None, "z"), P("z", None, None), P(None, "z"))
    return jax.shard_map(
        per_device,
        mesh=split,
        in_specs=placed,
        out_specs=(P(vel, "z"), P(None, "z")),
        check_vma=False,
    )
```

time: 280 us -> 196 us (0.70)
  local copies, waits for them, and re-layouts: 95.1 us -> 0.97 us
  Pallas kernels: 0 us -> 57.5 us
  starting transfers between devices: 34.6 us -> 14.4 us
  other arithmetic: 19 us -> 4.16 us
  between operations: 14.8 us -> 0.72 us
  blocking collectives: 71.1 us -> 76.8 us
  matrix products: 4.28 us -> 0 us
    gather x34 -> x0, local copies, waits for them, and re-layouts: 81.8 us -> none  [the longest x16 44.5 us: per_device(): jnp.take(ghosts, ghost_index[side], axis=1)]
    pallas_call x0 -> x4, Pallas kernels: none -> 57.5 us  [the longest x1 26.3 us: per_device(): pl.pallas_call(second_kernel, out_shape=(shape(GROUPS, NODES, CELLS), sha...]
    all_to_all x4 -> x2, starting transfers between devices: 34.3 us -> 14.4 us  [the longest x1 10.9 us: per_device(): block = lax.all_to_all(block, 'z', 0, 0, tiled=True)]
    select_n x11 -> x0, other arithmetic: 8.26 us -> none  [the longest x2 7.53 us: per_device(): ghosts = jnp.take(border, pull_index, axis=1)]
    add x6 -> x0, other arithmetic: 6.61 us -> none  [the longest x2 6.51 us: relax(): current + time_step * (params[23][None, :] * (gauss - current) - outflow...]
    all_to_all x2 -> x6, blocking collectives: 71.1 us -> 76.8 us  [the longest x4 54.2 us: spread(): return lax.all_to_all(copies, axes, 0, 0, tiled=True)]
    all_gather x1 -> x0, local copies, waits for them, and re-layouts: 5.34 us -> none  [per_device(): border = lax.all_gather(current, 'space', axis=1, tiled=True)]
    dot_general x5 -> x0, matrix products: 4.28 us -> none  [the longest x3 2.99 us: reduce_moments(): jnp.dot(moment_table, current, precision=lax.Precision.HIGHEST, preferred...]
  transfers between devices with their start and end apart: 6 -> 2, of which waited for: 4 -> 2; matrix products, arithmetic and copies ran while one was open for 10% -> 0% of each run, Pallas kernels for 0% -> 0%
where the time goes in v1:
time: 196 us; the launch traced here: 195 us
  blocking collectives  76.8 us (39%)
  Pallas kernels  57.5 us (29%)
  waiting for transfers between devices  40.8 us (21%)
  starting transfers between devices  14.4 us (7%)
  other arithmetic  4.16 us (2%)
    all_to_all x4, blocking collectives, spread(): return lax.all_to_all(copies, axes, 0, 0, tiled=True)  54.2 us
    pallas_call x1, Pallas kernels, per_device(): pl.pallas_call(second_kernel, out_shape=(shape(GROUPS, NODES, CELLS), sha...  26.3 us
    pallas_call x1, Pallas kernels, per_device(): pl.pallas_call(first_kernel, out_shape=(shape(GROUPS, 8, LANES, dtype=jnp...  26.2 us
    all_to_all x1, waiting for transfers between devices, per_device(): block = lax.all_to_all(block, 'z', 0, 0, tiled=True)  23.5 us
    all_to_all x2, blocking collectives, per_device(): mine = jnp.sum(lax.all_to_all(sums, ('z', 'c'), 0, 0, tiled=True), axis=0)  22.6 us
    all_to_all x1, waiting for transfers between devices, per_device(): lax.all_to_all(value, 'z', 0, 0, tiled=True).reshape(GROUPS * NODES, CELLS)  17.3 us
    all_to_all x1, starting transfers between devices, per_device(): block = lax.all_to_all(block, 'z', 0, 0, tiled=True)  10.9 us
    pallas_call x1, Pallas kernels, per_device(): pl.pallas_call(fields_kernel, out_shape=shape(24, LANES), in_specs=[VMEM]...  4.85 us
  transfers between devices with their start and end apart: 2, of which 2 were waited for; matrix products, arithmetic and copies ran while one was open for 0% of the time, Pallas kernels for 0%

profile of v1, /device:TPU:1, one launch (start us, length us, event | category | flops | bytes accessed | tf_op | source)
XLA Modules:
  0.0 195.3 jit_solution(18389568948995917257)
XLA Ops:
  0.6 0.0 copy-start.1
  0.6 0.7 convert_bitcast_fusion.1
  1.3 0.0 copy-start
  1.3 0.7 convert_element_type.23
  2.0 0.0 copy-done.1
  2.0 0.0 copy-done
  2.0 0.1 pad.7.clone
  2.1 0.1 maximum_maximum_fusion
  2.2 2.0 %pad_maximum_fusion = f32[8,96,256]{2,1,0:T(8,128)} fusion(f32[8,32,256]{2,1,0:T(8,128)S(1)} %broadcast_in_dim.24, f32[8,64,256]{2,1,0:T(8,128)} %bitcast.14), kind=kLoop, calls=%fused_computation | loop fusion | flops 196608 | bytes 1572864 | tf_op jit(solution)/shard_map/concatenate | solution.py:409
  4.2 10.9 %all-to-all-start = ((f32[8,96,256]{2,1,0:T(8,128)}), f32[8,96,256]{2,1,0:T(8,128)S(1)}, u32[]{:S(2)}, u32[]{:S(2)}) async-start(f32[8,96,256]{2,1,0:T(8,128)} %pad_maximum_fusion), calls=%async_computation | async-start | bytes 1572864 | tf_op jit(solution)/shard_map/all_to_all | solution.py:412
  15.1 0.1 fusion.1.node_ref
  15.2 23.5 %all-to-all-done.block_ref = f32[8,96,256]{2,1,0:T(8,128)S(1)} async-done(((f32[8,96,256]{2,1,0:T(8,128)}), f32[8,96,256]{2,1,0:T(8,128)S(1)}, u32[]{:S(2)}, u32[]{:S(2)}) %all-to-all-start) | async-done | bytes 786464 | tf_op jit(solution)/shard_map/all_to_all | solution.py:412
  38.7 26.2 %shard_map.68 = (s32[8,8,128]{2,1,0:T(8,128)S(1)}, f32[8,64,256]{2,1,0:T(8,128)S(1)}, f32[16,16,128]{2,1,0:T(8,128)S(1)}) custom-call(f32[1,4]{1,0:T(1,128)S(1)} %fusion.1.node_ref, f32[8,96,256]{2,1,0:T(8,128)S(1)} %all-to-all-done.block_ref), custom_call_target="tpu_custom_call" | custom-call | tf_op jit(solution)/shard_map/pallas_call | solution.py:414
  64.9 12.1 %all_to_all.40 = f32[16,16,128]{2,1,0:T(8,128)S(1)} all-to-all(f32[16,16,128]{2,1,0:T(8,128)S(1)} %get-tuple-element.9), channel_id=1, replica_groups=mesh['z'=8,'x'=4,'y'=8,'c'=2] {'z','c'}, dimensions={0} | all-to-all | bytes 262144 | tf_op jit(solution)/shard_map/all_to_all | solution.py:426
  77.1 20.2 %all_to_all.41.parts_ref = f32[32,16,128]{2,1,0:T(8,128)S(1)} all-to-all(f32[32,16,128]{2,1,0:T(8,128)S(1)} %broadcast_in_dim.25), channel_id=1, replica_groups=mesh['z'=8,'x'=4,'y'=8,'c'=2] {'x','y'}, dimensions={0} | all-to-all | bytes 524288 | tf_op jit(solution)/shard_map/all_to_all | solution.py:390
  97.3 4.8 %shard_map.69 = f32[24,128]{1,0:T(8,128)S(1)} custom-call(f32[32,16,128]{2,1,0:T(8,128)S(1)} %all_to_all.41.parts_ref), custom_call_target="tpu_custom_call" | custom-call | tf_op jit(solution)/shard_map/pallas_call | solution.py:427
  102.1 14.9 %all_to_all.42.params_ref = f32[16,24,128]{2,1,0:T(8,128)S(1)} all-to-all(f32[16,24,128]{2,1,0:T(8,128)S(1)} %broadcast_in_dim.26), channel_id=1, replica_groups=mesh['z'=8,'x'=4,'y'=8,'c'=2] {'z','c'}, dimensions={0} | all-to-all | bytes 393216 | tf_op jit(solution)/shard_map/all_to_all | solution.py:390
  117.1 26.3 %shard_map.70 = (f32[8,64,256]{2,1,0:T(8,128)}, f32[16,8,128]{2,1,0:T(8,128)S(1)}) custom-call(f32[1,4]{1,0:T(1,128)S(1)} %fusion.1.node_ref, f32[8,96,256]{2,1,0:T(8,128)S(1)} %all-to-all-done.block_ref, s32[8,8,128]{2,1,0:T(8,128)S(1)} %get-tuple-element.7.near_ref, f32[8,64,256]{2,1,0:T(8,128)S(1)} %get-tuple-element.8.flux_ref, ...), custom_call_target="tpu_custom_call" | custom-call | tf_op jit(solution)/shard_map/pallas_call | solution.py:437
  143.4 10.5 %all_to_all.43 = f32[16,8,128]{2,1,0:T(8,128)S(1)} all-to-all(f32[16,8,128]{2,1,0:T(8,128)S(1)} %get-tuple-element.11), channel_id=1, replica_groups=mesh['z'=8,'x'=4,'y'=8,'c'=2] {'z','c'}, dimensions={0} | all-to-all | bytes 131072 | tf_op jit(solution)/shard_map/all_to_all | solution.py:447
  153.9 13.6 %all_to_all.44.parts_ref = f32[32,8,128]{2,1,0:T(8,128)S(1)} all-to-all(f32[32,8,128]{2,1,0:T(8,128)S(1)} %broadcast_in_dim.27), channel_id=1, replica_groups=mesh['z'=8,'x'=4,'y'=8,'c'=2] {'x','y'}, dimensions={0} | all-to-all | bytes 262144 | tf_op jit(solution)/shard_map/all_to_all | solution.py:390
  167.5 0.1 shard_map.71
  167.6 5.5 %all_to_all.45 = f32[2,16,128]{2,1,0:T(8,128)S(1)} all-to-all(f32[2,16,128]{2,1,0:T(8,128)S(1)} %broadcast_in_dim.28), channel_id=1, replica_groups=mesh['z'=8,'x'=4,'y'=8,'c'=2] {'c'}, dimensions={0} | all-to-all | bytes 32768 | tf_op jit(solution)/shard_map/all_to_all | solution.py:390
  173.0 3.5 %all-to-all-start.4 = ((f32[8,64,256]{2,1,0:T(8,128)}), f32[8,64,256]{2,1,0:T(8,128)S(1)}, u32[]{:S(2)}, u32[]{:S(2)}) async-start(f32[8,64,256]{2,1,0:T(8,128)} %get-tuple-element.10), calls=%async_computation.4 | async-start | bytes 1048576 | tf_op jit(solution)/shard_map/all_to_all | solution.py:446
  176.6 0.6 pad_maximum_fusion.1
  177.2 17.3 %all-to-all-done.4 = f32[8,64,256]{2,1,0:T(8,128)S(1)} async-done(((f32[8,64,256]{2,1,0:T(8,128)}), f32[8,64,256]{2,1,0:T(8,128)S(1)}, u32[]{:S(2)}, u32[]{:S(2)}) %all-to-all-start.4) | async-done | bytes 524320 | tf_op jit(solution)/shard_map/all_to_all | solution.py:446
  194.5 0.8 copy.9
  (11 shorter events, 0.1 us)
Async XLA Ops:
  0.6 1.4 copy-start.1
  1.3 0.7 copy-start
  4.2 34.4 %all-to-all-start = ((f32[8,96,256]{2,1,0:T(8,128)}), f32[8,96,256]{2,1,0:T(8,128)S(1)}, u32[]{:S(2)}, u32[]{:S(2)}) async-start(f32[8,96,256]{2,1,0:T(8,128)} %pad_maximum_fusion), calls=%async_computation | async-start | bytes 1572864 | tf_op jit(solution)/shard_map/all_to_all | solution.py:412
  173.0 21.4 %all-to-all-start.4 = ((f32[8,64,256]{2,1,0:T(8,128)}), f32[8,64,256]{2,1,0:T(8,128)S(1)}, u32[]{:S(2)}, u32[]{:S(2)}) async-start(f32[8,64,256]{2,1,0:T(8,128)} %get-tuple-element.10), calls=%async_computation.4 | async-start | bytes 1048576 | tf_op jit(solution)/shard_map/all_to_all | solution.py:446

commit v2 on v1

--- a/solution.py
+++ b/solution.py
@@ -1,5 +1,3 @@
-import functools
-
 import jax
 import jax.numpy as jnp
 from jax import lax
@@ -77,40 +75,33 @@
     return jnp.where(adj < CELLS, own, far).astype(jnp.int32)
 
 
-def transport(value_ref, normal_ref, near, node_ref, g, half):
-    at = slice(half * LANES, (half + 1) * LANES)
-    lanes, tiles = [], []
+def split_terms(value_ref, terms_ref, g):
+    value = value_ref[g, :NODES, :]
+    high = value.astype(jnp.bfloat16)
+    terms_ref[g, :NODES, :] = high
+    terms_ref[g, NODES:, :] = (value - high.astype(jnp.float32)).astype(jnp.bfloat16)
+
+
+def transport(value_ref, terms_ref, normal_ref, near, node_ref, g):
+    own = value_ref[g, :NODES, :]
+    x = node_x(NODES, CELLS)
+    second = lax.broadcasted_iota(jnp.int32, (NODES, CELLS), 0) >= VXY
+    place = lax.broadcasted_iota(jnp.int32, (CELLS, CELLS), 0)
+    total = jnp.zeros((NODES, CELLS), jnp.float32)
     for face in range(FACES):
-        row = jnp.broadcast_to(near[half * FACES + face : half * FACES + face + 1, :], (8, LANES))
-        lanes.append(row & (LANES - 1))
-        tiles.append(row >> 7)
-    blocks = NODES // 8
-    found = [[None] * blocks for _ in range(FACES)]
-    for t in range(TILES):
-        hit = [tiles[face] == t for face in range(FACES)]
-        for b in range(blocks):
-            source = value_ref[t // 2, b * 8 : b * 8 + 8, (t % 2) * LANES : (t % 2 + 1) * LANES]
-            for face in range(FACES):
-                got = take_lanes(source, lanes[face])
-                found[face][b] = got if t == 0 else jnp.where(hit[face], got, found[face][b])
-    out = []
-    speeds = []
-    for face in range(FACES):
-        normal = [
-            normal_ref[g, ROW_NORMAL + 3 * face + d : ROW_NORMAL + 3 * face + d + 1, at] for d in range(3)
-        ]
+        row = jnp.concatenate([near[face : face + 1, :], near[FACES + face : FACES + face + 1, :]], axis=1)
+        chosen = jnp.where(place == (row & (CELLS - 1)), 1.0, 0.0).astype(jnp.bfloat16)
+        group = row >> 8
+        found = None
+        for s in range(GROUPS):
+            both = jnp.dot(terms_ref[s], chosen, preferred_element_type=jnp.float32)
+            got = both[:NODES] + both[NODES:]
+            found = got if s == 0 else jnp.where(group == s, got, found)
+        normal = [normal_ref[g, ROW_NORMAL + 3 * face + d : ROW_NORMAL + 3 * face + d + 1, :] for d in range(3)]
         fixed = [normal[1] * node_ref[0, y] + normal[2] * node_ref[0, 2] for y in range(2)]
-        speeds.append((jnp.broadcast_to(normal[0], (8, LANES)), [jnp.broadcast_to(f, (8, LANES)) for f in fixed]))
-    comp_x = node_x(VXY, LANES)
-    for b in range(blocks):
-        own = value_ref[g, b * 8 : b * 8 + 8, at]
-        vx = comp_x[(b % 4) * 8 : (b % 4) * 8 + 8, :]
-        total = jnp.zeros((8, LANES), jnp.float32)
-        for face in range(FACES):
-            speed = speeds[face][0] * vx + speeds[face][1][b // 4]
-            total = total + speed * jnp.where(speed > 0.0, own, found[face][b])
-        out.append(total)
-    return jnp.concatenate(out, axis=0)
+        speed = normal[0] * x + jnp.where(second, fixed[1], fixed[0])
+        total = total + speed * jnp.where(speed > 0.0, own, found)
+    return total
 
 
 def moment_table(node_ref, third):
@@ -128,23 +119,21 @@
     return table
 
 
-def first_kernel(node_ref, block_ref, near_ref, flux_ref, sums_ref):
+def first_kernel(node_ref, block_ref, near_ref, flux_ref, sums_ref, terms_ref):
     table = moment_table(node_ref, False)
+    for g in range(GROUPS):
+        split_terms(block_ref, terms_ref, g)
 
     def group(g, carry):
         near = neighbour_tiles(block_ref, g)
         near_ref[g] = near
-        for half in range(2):
-            at = slice(half * LANES, (half + 1) * LANES)
-            flux = transport(block_ref, block_ref, near, node_ref, g, half)
-            flux_ref[g, :, at] = flux
-            own = block_ref[g, :NODES, at]
-            sums_ref[g * 2 + half, :8, :] = jnp.dot(
-                table, own, precision=HIGHEST, preferred_element_type=jnp.float32
-            )
-            sums_ref[g * 2 + half, 8:, :] = jnp.dot(
-                table, flux, precision=HIGHEST, preferred_element_type=jnp.float32
-            )
+        flux = transport(block_ref, terms_ref, block_ref, near, node_ref, g)
+        flux_ref[g] = flux
+        own = block_ref[g, :NODES, :]
+        for base, value in ((0, own), (8, flux)):
+            sums = jnp.dot(table, value, precision=HIGHEST, preferred_element_type=jnp.float32)
+            for half in range(2):
+                sums_ref[g * 2 + half, base : base + 8, :] = sums[:, half * LANES : (half + 1) * LANES]
         return carry
 
     lax.fori_loop(0, GROUPS, group, 0)
@@ -320,7 +309,7 @@
     return jnp.concatenate(parts, axis=0)
 
 
-def second_kernel(node_ref, block_ref, near_ref, flux_ref, params_ref, out_ref, sums_ref, value_ref):
+def second_kernel(node_ref, block_ref, near_ref, flux_ref, params_ref, out_ref, sums_ref, value_ref, terms_ref):
     table = moment_table(node_ref, True)
 
     def first_step(g, carry):
@@ -329,16 +318,16 @@
             value_ref[g, :, at] = relaxed_tile(
                 block_ref[g, :NODES, at], flux_ref[g, :, at], params_ref, 0, g * 2 + half, node_ref
             )
+        split_terms(value_ref, terms_ref, g)
         return carry
 
     lax.fori_loop(0, GROUPS, first_step, 0)
 
     def second_step(g, carry):
-        near = near_ref[g]
+        flux = transport(value_ref, terms_ref, block_ref, near_ref[g], node_ref, g)
         for half in range(2):
             at = slice(half * LANES, (half + 1) * LANES)
-            flux = transport(value_ref, block_ref, near, node_ref, g, half)
-            value = relaxed_tile(value_ref[g, :, at], flux, params_ref, 12, g * 2 + half, node_ref)
+            value = relaxed_tile(value_ref[g, :, at], flux[:, at], params_ref, 12, g * 2 + half, node_ref)
             out_ref[g, :, at] = value
             sums_ref[g * 2 + half] = jnp.dot(
                 table, value, precision=HIGHEST, preferred_element_type=jnp.float32
@@ -382,6 +371,7 @@
 
 VMEM = pl.BlockSpec(memory_space=pltpu.VMEM)
 SMEM = pl.BlockSpec(memory_space=pltpu.SMEM)
+TERMS = pltpu.VMEM((GROUPS, 2 * NODES, CELLS), jnp.bfloat16)
 TABLES = [pltpu.VMEM((VXY, VXY, LANES), jnp.float32)] * 3
 
 
@@ -420,6 +410,7 @@
         ),
         in_specs=[SMEM, VMEM],
         out_specs=(VMEM, VMEM, VMEM),
+        scratch_shapes=[TERMS],
         compiler_params=PARAMS,
     )(node, block)
 
@@ -439,7 +430,7 @@
         out_shape=(shape(GROUPS, NODES, CELLS), shape(TILES, 8, LANES)),
         in_specs=[SMEM, VMEM, VMEM, VMEM, VMEM],
         out_specs=(VMEM, VMEM),
-        scratch_shapes=[pltpu.VMEM((GROUPS, NODES, CELLS), jnp.float32)],
+        scratch_shapes=[pltpu.VMEM((GROUPS, NODES, CELLS), jnp.float32), TERMS],
         compiler_params=PARAMS,
     )(node, block, near, flux, params)
 

time: 196 us -> 161 us (0.82)
  Pallas kernels: 57.5 us -> 22.7 us
    pallas_call x1, Pallas kernels: 26.2 us -> 8.8 us  [per_device(): pl.pallas_call(first_kernel, out_shape=(shape(GROUPS, 8, LANES, dtype=jnp...]
    pallas_call x1, Pallas kernels: 26.3 us -> 8.99 us  [per_device(): pl.pallas_call(second_kernel, out_shape=(shape(GROUPS, NODES, CELLS), sha...]
where the time goes in v2:
time: 161 us
  blocking collectives  76.8 us (48%)
  waiting for transfers between devices  40.8 us (25%)
  Pallas kernels  22.7 us (14%)
  starting transfers between devices  14.4 us (9%)
  other arithmetic  4.16 us (3%)
    all_to_all x4, blocking collectives, spread(): return lax.all_to_all(copies, axes, 0, 0, tiled=True)  54.2 us
    all_to_all x1, waiting for transfers between devices, per_device(): block = lax.all_to_all(block, 'z', 0, 0, tiled=True)  23.5 us
    all_to_all x2, blocking collectives, per_device(): mine = jnp.sum(lax.all_to_all(sums, ('z', 'c'), 0, 0, tiled=True), axis=0)  22.6 us
    all_to_all x1, waiting for transfers between devices, per_device(): lax.all_to_all(value, 'z', 0, 0, tiled=True).reshape(GROUPS * NODES, CELLS)  17.3 us
    all_to_all x1, starting transfers between devices, per_device(): block = lax.all_to_all(block, 'z', 0, 0, tiled=True)  10.9 us
    pallas_call x1, Pallas kernels, per_device(): pl.pallas_call(second_kernel, out_shape=(shape(GROUPS, NODES, CELLS), sha...  8.99 us
    pallas_call x1, Pallas kernels, per_device(): pl.pallas_call(first_kernel, out_shape=(shape(GROUPS, 8, LANES, dtype=jnp...  8.8 us
    pallas_call x1, Pallas kernels, per_device(): pl.pallas_call(fields_kernel, out_shape=shape(24, LANES), in_specs=[VMEM]...  4.85 us
  transfers between devices with their start and end apart: 2, of which 2 were waited for; matrix products, arithmetic and copies ran while one was open for 0% of the time, Pallas kernels for 0%

profile of v2, /device:TPU:1, one launch (start us, length us, event | category | flops | bytes accessed | tf_op | source)
XLA Modules:
  0.0 160.5 jit_solution(4153647104039427298)
XLA Ops:
  0.6 0.0 copy-start.1
  0.6 0.7 convert_bitcast_fusion.1
  1.3 0.0 copy-start
  1.3 0.7 convert_element_type.23
  2.0 0.0 copy-done.1
  2.0 0.0 copy-done
  2.0 0.1 pad.7.clone
  2.1 0.1 maximum_maximum_fusion
  2.2 2.0 %pad_maximum_fusion = f32[8,96,256]{2,1,0:T(8,128)} fusion(f32[8,32,256]{2,1,0:T(8,128)S(1)} %broadcast_in_dim.24, f32[8,64,256]{2,1,0:T(8,128)} %bitcast.14), kind=kLoop, calls=%fused_computation | loop fusion | flops 196608 | bytes 1572864 | tf_op jit(solution)/shard_map/concatenate | solution.py:399
  4.2 10.9 %all-to-all-start = ((f32[8,96,256]{2,1,0:T(8,128)}), f32[8,96,256]{2,1,0:T(8,128)S(1)}, u32[]{:S(2)}, u32[]{:S(2)}) async-start(f32[8,96,256]{2,1,0:T(8,128)} %pad_maximum_fusion), calls=%async_computation | async-start | bytes 1572864 | tf_op jit(solution)/shard_map/all_to_all | solution.py:402
  15.1 0.1 fusion.1.node_ref
  15.2 23.5 %all-to-all-done.block_ref = f32[8,96,256]{2,1,0:T(8,128)S(1)} async-done(((f32[8,96,256]{2,1,0:T(8,128)}), f32[8,96,256]{2,1,0:T(8,128)S(1)}, u32[]{:S(2)}, u32[]{:S(2)}) %all-to-all-start) | async-done | bytes 786464 | tf_op jit(solution)/shard_map/all_to_all | solution.py:402
  38.7 8.8 %shard_map.68 = (s32[8,8,128]{2,1,0:T(8,128)S(1)}, f32[8,64,256]{2,1,0:T(8,128)S(1)}, f32[16,16,128]{2,1,0:T(8,128)S(1)}) custom-call(f32[1,4]{1,0:T(1,128)S(1)} %fusion.1.node_ref, f32[8,96,256]{2,1,0:T(8,128)S(1)} %all-to-all-done.block_ref), custom_call_target="tpu_custom_call" | custom-call | tf_op jit(solution)/shard_map/pallas_call | solution.py:404
  47.5 12.1 %all_to_all.40 = f32[16,16,128]{2,1,0:T(8,128)S(1)} all-to-all(f32[16,16,128]{2,1,0:T(8,128)S(1)} %get-tuple-element.9), channel_id=1, replica_groups=mesh['z'=8,'x'=4,'y'=8,'c'=2] {'z','c'}, dimensions={0} | all-to-all | bytes 262144 | tf_op jit(solution)/shard_map/all_to_all | solution.py:417
  59.6 20.2 %all_to_all.41.parts_ref = f32[32,16,128]{2,1,0:T(8,128)S(1)} all-to-all(f32[32,16,128]{2,1,0:T(8,128)S(1)} %broadcast_in_dim.25), channel_id=1, replica_groups=mesh['z'=8,'x'=4,'y'=8,'c'=2] {'x','y'}, dimensions={0} | all-to-all | bytes 524288 | tf_op jit(solution)/shard_map/all_to_all | solution.py:380
  79.8 4.8 %shard_map.69 = f32[24,128]{1,0:T(8,128)S(1)} custom-call(f32[32,16,128]{2,1,0:T(8,128)S(1)} %all_to_all.41.parts_ref), custom_call_target="tpu_custom_call" | custom-call | tf_op jit(solution)/shard_map/pallas_call | solution.py:418
  84.7 14.9 %all_to_all.42.params_ref = f32[16,24,128]{2,1,0:T(8,128)S(1)} all-to-all(f32[16,24,128]{2,1,0:T(8,128)S(1)} %broadcast_in_dim.26), channel_id=1, replica_groups=mesh['z'=8,'x'=4,'y'=8,'c'=2] {'z','c'}, dimensions={0} | all-to-all | bytes 393216 | tf_op jit(solution)/shard_map/all_to_all | solution.py:380
  99.7 9.0 %shard_map.70 = (f32[8,64,256]{2,1,0:T(8,128)}, f32[16,8,128]{2,1,0:T(8,128)S(1)}) custom-call(f32[1,4]{1,0:T(1,128)S(1)} %fusion.1.node_ref, f32[8,96,256]{2,1,0:T(8,128)S(1)} %all-to-all-done.block_ref, s32[8,8,128]{2,1,0:T(8,128)S(1)} %get-tuple-element.7.near_ref, f32[8,64,256]{2,1,0:T(8,128)S(1)} %get-tuple-element.8.flux_ref, ...), custom_call_target="tpu_custom_call" | custom-call | tf_op jit(solution)/shard_map/pallas_call | solution.py:428
  108.6 10.5 %all_to_all.43 = f32[16,8,128]{2,1,0:T(8,128)S(1)} all-to-all(f32[16,8,128]{2,1,0:T(8,128)S(1)} %get-tuple-element.11), channel_id=1, replica_groups=mesh['z'=8,'x'=4,'y'=8,'c'=2] {'z','c'}, dimensions={0} | all-to-all | bytes 131072 | tf_op jit(solution)/shard_map/all_to_all | solution.py:438
  119.2 13.6 %all_to_all.44.parts_ref = f32[32,8,128]{2,1,0:T(8,128)S(1)} all-to-all(f32[32,8,128]{2,1,0:T(8,128)S(1)} %broadcast_in_dim.27), channel_id=1, replica_groups=mesh['z'=8,'x'=4,'y'=8,'c'=2] {'x','y'}, dimensions={0} | all-to-all | bytes 262144 | tf_op jit(solution)/shard_map/all_to_all | solution.py:380
  132.7 0.1 shard_map.71
  132.8 5.5 %all_to_all.45 = f32[2,16,128]{2,1,0:T(8,128)S(1)} all-to-all(f32[2,16,128]{2,1,0:T(8,128)S(1)} %broadcast_in_dim.28), channel_id=1, replica_groups=mesh['z'=8,'x'=4,'y'=8,'c'=2] {'c'}, dimensions={0} | all-to-all | bytes 32768 | tf_op jit(solution)/shard_map/all_to_all | solution.py:380
  138.3 3.5 %all-to-all-start.4 = ((f32[8,64,256]{2,1,0:T(8,128)}), f32[8,64,256]{2,1,0:T(8,128)S(1)}, u32[]{:S(2)}, u32[]{:S(2)}) async-start(f32[8,64,256]{2,1,0:T(8,128)} %get-tuple-element.10), calls=%async_computation.4 | async-start | bytes 1048576 | tf_op jit(solution)/shard_map/all_to_all | solution.py:437
  141.8 0.6 pad_maximum_fusion.1
  142.4 17.3 %all-to-all-done.4 = f32[8,64,256]{2,1,0:T(8,128)S(1)} async-done(((f32[8,64,256]{2,1,0:T(8,128)}), f32[8,64,256]{2,1,0:T(8,128)S(1)}, u32[]{:S(2)}, u32[]{:S(2)}) %all-to-all-start.4) | async-done | bytes 524320 | tf_op jit(solution)/shard_map/all_to_all | solution.py:437
  159.7 0.8 copy.9
  (11 shorter events, 0.1 us)
Async XLA Ops:
  0.6 1.4 copy-start.1
  1.3 0.7 copy-start
  4.2 34.4 %all-to-all-start = ((f32[8,96,256]{2,1,0:T(8,128)}), f32[8,96,256]{2,1,0:T(8,128)S(1)}, u32[]{:S(2)}, u32[]{:S(2)}) async-start(f32[8,96,256]{2,1,0:T(8,128)} %pad_maximum_fusion), calls=%async_computation | async-start | bytes 1572864 | tf_op jit(solution)/shard_map/all_to_all | solution.py:402
  138.3 21.4 %all-to-all-start.4 = ((f32[8,64,256]{2,1,0:T(8,128)}), f32[8,64,256]{2,1,0:T(8,128)S(1)}, u32[]{:S(2)}, u32[]{:S(2)}) async-start(f32[8,64,256]{2,1,0:T(8,128)} %get-tuple-element.10), calls=%async_computation.4 | async-start | bytes 1048576 | tf_op jit(solution)/shard_map/all_to_all | solution.py:437

commit v3 on v2

--- a/solution.py
+++ b/solution.py
@@ -25,8 +25,7 @@
 ROW_ADJ = NODES
 ROW_NORMAL = ROW_ADJ + FACES
 ROW_SEND = ROW_NORMAL + 3 * FACES
-ROW_COUNT = ROW_SEND + GROUPS
-ROWS = ROW_COUNT + GROUPS
+ROWS = ROW_SEND + GROUPS
 
 HIGHEST = lax.Precision.HIGHEST
 PARAMS = pltpu.CompilerParams(vmem_limit_bytes=48 * 1024 * 1024)
@@ -45,23 +44,33 @@
     return ((row & (VXY - 1)).astype(jnp.float32) - (VXY - 1) / 2.0) * spacing
 
 
+def pack_kernel(value_ref, adjacency_ref, normal_ref, send_ref, count_ref, out_ref):
+    adj = adjacency_ref[...]
+    place = adj - CELLS
+    counts = count_ref[...] * TILE
+    end = jnp.zeros((1, 1), jnp.int32)
+    source = jnp.zeros(adj.shape, jnp.int32)
+    start = jnp.zeros(adj.shape, jnp.int32)
+    for s in range(GROUPS - 1):
+        end = end + counts[:, s : s + 1]
+        past = end <= place
+        source = source + jnp.where(past, 1, 0)
+        start = jnp.where(past, end, start)
+    slot = jnp.clip(place - start, 0, CELLS - 1)
+    rows = [jnp.where(adj < CELLS, adj, CELLS + CELLS * source + slot).astype(jnp.float32)]
+    rows += [normal_ref[d] for d in range(3)]
+    rows = jnp.concatenate(rows + [send_ref[0].astype(jnp.float32)], axis=0)
+    for g in range(GROUPS):
+        out_ref[g, :NODES, :] = value_ref[g * NODES : (g + 1) * NODES, :]
+        out_ref[g, NODES:, :] = rows
+
+
 def neighbour_tiles(block_ref, g):
     adj = block_ref[g, ROW_ADJ : ROW_ADJ + FACES, :]
-    adj = jnp.concatenate([adj[:, :LANES], adj[:, LANES:]], axis=0)
-    place = adj - CELLS
-    end = jnp.zeros((1, LANES), jnp.float32)
-    source = jnp.zeros(adj.shape, jnp.float32)
-    start = jnp.zeros(adj.shape, jnp.float32)
-    for s in range(GROUPS):
-        end = end + TILE * block_ref[g, ROW_COUNT + s : ROW_COUNT + s + 1, :LANES]
-        past = end <= place
-        source = source + jnp.where(past, 1.0, 0.0)
-        if s < GROUPS - 1:
-            start = jnp.where(past, jnp.broadcast_to(end, adj.shape), start)
-    source = jnp.minimum(source, GROUPS - 1.0)
-    slot = jnp.clip(place - start, 0.0, CELLS - 1.0).astype(jnp.int32)
-    table = source.astype(jnp.int32) * 2 + (slot >> 7)
-    lane = slot & (LANES - 1)
+    adj = jnp.concatenate([adj[:, :LANES], adj[:, LANES:]], axis=0).astype(jnp.int32)
+    place = jnp.maximum(adj - CELLS, 0)
+    table = place >> 7
+    lane = place & (LANES - 1)
     mine = lax.broadcasted_iota(jnp.int32, adj.shape, 0) == g
     listed = jnp.zeros(adj.shape, jnp.float32)
     for s in range(GROUPS):
@@ -70,9 +79,8 @@
             row = column_sum(jnp.where(mine, rows, 0.0))
             found = take_lanes(jnp.broadcast_to(row, adj.shape), lane)
             listed = jnp.where(table == s * 2 + half, found, listed)
-    far = source * CELLS + listed
-    own = adj + jnp.float32(CELLS) * lax.convert_element_type(g, jnp.float32)
-    return jnp.where(adj < CELLS, own, far).astype(jnp.int32)
+    far = (place >> 8) * CELLS + listed.astype(jnp.int32)
+    return jnp.where(adj < CELLS, adj + CELLS * g, far)
 
 
 def split_terms(value_ref, terms_ref, g):
@@ -97,22 +105,25 @@
             both = jnp.dot(terms_ref[s], chosen, preferred_element_type=jnp.float32)
             got = both[:NODES] + both[NODES:]
             found = got if s == 0 else jnp.where(group == s, got, found)
-        normal = [normal_ref[g, ROW_NORMAL + 3 * face + d : ROW_NORMAL + 3 * face + d + 1, :] for d in range(3)]
+        normal = [normal_ref[g, ROW_NORMAL + FACES * d + face : ROW_NORMAL + FACES * d + face + 1, :] for d in range(3)]
         fixed = [normal[1] * node_ref[0, y] + normal[2] * node_ref[0, 2] for y in range(2)]
         speed = normal[0] * x + jnp.where(second, fixed[1], fixed[0])
         total = total + speed * jnp.where(speed > 0.0, own, found)
     return total
 
 
-def moment_table(node_ref, third):
-    row = lax.broadcasted_iota(jnp.int32, (8, NODES), 0)
-    col = lax.broadcasted_iota(jnp.int32, (8, NODES), 1)
+def moment_table(node_ref, rows, cols):
+    row = lax.broadcasted_iota(jnp.int32, (rows, cols), 0)
+    col = lax.broadcasted_iota(jnp.int32, (rows, cols), 1)
+    if rows > 8:
+        row = jnp.where(col >= NODES, row - 6, jnp.where(row < 6, row, rows))
+        col = col & (NODES - 1)
     x = ((col & (VXY - 1)).astype(jnp.float32) - (VXY - 1) / 2.0) * spacing
     y = jnp.where(col >= VXY, node_ref[0, 1], node_ref[0, 0])
     flat = x * x + y * y
-    table = jnp.zeros((8, NODES), jnp.float32)
+    table = jnp.zeros((rows, cols), jnp.float32)
     picks = [jnp.ones_like(x), x, y, x * x, y * y, x * y]
-    if third:
+    if rows == 8:
         picks += [x * flat, y * flat]
     for i, pick in enumerate(picks):
         table = jnp.where(row == i, pick, table)
@@ -120,7 +131,7 @@
 
 
 def first_kernel(node_ref, block_ref, near_ref, flux_ref, sums_ref, terms_ref):
-    table = moment_table(node_ref, False)
+    table = moment_table(node_ref, 16, 2 * NODES)
     for g in range(GROUPS):
         split_terms(block_ref, terms_ref, g)
 
@@ -129,11 +140,13 @@
         near_ref[g] = near
         flux = transport(block_ref, terms_ref, block_ref, near, node_ref, g)
         flux_ref[g] = flux
-        own = block_ref[g, :NODES, :]
-        for base, value in ((0, own), (8, flux)):
-            sums = jnp.dot(table, value, precision=HIGHEST, preferred_element_type=jnp.float32)
-            for half in range(2):
-                sums_ref[g * 2 + half, base : base + 8, :] = sums[:, half * LANES : (half + 1) * LANES]
+        both = jnp.concatenate([block_ref[g, :NODES, :], flux], axis=0)
+        sums = jnp.dot(table, both, precision=HIGHEST, preferred_element_type=jnp.float32)
+        for half in range(2):
+            for q in range(3):
+                sums_ref[g * 2 + half, :, q * LANES : (q + 1) * LANES] = sums[
+                    q * 4 : q * 4 + 4, half * LANES : (half + 1) * LANES
+                ]
         return carry
 
     lax.fori_loop(0, GROUPS, group, 0)
@@ -253,34 +266,36 @@
         out_ref[base + i : base + i + 1, :] = row
 
 
-def level_sums(parts_ref, rows):
-    zero = jnp.zeros((rows, LANES), jnp.float32)
-    s0, s1, s2, s3 = zero, zero, zero, zero
+def level_sums(parts_ref, orders):
+    sums = [jnp.zeros(parts_ref.shape[1:], jnp.float32) for _ in range(orders)]
     for i in range(LEVELS):
         part = parts_ref[i]
-        z = level(i)
-        s0 = s0 + part
-        s1 = s1 + z * part
-        s2 = s2 + (z * z) * part
-        if rows == 8:
-            s3 = s3 + (z * z * z) * part
-    return s0, s1, s2, s3
-
-
-def ten(s0, s1, s2, base):
-    def row(a, i):
-        return a[base + i : base + i + 1, :] / TOTAL
-
+        for order in range(orders):
+            sums[order] = sums[order] + level(i) ** order * part
+    return sums
+
+
+def ten(row0, row1, row2):
     return [
-        row(s0, 0), row(s0, 1), row(s0, 2), row(s1, 0), row(s0, 3), row(s0, 4), row(s2, 0),
-        row(s0, 5), row(s1, 1), row(s1, 2),
+        row0(0), row0(1), row0(2), row1(0), row0(3), row0(4), row2(0), row0(5), row1(1), row1(2),
     ]
 
 
 def fields_kernel(parts_ref, out_ref, pair_ref, row_ref, col_ref):
-    s0, s1, s2, _ = level_sums(parts_ref, 16)
-    now = ten(s0, s1, s2, 0)
-    moved = ten(s0, s1, s2, 8)
+    sums = level_sums(parts_ref, 3)
+
+    def rows(base):
+        def of(a):
+            def row(i):
+                i = base + i
+                return a[i % 4 : i % 4 + 1, i // 4 * LANES : (i // 4 + 1) * LANES] / TOTAL
+
+            return row
+
+        return [of(a) for a in sums]
+
+    now = ten(*rows(0))
+    moved = ten(*rows(6))
     density, mean, inverse, collide = coefficients(now)
     gauss = equilibrium_moments(mean, inverse, pair_ref, row_ref, col_ref)
     beta = time_step * collide * density * TOTAL / gauss[0]
@@ -310,7 +325,7 @@
 
 
 def second_kernel(node_ref, block_ref, near_ref, flux_ref, params_ref, out_ref, sums_ref, value_ref, terms_ref):
-    table = moment_table(node_ref, True)
+    table = moment_table(node_ref, 8, NODES)
 
     def first_step(g, carry):
         for half in range(2):
@@ -338,17 +353,12 @@
 
 
 def final_kernel(parts_ref, out_ref):
-    s0, s1, s2, s3 = level_sums(parts_ref, 8)
-
-    def row(a, i):
-        return a[i : i + 1, :] / TOTAL
-
-    density, (ux, uy, uz), b, theta, _ = macroscopic(ten(s0, s1, s2, 0))
-    third = [
-        row(s0, 6) + row(s2, 1),
-        row(s0, 7) + row(s2, 2),
-        row(s1, 3) + row(s1, 4) + row(s3, 0),
-    ]
+    def of(a):
+        return lambda i: a[i : i + 1, :] / TOTAL
+
+    row0, row1, row2, row3 = (of(a) for a in level_sums(parts_ref, 4))
+    density, (ux, uy, uz), b, theta, _ = macroscopic(ten(row0, row1, row2))
+    third = [row0(6) + row2(1), row0(7) + row2(2), row1(3) + row1(4) + row3(0)]
     trace = b[0] + b[1] + b[2]
     square = ux * ux + uy * uy + uz * uz
     stress = (
@@ -387,18 +397,13 @@
     node = jnp.stack([row, row + 1, vel // 2, vel // 2]).astype(jnp.float32)
     node = ((node - (VXY - 1) / 2.0) * spacing).reshape(1, 4)
 
-    extra = jnp.concatenate(
-        [
-            adjacency.astype(jnp.float32),
-            normals.reshape(3 * FACES, CELLS),
-            send_list[0].astype(jnp.float32),
-            jnp.broadcast_to(block_counts.astype(jnp.float32), (GROUPS, CELLS)),
-        ],
-        axis=0,
-    )
-    block = jnp.concatenate(
-        [distribution.reshape(GROUPS, NODES, CELLS), jnp.broadcast_to(extra, (GROUPS, *extra.shape))], axis=1
-    )
+    block = pl.pallas_call(
+        pack_kernel,
+        out_shape=shape(GROUPS, ROWS, CELLS),
+        in_specs=[VMEM] * 5,
+        out_specs=VMEM,
+        compiler_params=PARAMS,
+    )(distribution, adjacency, jnp.transpose(normals, (1, 0, 2)), send_list, block_counts.reshape(1, GROUPS))
     block = lax.all_to_all(block, "z", 0, 0, tiled=True)
 
     near, flux, sums = pl.pallas_call(
@@ -406,7 +411,7 @@
         out_shape=(
             shape(GROUPS, 8, LANES, dtype=jnp.int32),
             shape(GROUPS, NODES, CELLS),
-            shape(TILES, 16, LANES),
+            shape(TILES, 4, 3 * LANES),
         ),
         in_specs=[SMEM, VMEM],
         out_specs=(VMEM, VMEM, VMEM),
@@ -443,8 +448,11 @@
         out_specs=VMEM,
         compiler_params=PARAMS,
     )(spread(mine, ("x", "y"), LEVELS))
-    both = spread(fields, "c", 2)
-    return relaxed, jnp.concatenate([both[0], both[1]], axis=1)[:13]
+    other = lax.ppermute(fields, "c", [(0, 1), (1, 0)])
+    fields = jnp.where(
+        c == 0, jnp.concatenate([fields, other], axis=1), jnp.concatenate([other, fields], axis=1)
+    )
+    return relaxed, fields[:13]
 
 
 def solution(mesh):

time: 161 us -> 153 us (0.950); the launches traced: 161 us -> 151 us
  waiting for transfers between devices: 40.8 us -> 33 us
  blocking collectives: 76.8 us -> 69.2 us
  starting transfers between devices: 14.4 us -> 18.4 us
  local copies, waits for them, and re-layouts: 0.97 us -> 4.63 us
  other arithmetic: 4.16 us -> 0.74 us
    all_to_all x1, waiting for transfers between devices: 17.3 us -> 10.1 us  [per_device(): lax.all_to_all(value, 'z', 0, 0, tiled=True).reshape(GROUPS * NODES, CELLS)]
    all_to_all x4 -> x3, blocking collectives: 54.2 us -> 47.3 us  [spread(): return lax.all_to_all(copies, axes, 0, 0, tiled=True)]
    ppermute x0 -> x1, starting transfers between devices: none -> 4.01 us  [per_device(): other = lax.ppermute(fields, 'c', [(0, 1), (1, 0)])]
    unnamed x6 -> x11, local copies, waits for them, and re-layouts: 0.81 us -> 4.57 us
    concatenate x3 -> x0, other arithmetic: 2.67 us -> none  [the longest x1 1.99 us: per_device(): jnp.concatenate([distribution.reshape(GROUPS, NODES, CELLS), jnp.broadcas...]
  transfers between devices with their start and end apart: 2 -> 3, of which waited for: 2 -> 3; matrix products, arithmetic and copies ran while one was open for 0% -> 0% of each run, Pallas kernels for 0% -> 0%
where the time goes in v3:
time: 153 us; the launch traced here: 151 us
  blocking collectives  69.2 us (45%)
  waiting for transfers between devices  33 us (22%)
  Pallas kernels  24.1 us (16%)
  starting transfers between devices  18.4 us (12%)
  local copies, waits for them, and re-layouts  4.63 us (3%)
    all_to_all x3, blocking collectives, spread(): return lax.all_to_all(copies, axes, 0, 0, tiled=True)  47.3 us
    all_to_all x1, waiting for transfers between devices, per_device(): block = lax.all_to_all(block, 'z', 0, 0, tiled=True)  22.1 us
    all_to_all x2, blocking collectives, per_device(): mine = jnp.sum(lax.all_to_all(sums, ('z', 'c'), 0, 0, tiled=True), axis=0)  21.9 us
    all_to_all x1, starting transfers between devices, per_device(): block = lax.all_to_all(block, 'z', 0, 0, tiled=True)  10.9 us
    all_to_all x1, waiting for transfers between devices, per_device(): lax.all_to_all(value, 'z', 0, 0, tiled=True).reshape(GROUPS * NODES, CELLS)  10.1 us
    pallas_call x1, Pallas kernels, per_device(): pl.pallas_call(first_kernel, out_shape=(shape(GROUPS, 8, LANES, dtype=jnp...  9.22 us
    pallas_call x1, Pallas kernels, per_device(): pl.pallas_call(second_kernel, out_shape=(shape(GROUPS, NODES, CELLS), sha...  8.98 us
    pallas_call x1, Pallas kernels, per_device(): pl.pallas_call(fields_kernel, out_shape=shape(24, LANES), in_specs=[VMEM]...  4.84 us
  transfers between devices with their start and end apart: 3, of which 3 were waited for; matrix products, arithmetic and copies ran while one was open for 0% of the time, Pallas kernels for 0%

profile of v3, /device:TPU:1, one launch (start us, length us, event | category | flops | bytes accessed | tf_op | source)
XLA Modules:
  0.0 150.8 jit_solution(11635597597420205978)
XLA Ops:
  0.6 0.0 copy-start.4
  0.6 0.6 copy-done.4
  1.3 0.0 copy-start
  1.3 1.0 copy-done
  2.3 0.0 copy-start.1
  2.3 0.7 copy-done.1
  3.0 0.0 copy-start.2
  3.0 0.7 copy-done.2
  3.7 0.0 copy-start.3
  3.7 0.7 copy-done.3
  4.4 1.0 shard_map.68
  5.5 10.9 %all-to-all-start = ((f32[8,88,256]{2,1,0:T(8,128)}), f32[8,88,256]{2,1,0:T(8,128)S(1)}, u32[]{:S(2)}, u32[]{:S(2)}) async-start(f32[8,88,256]{2,1,0:T(8,128)} %shard_map.68), calls=%async_computation | async-start | bytes 1441792 | tf_op jit(solution)/shard_map/all_to_all | solution.py:407
  16.3 0.1 fusion.2.node_ref
  16.4 22.1 %all-to-all-done.block_ref = f32[8,88,256]{2,1,0:T(8,128)S(1)} async-done(((f32[8,88,256]{2,1,0:T(8,128)}), f32[8,88,256]{2,1,0:T(8,128)S(1)}, u32[]{:S(2)}, u32[]{:S(2)}) %all-to-all-start) | async-done | bytes 720928 | tf_op jit(solution)/shard_map/all_to_all | solution.py:407
  38.5 9.2 %shard_map.69 = (s32[8,8,128]{2,1,0:T(8,128)S(1)}, f32[8,64,256]{2,1,0:T(8,128)S(1)}, f32[16,4,384]{2,1,0:T(4,128)S(1)}) custom-call(f32[1,4]{1,0:T(1,128)S(1)} %fusion.2.node_ref, f32[8,88,256]{2,1,0:T(8,128)S(1)} %all-to-all-done.block_ref), custom_call_target="tpu_custom_call" | custom-call | tf_op jit(solution)/shard_map/pallas_call | solution.py:409
  47.7 11.5 %all_to_all.35 = f32[16,4,384]{2,1,0:T(4,128)S(1)} all-to-all(f32[16,4,384]{2,1,0:T(4,128)S(1)} %get-tuple-element.9), channel_id=1, replica_groups=mesh['z'=8,'x'=4,'y'=8,'c'=2] {'z','c'}, dimensions={0} | all-to-all | bytes 196608 | tf_op jit(solution)/shard_map/all_to_all | solution.py:422
  59.2 19.3 %all_to_all.36.parts_ref = f32[32,4,384]{2,1,0:T(4,128)S(1)} all-to-all(f32[32,4,384]{2,1,0:T(4,128)S(1)} %broadcast_in_dim.9), channel_id=1, replica_groups=mesh['z'=8,'x'=4,'y'=8,'c'=2] {'x','y'}, dimensions={0} | all-to-all | bytes 393216 | tf_op jit(solution)/shard_map/all_to_all | solution.py:390
  78.5 4.8 %shard_map.70 = f32[24,128]{1,0:T(8,128)S(1)} custom-call(f32[32,4,384]{2,1,0:T(4,128)S(1)} %all_to_all.36.parts_ref), custom_call_target="tpu_custom_call" | custom-call | tf_op jit(solution)/shard_map/pallas_call | solution.py:423
  83.4 15.2 %all_to_all.37.params_ref = f32[16,24,128]{2,1,0:T(8,128)S(1)} all-to-all(f32[16,24,128]{2,1,0:T(8,128)S(1)} %broadcast_in_dim.10), channel_id=1, replica_groups=mesh['z'=8,'x'=4,'y'=8,'c'=2] {'z','c'}, dimensions={0} | all-to-all | bytes 393216 | tf_op jit(solution)/shard_map/all_to_all | solution.py:390
  98.5 9.0 %shard_map.71 = (f32[8,64,256]{2,1,0:T(8,128)}, f32[16,8,128]{2,1,0:T(8,128)S(1)}) custom-call(f32[1,4]{1,0:T(1,128)S(1)} %fusion.2.node_ref, f32[8,88,256]{2,1,0:T(8,128)S(1)} %all-to-all-done.block_ref, s32[8,8,128]{2,1,0:T(8,128)S(1)} %get-tuple-element.7.near_ref, f32[8,64,256]{2,1,0:T(8,128)S(1)} %get-tuple-element.8.flux_ref, ...), custom_call_target="tpu_custom_call" | custom-call | tf_op jit(solution)/shard_map/pallas_call | solution.py:433
  107.5 10.4 %all_to_all.38 = f32[16,8,128]{2,1,0:T(8,128)S(1)} all-to-all(f32[16,8,128]{2,1,0:T(8,128)S(1)} %get-tuple-element.11), channel_id=1, replica_groups=mesh['z'=8,'x'=4,'y'=8,'c'=2] {'z','c'}, dimensions={0} | all-to-all | bytes 131072 | tf_op jit(solution)/shard_map/all_to_all | solution.py:443
  118.0 12.9 %all_to_all.39.parts_ref = f32[32,8,128]{2,1,0:T(8,128)S(1)} all-to-all(f32[32,8,128]{2,1,0:T(8,128)S(1)} %broadcast_in_dim.11), channel_id=1, replica_groups=mesh['z'=8,'x'=4,'y'=8,'c'=2] {'x','y'}, dimensions={0} | all-to-all | bytes 262144 | tf_op jit(solution)/shard_map/all_to_all | solution.py:390
  130.9 3.5 %all-to-all-start.4 = ((f32[8,64,256]{2,1,0:T(8,128)}), f32[8,64,256]{2,1,0:T(8,128)S(1)}, u32[]{:S(2)}, u32[]{:S(2)}) async-start(f32[8,64,256]{2,1,0:T(8,128)} %get-tuple-element.10), calls=%async_computation.4 | async-start | bytes 1048576 | tf_op jit(solution)/shard_map/all_to_all | solution.py:442
  134.4 0.1 shard_map.72
  134.5 4.0 %collective-permute-start = (f32[16,128]{1,0:T(8,128)S(1)}, f32[16,128]{1,0:T(8,128)S(1)}, u32[]{:S(2)}, u32[]{:S(2)}) collective-permute-start(f32[16,128]{1,0:T(8,128)S(1)} %shard_map.72), channel_id=1, source_target_pairs={{0,1},{1,0},{2,3},{3,2},{4,5},{5,4},{6,7},{7,6},{8,9},{9,8},{10,11... | collective-permute-start | bytes 24584 | tf_op jit(solution)/shard_map/ppermute | solution.py:451
  138.5 0.8 collective-permute-done
  139.3 0.6 fusion
  139.9 10.1 %all-to-all-done.4 = f32[8,64,256]{2,1,0:T(8,128)S(1)} async-done(((f32[8,64,256]{2,1,0:T(8,128)}), f32[8,64,256]{2,1,0:T(8,128)S(1)}, u32[]{:S(2)}, u32[]{:S(2)}) %all-to-all-start.4) | async-done | bytes 524320 | tf_op jit(solution)/shard_map/all_to_all | solution.py:442
  150.0 0.8 copy.8
  (5 shorter events, 0.1 us)
Async XLA Ops:
  0.6 0.7 copy-start.4
  1.3 1.0 copy-start
  2.3 0.7 copy-start.1
  3.0 0.7 copy-start.2
  3.7 0.7 copy-start.3
  5.5 33.0 %all-to-all-start = ((f32[8,88,256]{2,1,0:T(8,128)}), f32[8,88,256]{2,1,0:T(8,128)S(1)}, u32[]{:S(2)}, u32[]{:S(2)}) async-start(f32[8,88,256]{2,1,0:T(8,128)} %shard_map.68), calls=%async_computation | async-start | bytes 1441792 | tf_op jit(solution)/shard_map/all_to_all | solution.py:407
  130.9 19.1 %all-to-all-start.4 = ((f32[8,64,256]{2,1,0:T(8,128)}), f32[8,64,256]{2,1,0:T(8,128)S(1)}, u32[]{:S(2)}, u32[]{:S(2)}) async-start(f32[8,64,256]{2,1,0:T(8,128)} %get-tuple-element.10), calls=%async_computation.4 | async-start | bytes 1048576 | tf_op jit(solution)/shard_map/all_to_all | solution.py:442
  134.5 4.8 %collective-permute-start = (f32[16,128]{1,0:T(8,128)S(1)}, f32[16,128]{1,0:T(8,128)S(1)}, u32[]{:S(2)}, u32[]{:S(2)}) collective-permute-start(f32[16,128]{1,0:T(8,128)S(1)} %shard_map.72), channel_id=1, source_target_pairs={{0,1},{1,0},{2,3},{3,2},{4,5},{5,4},{6,7},{7,6},{8,9},{9,8},{10,11... | collective-permute-start | bytes 24584 | tf_op jit(solution)/shard_map/ppermute | solution.py:451

commit v4 on v3

--- a/solution.py
+++ b/solution.py
@@ -27,7 +27,6 @@
 ROW_SEND = ROW_NORMAL + 3 * FACES
 ROWS = ROW_SEND + GROUPS
 
-HIGHEST = lax.Precision.HIGHEST
 PARAMS = pltpu.CompilerParams(vmem_limit_bytes=48 * 1024 * 1024)
 
 
@@ -44,7 +43,26 @@
     return ((row & (VXY - 1)).astype(jnp.float32) - (VXY - 1) / 2.0) * spacing
 
 
-def pack_kernel(value_ref, adjacency_ref, normal_ref, send_ref, count_ref, out_ref):
+def pack_kernel(
+    value_hbm, adjacency_hbm, normal_hbm, send_hbm, count_hbm, out_hbm,
+    adjacency_ref, normal_ref, send_ref, count_ref, rows_ref, in_sem, value_sem, rows_sem,
+):
+    pairs = (
+        (count_hbm, count_ref), (adjacency_hbm, adjacency_ref), (normal_hbm, normal_ref), (send_hbm, send_ref),
+    )
+    small = [pltpu.make_async_copy(a, b, in_sem.at[i]) for i, (a, b) in enumerate(pairs)]
+    for copy in small:
+        copy.start()
+    large = [
+        pltpu.make_async_copy(
+            value_hbm.at[pl.ds(g * NODES, NODES), :], out_hbm.at[g, pl.ds(0, NODES), :], value_sem.at[g]
+        )
+        for g in range(GROUPS)
+    ]
+    for copy in large:
+        copy.start()
+    for copy in small:
+        copy.wait()
     adj = adjacency_ref[...]
     place = adj - CELLS
     counts = count_ref[...] * TILE
@@ -59,28 +77,37 @@
     slot = jnp.clip(place - start, 0, CELLS - 1)
     rows = [jnp.where(adj < CELLS, adj, CELLS + CELLS * source + slot).astype(jnp.float32)]
     rows += [normal_ref[d] for d in range(3)]
-    rows = jnp.concatenate(rows + [send_ref[0].astype(jnp.float32)], axis=0)
-    for g in range(GROUPS):
-        out_ref[g, :NODES, :] = value_ref[g * NODES : (g + 1) * NODES, :]
-        out_ref[g, NODES:, :] = rows
-
-
-def neighbour_tiles(block_ref, g):
-    adj = block_ref[g, ROW_ADJ : ROW_ADJ + FACES, :]
-    adj = jnp.concatenate([adj[:, :LANES], adj[:, LANES:]], axis=0).astype(jnp.int32)
-    place = jnp.maximum(adj - CELLS, 0)
-    table = place >> 7
-    lane = place & (LANES - 1)
-    mine = lax.broadcasted_iota(jnp.int32, adj.shape, 0) == g
-    listed = jnp.zeros(adj.shape, jnp.float32)
-    for s in range(GROUPS):
+    rows_ref[...] = jnp.concatenate(rows + [send_ref[0].astype(jnp.float32)], axis=0)
+    shared = [
+        pltpu.make_async_copy(rows_ref, out_hbm.at[g, pl.ds(NODES, ROWS - NODES), :], rows_sem.at[g])
+        for g in range(GROUPS)
+    ]
+    for copy in shared:
+        copy.start()
+    for copy in large + shared:
+        copy.wait()
+
+
+def find_neighbours(block_ref, near_ref):
+    base = CELLS * lax.broadcasted_iota(jnp.int32, (GROUPS, LANES), 0)
+    for face in range(FACES):
         for half in range(2):
-            rows = block_ref[s, ROW_SEND : ROW_SEND + GROUPS, half * LANES : (half + 1) * LANES]
-            row = column_sum(jnp.where(mine, rows, 0.0))
-            found = take_lanes(jnp.broadcast_to(row, adj.shape), lane)
-            listed = jnp.where(table == s * 2 + half, found, listed)
-    far = (place >> 8) * CELLS + listed.astype(jnp.int32)
-    return jnp.where(adj < CELLS, adj + CELLS * g, far)
+            at = slice(half * LANES, (half + 1) * LANES)
+            adj = jnp.concatenate(
+                [block_ref[g, ROW_ADJ + face : ROW_ADJ + face + 1, at] for g in range(GROUPS)], axis=0
+            ).astype(jnp.int32)
+            place = jnp.maximum(adj - CELLS, 0)
+            table = place >> 7
+            lane = place & (LANES - 1)
+            listed = jnp.zeros(adj.shape, jnp.float32)
+            for s in range(GROUPS):
+                for part in range(2):
+                    rows = block_ref[s, ROW_SEND : ROW_SEND + GROUPS, part * LANES : (part + 1) * LANES]
+                    listed = jnp.where(table == s * 2 + part, take_lanes(rows, lane), listed)
+            far = (place >> 8) * CELLS + listed.astype(jnp.int32)
+            near = jnp.where(adj < CELLS, adj + base, far)
+            for g in range(GROUPS):
+                near_ref[g, face : face + 1, at] = near[g : g + 1, :]
 
 
 def split_terms(value_ref, terms_ref, g):
@@ -97,7 +124,7 @@
     place = lax.broadcasted_iota(jnp.int32, (CELLS, CELLS), 0)
     total = jnp.zeros((NODES, CELLS), jnp.float32)
     for face in range(FACES):
-        row = jnp.concatenate([near[face : face + 1, :], near[FACES + face : FACES + face + 1, :]], axis=1)
+        row = near[face : face + 1, :]
         chosen = jnp.where(place == (row & (CELLS - 1)), 1.0, 0.0).astype(jnp.bfloat16)
         group = row >> 8
         found = None
@@ -112,40 +139,41 @@
     return total
 
 
-def moment_table(node_ref, rows, cols):
-    row = lax.broadcasted_iota(jnp.int32, (rows, cols), 0)
-    col = lax.broadcasted_iota(jnp.int32, (rows, cols), 1)
-    if rows > 8:
-        row = jnp.where(col >= NODES, row - 6, jnp.where(row < 6, row, rows))
-        col = col & (NODES - 1)
-    x = ((col & (VXY - 1)).astype(jnp.float32) - (VXY - 1) / 2.0) * spacing
-    y = jnp.where(col >= VXY, node_ref[0, 1], node_ref[0, 0])
-    flat = x * x + y * y
-    table = jnp.zeros((rows, cols), jnp.float32)
-    picks = [jnp.ones_like(x), x, y, x * x, y * y, x * y]
-    if rows == 8:
-        picks += [x * flat, y * flat]
-    for i, pick in enumerate(picks):
-        table = jnp.where(row == i, pick, table)
-    return table
+def plane_sums(value, node_ref, third):
+    x = node_x(VXY, value.shape[1])
+    sums = []
+    for y in range(2):
+        part = value[y * VXY : (y + 1) * VXY, :]
+        powers = [part]
+        for _ in range(3 if third else 2):
+            powers.append(x * powers[-1])
+        sums.append([column_sum(p) for p in powers])
+    low, high = sums
+    ya, yb = node_ref[0, 0], node_ref[0, 1]
+
+    def over(i, order=0):
+        return ya**order * low[i] + yb**order * high[i] if order else low[i] + high[i]
+
+    rows = [over(0), over(1), over(0, 1), over(2), over(0, 2), over(1, 1)]
+    if third:
+        rows += [over(3) + over(1, 2), over(2, 1) + over(0, 3)]
+    return rows
 
 
 def first_kernel(node_ref, block_ref, near_ref, flux_ref, sums_ref, terms_ref):
-    table = moment_table(node_ref, 16, 2 * NODES)
+    find_neighbours(block_ref, near_ref)
     for g in range(GROUPS):
         split_terms(block_ref, terms_ref, g)
 
     def group(g, carry):
-        near = neighbour_tiles(block_ref, g)
-        near_ref[g] = near
-        flux = transport(block_ref, terms_ref, block_ref, near, node_ref, g)
+        flux = transport(block_ref, terms_ref, block_ref, near_ref[g], node_ref, g)
         flux_ref[g] = flux
-        both = jnp.concatenate([block_ref[g, :NODES, :], flux], axis=0)
-        sums = jnp.dot(table, both, precision=HIGHEST, preferred_element_type=jnp.float32)
-        for half in range(2):
-            for q in range(3):
-                sums_ref[g * 2 + half, :, q * LANES : (q + 1) * LANES] = sums[
-                    q * 4 : q * 4 + 4, half * LANES : (half + 1) * LANES
+        rows = plane_sums(block_ref[g, :NODES, :], node_ref, False) + plane_sums(flux, node_ref, False)
+        for i, row in enumerate(rows):
+            for half in range(2):
+                q = i // 4
+                sums_ref[g * 2 + half, i % 4 : i % 4 + 1, q * LANES : (q + 1) * LANES] = row[
+                    :, half * LANES : (half + 1) * LANES
                 ]
         return carry
 
@@ -325,8 +353,6 @@
 
 
 def second_kernel(node_ref, block_ref, near_ref, flux_ref, params_ref, out_ref, sums_ref, value_ref, terms_ref):
-    table = moment_table(node_ref, 8, NODES)
-
     def first_step(g, carry):
         for half in range(2):
             at = slice(half * LANES, (half + 1) * LANES)
@@ -344,9 +370,8 @@
             at = slice(half * LANES, (half + 1) * LANES)
             value = relaxed_tile(value_ref[g, :, at], flux[:, at], params_ref, 12, g * 2 + half, node_ref)
             out_ref[g, :, at] = value
-            sums_ref[g * 2 + half] = jnp.dot(
-                table, value, precision=HIGHEST, preferred_element_type=jnp.float32
-            )
+            for i, row in enumerate(plane_sums(value, node_ref, True)):
+                sums_ref[g * 2 + half, i : i + 1, :] = row
         return carry
 
     lax.fori_loop(0, GROUPS, second_step, 0)
@@ -380,6 +405,7 @@
 
 
 VMEM = pl.BlockSpec(memory_space=pltpu.VMEM)
+ANY = pl.BlockSpec(memory_space=pl.ANY)
 SMEM = pl.BlockSpec(memory_space=pltpu.SMEM)
 TERMS = pltpu.VMEM((GROUPS, 2 * NODES, CELLS), jnp.bfloat16)
 TABLES = [pltpu.VMEM((VXY, VXY, LANES), jnp.float32)] * 3
@@ -400,16 +426,26 @@
     block = pl.pallas_call(
         pack_kernel,
         out_shape=shape(GROUPS, ROWS, CELLS),
-        in_specs=[VMEM] * 5,
-        out_specs=VMEM,
-        compiler_params=PARAMS,
+        in_specs=[ANY] * 5,
+        out_specs=ANY,
+        scratch_shapes=[
+            pltpu.VMEM((FACES, CELLS), jnp.int32),
+            pltpu.VMEM((3, FACES, CELLS), jnp.float32),
+            pltpu.VMEM((1, GROUPS, CELLS), jnp.int32),
+            pltpu.VMEM((1, GROUPS), jnp.int32),
+            pltpu.VMEM((ROWS - NODES, CELLS), jnp.float32),
+            pltpu.SemaphoreType.DMA((4,)),
+            pltpu.SemaphoreType.DMA((GROUPS,)),
+            pltpu.SemaphoreType.DMA((GROUPS,)),
+        ],
+        compiler_params=pltpu.CompilerParams(vmem_limit_bytes=60 * 1024 * 1024),
     )(distribution, adjacency, jnp.transpose(normals, (1, 0, 2)), send_list, block_counts.reshape(1, GROUPS))
     block = lax.all_to_all(block, "z", 0, 0, tiled=True)
 
     near, flux, sums = pl.pallas_call(
         first_kernel,
         out_shape=(
-            shape(GROUPS, 8, LANES, dtype=jnp.int32),
+            shape(GROUPS, FACES, CELLS, dtype=jnp.int32),
             shape(GROUPS, NODES, CELLS),
             shape(TILES, 4, 3 * LANES),
         ),

time: 153 us -> 162 us (1.059)
  Pallas kernels: 24.1 us -> 37.1 us
  local copies, waits for them, and re-layouts: 4.63 us -> 0.85 us
    pallas_call x1, Pallas kernels: 1.03 us -> 17.2 us  [per_device(): pl.pallas_call(pack_kernel, out_shape=shape(GROUPS, ROWS, CELLS), in_spec...]
    unnamed x11 -> x1, local copies, waits for them, and re-layouts: 4.57 us -> 0.79 us
    pallas_call x1, Pallas kernels: 9.22 us -> 6.95 us  [per_device(): pl.pallas_call(first_kernel, out_shape=(shape(GROUPS, FACES, CELLS, dtype...]
where the time goes in v4:
time: 162 us; the launch traced here: 160 us
  blocking collectives  69.2 us (43%)
  Pallas kernels  37.1 us (23%)
  waiting for transfers between devices  33 us (20%)
  starting transfers between devices  18.4 us (11%)
    all_to_all x3, blocking collectives, spread(): return lax.all_to_all(copies, axes, 0, 0, tiled=True)  47.4 us
    all_to_all x1, waiting for transfers between devices, per_device(): block = lax.all_to_all(block, 'z', 0, 0, tiled=True)  22.1 us
    all_to_all x2, blocking collectives, per_device(): mine = jnp.sum(lax.all_to_all(sums, ('z', 'c'), 0, 0, tiled=True), axis=0)  21.9 us
    pallas_call x1, Pallas kernels, per_device(): pl.pallas_call(pack_kernel, out_shape=shape(GROUPS, ROWS, CELLS), in_spec...  17.2 us
    all_to_all x1, starting transfers between devices, per_device(): block = lax.all_to_all(block, 'z', 0, 0, tiled=True)  10.9 us
    all_to_all x1, waiting for transfers between devices, per_device(): lax.all_to_all(value, 'z', 0, 0, tiled=True).reshape(GROUPS * NODES, CELLS)  10.1 us
    pallas_call x1, Pallas kernels, per_device(): pl.pallas_call(second_kernel, out_shape=(shape(GROUPS, NODES, CELLS), sha...  8.04 us
    pallas_call x1, Pallas kernels, per_device(): pl.pallas_call(first_kernel, out_shape=(shape(GROUPS, FACES, CELLS, dtype...  6.95 us
  transfers between devices with their start and end apart: 3, of which 3 were waited for; matrix products, arithmetic and copies ran while one was open for 0% of the time, Pallas kernels for 0%

profile of v4, /device:TPU:1, one launch (start us, length us, event | category | flops | bytes accessed | tf_op | source)
XLA Modules:
  0.0 159.9 jit_solution(12743247087204463698)
XLA Ops:
  0.6 17.2 %shard_map.68 = f32[8,88,256]{2,1,0:T(8,128)} custom-call(f32[512,256]{1,0:T(8,128)} %value_hbm.1, s32[4,256]{1,0:T(4,128)} %adjacency_hbm.1, f32[3,4,256]{2,1,0:T(4,128)} %bitcast.7, s32[1,8,256]{2,1,0:T(8,128)} %send_hbm.1, s32[1,8]{1,0:T(1,128)} %bitcast.8), custom_call_target="tpu_custom_call" | custom-call | tf_op jit(solution)/shard_map/pallas_call | solution.py:426
  17.8 10.9 %all-to-all-start = ((f32[8,88,256]{2,1,0:T(8,128)}), f32[8,88,256]{2,1,0:T(8,128)S(1)}, u32[]{:S(2)}, u32[]{:S(2)}) async-start(f32[8,88,256]{2,1,0:T(8,128)} %shard_map.68), calls=%async_computation | async-start | bytes 1441792 | tf_op jit(solution)/shard_map/all_to_all | solution.py:443
  28.7 0.1 fusion.2.node_ref
  28.8 22.1 %all-to-all-done.block_ref = f32[8,88,256]{2,1,0:T(8,128)S(1)} async-done(((f32[8,88,256]{2,1,0:T(8,128)}), f32[8,88,256]{2,1,0:T(8,128)S(1)}, u32[]{:S(2)}, u32[]{:S(2)}) %all-to-all-start) | async-done | bytes 720928 | tf_op jit(solution)/shard_map/all_to_all | solution.py:443
  50.9 6.9 %shard_map.69 = (s32[8,4,256]{2,1,0:T(4,128)S(1)}, f32[8,64,256]{2,1,0:T(8,128)S(1)}, f32[16,4,384]{2,1,0:T(4,128)S(1)}) custom-call(f32[1,4]{1,0:T(1,128)S(1)} %fusion.2.node_ref, f32[8,88,256]{2,1,0:T(8,128)S(1)} %all-to-all-done.block_ref), custom_call_target="tpu_custom_call" | custom-call | tf_op jit(solution)/shard_map/pallas_call | solution.py:445
  57.8 11.4 %all_to_all.35 = f32[16,4,384]{2,1,0:T(4,128)S(1)} all-to-all(f32[16,4,384]{2,1,0:T(4,128)S(1)} %get-tuple-element.9), channel_id=1, replica_groups=mesh['z'=8,'x'=4,'y'=8,'c'=2] {'z','c'}, dimensions={0} | all-to-all | bytes 196608 | tf_op jit(solution)/shard_map/all_to_all | solution.py:458
  69.3 19.3 %all_to_all.36.parts_ref = f32[32,4,384]{2,1,0:T(4,128)S(1)} all-to-all(f32[32,4,384]{2,1,0:T(4,128)S(1)} %broadcast_in_dim.9), channel_id=1, replica_groups=mesh['z'=8,'x'=4,'y'=8,'c'=2] {'x','y'}, dimensions={0} | all-to-all | bytes 393216 | tf_op jit(solution)/shard_map/all_to_all | solution.py:416
  88.6 4.8 %shard_map.70 = f32[24,128]{1,0:T(8,128)S(1)} custom-call(f32[32,4,384]{2,1,0:T(4,128)S(1)} %all_to_all.36.parts_ref), custom_call_target="tpu_custom_call" | custom-call | tf_op jit(solution)/shard_map/pallas_call | solution.py:459
  93.5 15.2 %all_to_all.37.params_ref = f32[16,24,128]{2,1,0:T(8,128)S(1)} all-to-all(f32[16,24,128]{2,1,0:T(8,128)S(1)} %broadcast_in_dim.10), channel_id=1, replica_groups=mesh['z'=8,'x'=4,'y'=8,'c'=2] {'z','c'}, dimensions={0} | all-to-all | bytes 393216 | tf_op jit(solution)/shard_map/all_to_all | solution.py:416
  108.6 8.0 %shard_map.71 = (f32[8,64,256]{2,1,0:T(8,128)}, f32[16,8,128]{2,1,0:T(8,128)S(1)}) custom-call(f32[1,4]{1,0:T(1,128)S(1)} %fusion.2.node_ref, f32[8,88,256]{2,1,0:T(8,128)S(1)} %all-to-all-done.block_ref, s32[8,4,256]{2,1,0:T(4,128)S(1)} %get-tuple-element.7.near_ref, f32[8,64,256]{2,1,0:T(8,128)S(1)} %get-tuple-element.8.flux_ref, ...), custom_call_target="tpu_custom_call" | custom-call | tf_op jit(solution)/shard_map/pallas_call | solution.py:469
  116.7 10.4 %all_to_all.38 = f32[16,8,128]{2,1,0:T(8,128)S(1)} all-to-all(f32[16,8,128]{2,1,0:T(8,128)S(1)} %get-tuple-element.11), channel_id=1, replica_groups=mesh['z'=8,'x'=4,'y'=8,'c'=2] {'z','c'}, dimensions={0} | all-to-all | bytes 131072 | tf_op jit(solution)/shard_map/all_to_all | solution.py:479
  127.2 12.9 %all_to_all.39.parts_ref = f32[32,8,128]{2,1,0:T(8,128)S(1)} all-to-all(f32[32,8,128]{2,1,0:T(8,128)S(1)} %broadcast_in_dim.11), channel_id=1, replica_groups=mesh['z'=8,'x'=4,'y'=8,'c'=2] {'x','y'}, dimensions={0} | all-to-all | bytes 262144 | tf_op jit(solution)/shard_map/all_to_all | solution.py:416
  140.1 3.5 %all-to-all-start.4 = ((f32[8,64,256]{2,1,0:T(8,128)}), f32[8,64,256]{2,1,0:T(8,128)S(1)}, u32[]{:S(2)}, u32[]{:S(2)}) async-start(f32[8,64,256]{2,1,0:T(8,128)} %get-tuple-element.10), calls=%async_computation.4 | async-start | bytes 1048576 | tf_op jit(solution)/shard_map/all_to_all | solution.py:478
  143.6 0.1 shard_map.72
  143.6 4.0 %collective-permute-start = (f32[16,128]{1,0:T(8,128)S(1)}, f32[16,128]{1,0:T(8,128)S(1)}, u32[]{:S(2)}, u32[]{:S(2)}) collective-permute-start(f32[16,128]{1,0:T(8,128)S(1)} %shard_map.72), channel_id=1, source_target_pairs={{0,1},{1,0},{2,3},{3,2},{4,5},{5,4},{6,7},{7,6},{8,9},{9,8},{10,11... | collective-permute-start | bytes 24584 | tf_op jit(solution)/shard_map/ppermute | solution.py:487
  147.6 0.8 collective-permute-done
  148.4 0.6 fusion
  149.1 10.1 %all-to-all-done.4 = f32[8,64,256]{2,1,0:T(8,128)S(1)} async-done(((f32[8,64,256]{2,1,0:T(8,128)}), f32[8,64,256]{2,1,0:T(8,128)S(1)}, u32[]{:S(2)}, u32[]{:S(2)}) %all-to-all-start.4) | async-done | bytes 524320 | tf_op jit(solution)/shard_map/all_to_all | solution.py:478
  159.1 0.8 copy.8
  (5 shorter events, 0.1 us)
Async XLA Ops:
  17.8 33.0 %all-to-all-start = ((f32[8,88,256]{2,1,0:T(8,128)}), f32[8,88,256]{2,1,0:T(8,128)S(1)}, u32[]{:S(2)}, u32[]{:S(2)}) async-start(f32[8,88,256]{2,1,0:T(8,128)} %shard_map.68), calls=%async_computation | async-start | bytes 1441792 | tf_op jit(solution)/shard_map/all_to_all | solution.py:443
  140.1 19.1 %all-to-all-start.4 = ((f32[8,64,256]{2,1,0:T(8,128)}), f32[8,64,256]{2,1,0:T(8,128)S(1)}, u32[]{:S(2)}, u32[]{:S(2)}) async-start(f32[8,64,256]{2,1,0:T(8,128)} %get-tuple-element.10), calls=%async_computation.4 | async-start | bytes 1048576 | tf_op jit(solution)/shard_map/all_to_all | solution.py:478
  143.6 4.8 %collective-permute-start = (f32[16,128]{1,0:T(8,128)S(1)}, f32[16,128]{1,0:T(8,128)S(1)}, u32[]{:S(2)}, u32[]{:S(2)}) collective-permute-start(f32[16,128]{1,0:T(8,128)S(1)} %shard_map.72), channel_id=1, source_target_pairs={{0,1},{1,0},{2,3},{3,2},{4,5},{5,4},{6,7},{7,6},{8,9},{9,8},{10,11... | collective-permute-start | bytes 24584 | tf_op jit(solution)/shard_map/ppermute | solution.py:487

commit v5 on v4

--- a/solution.py
+++ b/solution.py
@@ -44,8 +44,8 @@
 
 
 def pack_kernel(
-    value_hbm, adjacency_hbm, normal_hbm, send_hbm, count_hbm, out_hbm,
-    adjacency_ref, normal_ref, send_ref, count_ref, rows_ref, in_sem, value_sem, rows_sem,
+    value_hbm, adjacency_hbm, normal_hbm, send_hbm, count_hbm, out_ref,
+    adjacency_ref, normal_ref, send_ref, count_ref, in_sem, value_sem,
 ):
     pairs = (
         (count_hbm, count_ref), (adjacency_hbm, adjacency_ref), (normal_hbm, normal_ref), (send_hbm, send_ref),
@@ -55,7 +55,7 @@
         copy.start()
     large = [
         pltpu.make_async_copy(
-            value_hbm.at[pl.ds(g * NODES, NODES), :], out_hbm.at[g, pl.ds(0, NODES), :], value_sem.at[g]
+            value_hbm.at[pl.ds(g * NODES, NODES), :], out_ref.at[g, pl.ds(0, NODES), :], value_sem.at[g]
         )
         for g in range(GROUPS)
     ]
@@ -77,14 +77,10 @@
     slot = jnp.clip(place - start, 0, CELLS - 1)
     rows = [jnp.where(adj < CELLS, adj, CELLS + CELLS * source + slot).astype(jnp.float32)]
     rows += [normal_ref[d] for d in range(3)]
-    rows_ref[...] = jnp.concatenate(rows + [send_ref[0].astype(jnp.float32)], axis=0)
-    shared = [
-        pltpu.make_async_copy(rows_ref, out_hbm.at[g, pl.ds(NODES, ROWS - NODES), :], rows_sem.at[g])
-        for g in range(GROUPS)
-    ]
-    for copy in shared:
-        copy.start()
-    for copy in large + shared:
+    rows = jnp.concatenate(rows + [send_ref[0].astype(jnp.float32)], axis=0)
+    for g in range(GROUPS):
+        out_ref[g, NODES:, :] = rows
+    for copy in large:
         copy.wait()
 
 
@@ -427,15 +423,13 @@
         pack_kernel,
         out_shape=shape(GROUPS, ROWS, CELLS),
         in_specs=[ANY] * 5,
-        out_specs=ANY,
+        out_specs=VMEM,
         scratch_shapes=[
             pltpu.VMEM((FACES, CELLS), jnp.int32),
             pltpu.VMEM((3, FACES, CELLS), jnp.float32),
             pltpu.VMEM((1, GROUPS, CELLS), jnp.int32),
             pltpu.VMEM((1, GROUPS), jnp.int32),
-            pltpu.VMEM((ROWS - NODES, CELLS), jnp.float32),
             pltpu.SemaphoreType.DMA((4,)),
-            pltpu.SemaphoreType.DMA((GROUPS,)),
             pltpu.SemaphoreType.DMA((GROUPS,)),
         ],
         compiler_params=pltpu.CompilerParams(vmem_limit_bytes=60 * 1024 * 1024),

time: 162 us -> 147 us (0.907)
  Pallas kernels: 37.1 us -> 22 us
    pallas_call x1, Pallas kernels: 17.2 us -> 2.09 us  [per_device(): pl.pallas_call(pack_kernel, out_shape=shape(GROUPS, ROWS, CELLS), in_spec...]
where the time goes in v5:
time: 147 us; the launch traced here: 145 us
  blocking collectives  69.2 us (47%)
  waiting for transfers between devices  33 us (22%)
  Pallas kernels  22 us (15%)
  starting transfers between devices  18.4 us (13%)
    all_to_all x3, blocking collectives, spread(): return lax.all_to_all(copies, axes, 0, 0, tiled=True)  47.4 us
    all_to_all x1, waiting for transfers between devices, per_device(): block = lax.all_to_all(block, 'z', 0, 0, tiled=True)  22.1 us
    all_to_all x2, blocking collectives, per_device(): mine = jnp.sum(lax.all_to_all(sums, ('z', 'c'), 0, 0, tiled=True), axis=0)  21.9 us
    all_to_all x1, starting transfers between devices, per_device(): block = lax.all_to_all(block, 'z', 0, 0, tiled=True)  10.9 us
    all_to_all x1, waiting for transfers between devices, per_device(): lax.all_to_all(value, 'z', 0, 0, tiled=True).reshape(GROUPS * NODES, CELLS)  10.1 us
    pallas_call x1, Pallas kernels, per_device(): pl.pallas_call(second_kernel, out_shape=(shape(GROUPS, NODES, CELLS), sha...  8.04 us
    pallas_call x1, Pallas kernels, per_device(): pl.pallas_call(first_kernel, out_shape=(shape(GROUPS, FACES, CELLS, dtype...  6.95 us
    pallas_call x1, Pallas kernels, per_device(): pl.pallas_call(fields_kernel, out_shape=shape(24, LANES), in_specs=[VMEM]...  4.84 us
  transfers between devices with their start and end apart: 3, of which 3 were waited for; matrix products, arithmetic and copies ran while one was open for 0% of the time, Pallas kernels for 0%

profile of v5, /device:TPU:1, one launch (start us, length us, event | category | flops | bytes accessed | tf_op | source)
XLA Modules:
  0.0 144.8 jit_solution(3889060618129734041)
XLA Ops:
  0.6 2.1 %shard_map.68 = f32[8,88,256]{2,1,0:T(8,128)} custom-call(f32[512,256]{1,0:T(8,128)} %value_hbm.1, s32[4,256]{1,0:T(4,128)} %adjacency_hbm.1, f32[3,4,256]{2,1,0:T(4,128)} %bitcast.7, s32[1,8,256]{2,1,0:T(8,128)} %send_hbm.1, s32[1,8]{1,0:T(1,128)} %bitcast.8), custom_call_target="tpu_custom_call" | custom-call | tf_op jit(solution)/shard_map/pallas_call | solution.py:422
  2.7 10.9 %all-to-all-start = ((f32[8,88,256]{2,1,0:T(8,128)}), f32[8,88,256]{2,1,0:T(8,128)S(1)}, u32[]{:S(2)}, u32[]{:S(2)}) async-start(f32[8,88,256]{2,1,0:T(8,128)} %shard_map.68), calls=%async_computation | async-start | bytes 1441792 | tf_op jit(solution)/shard_map/all_to_all | solution.py:437
  13.6 0.1 fusion.2.node_ref
  13.7 22.1 %all-to-all-done.block_ref = f32[8,88,256]{2,1,0:T(8,128)S(1)} async-done(((f32[8,88,256]{2,1,0:T(8,128)}), f32[8,88,256]{2,1,0:T(8,128)S(1)}, u32[]{:S(2)}, u32[]{:S(2)}) %all-to-all-start) | async-done | bytes 720928 | tf_op jit(solution)/shard_map/all_to_all | solution.py:437
  35.8 6.9 %shard_map.69 = (s32[8,4,256]{2,1,0:T(4,128)S(1)}, f32[8,64,256]{2,1,0:T(8,128)S(1)}, f32[16,4,384]{2,1,0:T(4,128)S(1)}) custom-call(f32[1,4]{1,0:T(1,128)S(1)} %fusion.2.node_ref, f32[8,88,256]{2,1,0:T(8,128)S(1)} %all-to-all-done.block_ref), custom_call_target="tpu_custom_call" | custom-call | tf_op jit(solution)/shard_map/pallas_call | solution.py:439
  42.7 11.4 %all_to_all.35 = f32[16,4,384]{2,1,0:T(4,128)S(1)} all-to-all(f32[16,4,384]{2,1,0:T(4,128)S(1)} %get-tuple-element.9), channel_id=1, replica_groups=mesh['z'=8,'x'=4,'y'=8,'c'=2] {'z','c'}, dimensions={0} | all-to-all | bytes 196608 | tf_op jit(solution)/shard_map/all_to_all | solution.py:452
  54.2 19.3 %all_to_all.36.parts_ref = f32[32,4,384]{2,1,0:T(4,128)S(1)} all-to-all(f32[32,4,384]{2,1,0:T(4,128)S(1)} %broadcast_in_dim.9), channel_id=1, replica_groups=mesh['z'=8,'x'=4,'y'=8,'c'=2] {'x','y'}, dimensions={0} | all-to-all | bytes 393216 | tf_op jit(solution)/shard_map/all_to_all | solution.py:412
  73.5 4.8 %shard_map.70 = f32[24,128]{1,0:T(8,128)S(1)} custom-call(f32[32,4,384]{2,1,0:T(4,128)S(1)} %all_to_all.36.parts_ref), custom_call_target="tpu_custom_call" | custom-call | tf_op jit(solution)/shard_map/pallas_call | solution.py:453
  78.4 15.2 %all_to_all.37.params_ref = f32[16,24,128]{2,1,0:T(8,128)S(1)} all-to-all(f32[16,24,128]{2,1,0:T(8,128)S(1)} %broadcast_in_dim.10), channel_id=1, replica_groups=mesh['z'=8,'x'=4,'y'=8,'c'=2] {'z','c'}, dimensions={0} | all-to-all | bytes 393216 | tf_op jit(solution)/shard_map/all_to_all | solution.py:412
  93.5 8.0 %shard_map.71 = (f32[8,64,256]{2,1,0:T(8,128)}, f32[16,8,128]{2,1,0:T(8,128)S(1)}) custom-call(f32[1,4]{1,0:T(1,128)S(1)} %fusion.2.node_ref, f32[8,88,256]{2,1,0:T(8,128)S(1)} %all-to-all-done.block_ref, s32[8,4,256]{2,1,0:T(4,128)S(1)} %get-tuple-element.7.near_ref, f32[8,64,256]{2,1,0:T(8,128)S(1)} %get-tuple-element.8.flux_ref, ...), custom_call_target="tpu_custom_call" | custom-call | tf_op jit(solution)/shard_map/pallas_call | solution.py:463
  101.6 10.4 %all_to_all.38 = f32[16,8,128]{2,1,0:T(8,128)S(1)} all-to-all(f32[16,8,128]{2,1,0:T(8,128)S(1)} %get-tuple-element.11), channel_id=1, replica_groups=mesh['z'=8,'x'=4,'y'=8,'c'=2] {'z','c'}, dimensions={0} | all-to-all | bytes 131072 | tf_op jit(solution)/shard_map/all_to_all | solution.py:473
  112.1 12.9 %all_to_all.39.parts_ref = f32[32,8,128]{2,1,0:T(8,128)S(1)} all-to-all(f32[32,8,128]{2,1,0:T(8,128)S(1)} %broadcast_in_dim.11), channel_id=1, replica_groups=mesh['z'=8,'x'=4,'y'=8,'c'=2] {'x','y'}, dimensions={0} | all-to-all | bytes 262144 | tf_op jit(solution)/shard_map/all_to_all | solution.py:412
  125.0 3.5 %all-to-all-start.4 = ((f32[8,64,256]{2,1,0:T(8,128)}), f32[8,64,256]{2,1,0:T(8,128)S(1)}, u32[]{:S(2)}, u32[]{:S(2)}) async-start(f32[8,64,256]{2,1,0:T(8,128)} %get-tuple-element.10), calls=%async_computation.4 | async-start | bytes 1048576 | tf_op jit(solution)/shard_map/all_to_all | solution.py:472
  128.5 0.1 shard_map.72
  128.5 4.0 %collective-permute-start = (f32[16,128]{1,0:T(8,128)S(1)}, f32[16,128]{1,0:T(8,128)S(1)}, u32[]{:S(2)}, u32[]{:S(2)}) collective-permute-start(f32[16,128]{1,0:T(8,128)S(1)} %shard_map.72), channel_id=1, source_target_pairs={{0,1},{1,0},{2,3},{3,2},{4,5},{5,4},{6,7},{7,6},{8,9},{9,8},{10,11... | collective-permute-start | bytes 24584 | tf_op jit(solution)/shard_map/ppermute | solution.py:481
  132.6 0.8 collective-permute-done
  133.4 0.6 fusion
  134.0 10.1 %all-to-all-done.4 = f32[8,64,256]{2,1,0:T(8,128)S(1)} async-done(((f32[8,64,256]{2,1,0:T(8,128)}), f32[8,64,256]{2,1,0:T(8,128)S(1)}, u32[]{:S(2)}, u32[]{:S(2)}) %all-to-all-start.4) | async-done | bytes 524320 | tf_op jit(solution)/shard_map/all_to_all | solution.py:472
  144.0 0.8 copy.8
  (5 shorter events, 0.1 us)
Async XLA Ops:
  2.7 33.0 %all-to-all-start = ((f32[8,88,256]{2,1,0:T(8,128)}), f32[8,88,256]{2,1,0:T(8,128)S(1)}, u32[]{:S(2)}, u32[]{:S(2)}) async-start(f32[8,88,256]{2,1,0:T(8,128)} %shard_map.68), calls=%async_computation | async-start | bytes 1441792 | tf_op jit(solution)/shard_map/all_to_all | solution.py:437
  125.0 19.1 %all-to-all-start.4 = ((f32[8,64,256]{2,1,0:T(8,128)}), f32[8,64,256]{2,1,0:T(8,128)S(1)}, u32[]{:S(2)}, u32[]{:S(2)}) async-start(f32[8,64,256]{2,1,0:T(8,128)} %get-tuple-element.10), calls=%async_computation.4 | async-start | bytes 1048576 | tf_op jit(solution)/shard_map/all_to_all | solution.py:472
  128.5 4.8 %collective-permute-start = (f32[16,128]{1,0:T(8,128)S(1)}, f32[16,128]{1,0:T(8,128)S(1)}, u32[]{:S(2)}, u32[]{:S(2)}) collective-permute-start(f32[16,128]{1,0:T(8,128)S(1)} %shard_map.72), channel_id=1, source_target_pairs={{0,1},{1,0},{2,3},{3,2},{4,5},{5,4},{6,7},{7,6},{8,9},{9,8},{10,11... | collective-permute-start | bytes 24584 | tf_op jit(solution)/shard_map/ppermute | solution.py:481

commit v6 on v5

--- a/solution.py
+++ b/solution.py
@@ -27,7 +27,7 @@
 ROW_SEND = ROW_NORMAL + 3 * FACES
 ROWS = ROW_SEND + GROUPS
 
-PARAMS = pltpu.CompilerParams(vmem_limit_bytes=48 * 1024 * 1024)
+PARAMS = pltpu.CompilerParams(vmem_limit_bytes=52 * 1024 * 1024)
 
 
 def level(i):
@@ -84,7 +84,7 @@
         copy.wait()
 
 
-def find_neighbours(block_ref, near_ref):
+def find_neighbours(block_ref, kept_ref):
     base = CELLS * lax.broadcasted_iota(jnp.int32, (GROUPS, LANES), 0)
     for face in range(FACES):
         for half in range(2):
@@ -101,9 +101,9 @@
                     rows = block_ref[s, ROW_SEND : ROW_SEND + GROUPS, part * LANES : (part + 1) * LANES]
                     listed = jnp.where(table == s * 2 + part, take_lanes(rows, lane), listed)
             far = (place >> 8) * CELLS + listed.astype(jnp.int32)
-            near = jnp.where(adj < CELLS, adj + base, far)
+            near = jnp.where(adj < CELLS, adj + base, far).astype(jnp.float32)
             for g in range(GROUPS):
-                near_ref[g, face : face + 1, at] = near[g : g + 1, :]
+                kept_ref[g, ROW_NEAR + face : ROW_NEAR + face + 1, at] = near[g : g + 1, :]
 
 
 def split_terms(value_ref, terms_ref, g):
@@ -113,24 +113,37 @@
     terms_ref[g, NODES:, :] = (value - high.astype(jnp.float32)).astype(jnp.bfloat16)
 
 
-def transport(value_ref, terms_ref, normal_ref, near, node_ref, g):
-    own = value_ref[g, :NODES, :]
+def choice(row):
+    place = lax.broadcasted_iota(jnp.int32, (CELLS, CELLS), 0)
+    return jnp.where(place == (row & (CELLS - 1)), 1.0, 0.0).astype(jnp.bfloat16)
+
+
+def look_up(terms_ref, row):
+    chosen = choice(row)
+    group = row >> 8
+    found = None
+    for s in range(GROUPS):
+        both = jnp.dot(terms_ref[s], chosen, preferred_element_type=jnp.float32)
+        got = both[:NODES] + both[NODES:]
+        found = got if s == 0 else jnp.where(group == s, got, found)
+    return found
+
+
+def face_speeds(block_ref, node_ref, g, face):
+    normal = [block_ref[g, ROW_NORMAL + FACES * d + face : ROW_NORMAL + FACES * d + face + 1, :] for d in range(3)]
+    return normal[0], [normal[1] * node_ref[0, y] + normal[2] * node_ref[0, 2] for y in range(2)]
+
+
+def transport(block_ref, terms_ref, near, node_ref, g, kept_ref):
+    own = block_ref[g, :NODES, :]
     x = node_x(NODES, CELLS)
     second = lax.broadcasted_iota(jnp.int32, (NODES, CELLS), 0) >= VXY
-    place = lax.broadcasted_iota(jnp.int32, (CELLS, CELLS), 0)
     total = jnp.zeros((NODES, CELLS), jnp.float32)
     for face in range(FACES):
-        row = near[face : face + 1, :]
-        chosen = jnp.where(place == (row & (CELLS - 1)), 1.0, 0.0).astype(jnp.bfloat16)
-        group = row >> 8
-        found = None
-        for s in range(GROUPS):
-            both = jnp.dot(terms_ref[s], chosen, preferred_element_type=jnp.float32)
-            got = both[:NODES] + both[NODES:]
-            found = got if s == 0 else jnp.where(group == s, got, found)
-        normal = [normal_ref[g, ROW_NORMAL + FACES * d + face : ROW_NORMAL + FACES * d + face + 1, :] for d in range(3)]
-        fixed = [normal[1] * node_ref[0, y] + normal[2] * node_ref[0, 2] for y in range(2)]
-        speed = normal[0] * x + jnp.where(second, fixed[1], fixed[0])
+        found = look_up(terms_ref, near[face : face + 1, :])
+        kept_ref[g, face * NODES : (face + 1) * NODES, :] = found
+        slope, fixed = face_speeds(block_ref, node_ref, g, face)
+        speed = slope * x + jnp.where(second, fixed[1], fixed[0])
         total = total + speed * jnp.where(speed > 0.0, own, found)
     return total
 
@@ -156,14 +169,28 @@
     return rows
 
 
-def first_kernel(node_ref, block_ref, near_ref, flux_ref, sums_ref, terms_ref):
-    find_neighbours(block_ref, near_ref)
+ROW_FLUX = FACES * NODES
+ROW_NEAR = ROW_FLUX + NODES
+KEPT = ROW_NEAR + 8
+
+
+def near_rows(kept_ref, g):
+    return kept_ref[g, ROW_NEAR : ROW_NEAR + FACES, :].astype(jnp.int32)
+
+
+def first_kernel(node_ref, block_ref, kept_hbm, sums_ref, kept_ref, terms_ref, kept_sem):
+    find_neighbours(block_ref, kept_ref)
+
+    def out_copy(g):
+        return pltpu.make_async_copy(kept_ref.at[g], kept_hbm.at[g], kept_sem.at[g])
+
     for g in range(GROUPS):
         split_terms(block_ref, terms_ref, g)
 
     def group(g, carry):
-        flux = transport(block_ref, terms_ref, block_ref, near_ref[g], node_ref, g)
-        flux_ref[g] = flux
+        flux = transport(block_ref, terms_ref, near_rows(kept_ref, g), node_ref, g, kept_ref)
+        kept_ref[g, ROW_FLUX:ROW_NEAR, :] = flux
+        out_copy(g).start()
         rows = plane_sums(block_ref[g, :NODES, :], node_ref, False) + plane_sums(flux, node_ref, False)
         for i, row in enumerate(rows):
             for half in range(2):
@@ -174,6 +201,34 @@
         return carry
 
     lax.fori_loop(0, GROUPS, group, 0)
+    for g in range(GROUPS):
+        out_copy(g).wait()
+
+
+def between_kernel(kept_hbm, moved_hbm, flux_ref, moved_ref, terms_ref, flux_sem, moved_sem):
+    def flux_in(g):
+        rows = pl.ds(ROW_FLUX, KEPT - ROW_FLUX)
+        return pltpu.make_async_copy(kept_hbm.at[g, rows, :], flux_ref.at[g], flux_sem.at[g])
+
+    def out_copy(g):
+        return pltpu.make_async_copy(moved_ref.at[g], moved_hbm.at[g], moved_sem.at[g])
+
+    for g in range(GROUPS):
+        flux_in(g).start()
+    for g in range(GROUPS):
+        flux_in(g).wait()
+        split_terms(flux_ref, terms_ref, g)
+
+    def group(g, carry):
+        near = flux_ref[g, NODES : NODES + FACES, :].astype(jnp.int32)
+        for face in range(FACES):
+            moved_ref[g, face] = look_up(terms_ref, near[face : face + 1, :])
+        out_copy(g).start()
+        return carry
+
+    lax.fori_loop(0, GROUPS, group, 0)
+    for g in range(GROUPS):
+        out_copy(g).wait()
 
 
 def macroscopic(m):
@@ -332,45 +387,101 @@
     put_rows(out_ref, 12, mean, inverse, 1.0 - time_step * collide, beta)
 
 
-def relaxed_tile(value, flux, params_ref, base, tile, node_ref):
-    rows = [params_ref[tile, base + i : base + i + 1, :] for i in range(12)]
+def node_rows(params_ref, base, g, node_ref):
+    rows = [
+        jnp.concatenate([params_ref[g * 2 + half, base + i : base + i + 1, :] for half in range(2)], axis=1)
+        for i in range(12)
+    ]
     ixx, iyy, izz, ixy, ixz, iyz, lx, ly, lz, offset, alpha, beta = rows
     vz = node_ref[0, 2]
-    x = node_x(VXY, LANES)
-    parts = []
+    out = [-0.5 * ixx]
     for y in range(2):
         vy = node_ref[0, y]
-        slope = ixy * vy + ixz * vz + lx
-        rest = (iyy * vy + iyz * vz + ly) * vy + (izz * vz + lz) * vz + offset
-        energy = jnp.exp(-0.5 * ((ixx * x + slope) * x + rest))
-        at = slice(y * VXY, (y + 1) * VXY)
-        parts.append(alpha * value[at, :] + beta * energy - time_step * flux[at, :])
-    return jnp.concatenate(parts, axis=0)
-
-
-def second_kernel(node_ref, block_ref, near_ref, flux_ref, params_ref, out_ref, sums_ref, value_ref, terms_ref):
+        out.append(-0.5 * (ixy * vy + ixz * vz + lx))
+        out.append(-0.5 * ((iyy * vy + iyz * vz + ly) * vy + (izz * vz + lz) * vz + offset))
+    return out + [alpha, beta]
+
+
+def relaxed(value, flux, rows, x, y):
+    energy = jnp.exp((rows[0] * x + rows[1 + 2 * y]) * x + rows[2 + 2 * y])
+    return rows[5] * value + rows[6] * energy - time_step * flux
+
+
+def second_kernel(
+    node_ref, block_ref, kept_hbm, moved_hbm, params_ref, out_hbm, sums_ref,
+    value_ref, terms_ref, kept_ref, moved_ref, out_ref, kept_sem, moved_sem, out_sem,
+):
+    x = node_x(VXY, CELLS)
+
+    def kept_in(g):
+        return pltpu.make_async_copy(kept_hbm.at[g], kept_ref.at[g], kept_sem.at[g])
+
+    def moved_in(g):
+        return pltpu.make_async_copy(moved_hbm.at[g], moved_ref.at[g], moved_sem.at[g])
+
+    def out_copy(g):
+        return pltpu.make_async_copy(out_ref.at[g], out_hbm.at[g], out_sem.at[g])
+
+    for g in range(GROUPS):
+        kept_in(g).start()
+    for g in range(GROUPS):
+        moved_in(g).start()
+
     def first_step(g, carry):
-        for half in range(2):
-            at = slice(half * LANES, (half + 1) * LANES)
-            value_ref[g, :, at] = relaxed_tile(
-                block_ref[g, :NODES, at], flux_ref[g, :, at], params_ref, 0, g * 2 + half, node_ref
-            )
-        split_terms(value_ref, terms_ref, g)
+        kept_in(g).wait()
+        rows = node_rows(params_ref, 0, g, node_ref)
+        for y in range(2):
+            at = slice(y * VXY, (y + 1) * VXY)
+            flux = kept_ref[g, ROW_FLUX + y * VXY : ROW_FLUX + (y + 1) * VXY, :]
+            value_ref[g, at, :] = relaxed(block_ref[g, at, :], flux, rows, x, y)
+        rest = jnp.concatenate(rows + [jnp.zeros((1, CELLS), jnp.float32)], axis=0)
+        parts = []
+        for _ in range(3):
+            part = rest.astype(jnp.bfloat16).astype(jnp.float32)
+            parts.append(part)
+            rest = rest - part
+        parts.append(jnp.zeros((8, CELLS), jnp.float32))
+        terms_ref[g] = jnp.concatenate(parts, axis=0).astype(jnp.bfloat16)
         return carry
 
     lax.fori_loop(0, GROUPS, first_step, 0)
 
     def second_step(g, carry):
-        flux = transport(value_ref, terms_ref, block_ref, near_ref[g], node_ref, g)
-        for half in range(2):
-            at = slice(half * LANES, (half + 1) * LANES)
-            value = relaxed_tile(value_ref[g, :, at], flux[:, at], params_ref, 12, g * 2 + half, node_ref)
-            out_ref[g, :, at] = value
-            for i, row in enumerate(plane_sums(value, node_ref, True)):
-                sums_ref[g * 2 + half, i : i + 1, :] = row
+        moved_in(g).wait()
+        near = near_rows(kept_ref, g)
+        total = [jnp.zeros((VXY, CELLS), jnp.float32)] * 2
+        for face in range(FACES):
+            row = near[face : face + 1, :]
+            group = row >> 8
+            terms = terms_ref[...].reshape(GROUPS * 32, CELLS)
+            picked = jnp.dot(terms, choice(row), preferred_element_type=jnp.float32)
+            there = None
+            for s in range(GROUPS):
+                got = picked[s * 32 : s * 32 + 8] + picked[s * 32 + 8 : s * 32 + 16] + picked[s * 32 + 16 : s * 32 + 24]
+                there = got if s == 0 else jnp.where(group == s, got, there)
+            rows = [there[i : i + 1, :] for i in range(7)]
+            slope, fixed = face_speeds(block_ref, node_ref, g, face)
+            for y in range(2):
+                at = slice(y * VXY, (y + 1) * VXY)
+                found = kept_ref[g, face * NODES + y * VXY : face * NODES + (y + 1) * VXY, :]
+                far = relaxed(found, moved_ref[g, face, at, :], rows, x, y)
+                speed = slope * x + fixed[y]
+                total[y] = total[y] + speed * jnp.where(speed > 0.0, value_ref[g, at, :], far)
+        rows = node_rows(params_ref, 12, g, node_ref)
+        values = []
+        for y in range(2):
+            at = slice(y * VXY, (y + 1) * VXY)
+            values.append(relaxed(value_ref[g, at, :], total[y], rows, x, y))
+            out_ref[g, at, :] = values[y]
+        out_copy(g).start()
+        for i, row in enumerate(plane_sums(jnp.concatenate(values, axis=0), node_ref, True)):
+            for half in range(2):
+                sums_ref[g * 2 + half, i : i + 1, :] = row[:, half * LANES : (half + 1) * LANES]
         return carry
 
     lax.fori_loop(0, GROUPS, second_step, 0)
+    for g in range(GROUPS):
+        out_copy(g).wait()
 
 
 def final_kernel(parts_ref, out_ref):
@@ -402,7 +513,12 @@
 
 VMEM = pl.BlockSpec(memory_space=pltpu.VMEM)
 ANY = pl.BlockSpec(memory_space=pl.ANY)
+HBM = pl.BlockSpec(memory_space=pltpu.HBM)
 SMEM = pl.BlockSpec(memory_space=pltpu.SMEM)
+MOVED = pltpu.VMEM((GROUPS, FACES, NODES, CELLS), jnp.float32)
+KEEP = pltpu.VMEM((GROUPS, KEPT, CELLS), jnp.float32)
+VALUES = pltpu.VMEM((GROUPS, NODES, CELLS), jnp.float32)
+EACH = pltpu.SemaphoreType.DMA((GROUPS,))
 TERMS = pltpu.VMEM((GROUPS, 2 * NODES, CELLS), jnp.bfloat16)
 TABLES = [pltpu.VMEM((VXY, VXY, LANES), jnp.float32)] * 3
 
@@ -436,18 +552,28 @@
     )(distribution, adjacency, jnp.transpose(normals, (1, 0, 2)), send_list, block_counts.reshape(1, GROUPS))
     block = lax.all_to_all(block, "z", 0, 0, tiled=True)
 
-    near, flux, sums = pl.pallas_call(
+    kept, sums = pl.pallas_call(
         first_kernel,
         out_shape=(
-            shape(GROUPS, FACES, CELLS, dtype=jnp.int32),
-            shape(GROUPS, NODES, CELLS),
+            shape(GROUPS, KEPT, CELLS),
             shape(TILES, 4, 3 * LANES),
         ),
         in_specs=[SMEM, VMEM],
-        out_specs=(VMEM, VMEM, VMEM),
-        scratch_shapes=[TERMS],
+        out_specs=(HBM, VMEM),
+        scratch_shapes=[KEEP, TERMS, EACH],
         compiler_params=PARAMS,
     )(node, block)
+    moved = pl.pallas_call(
+        between_kernel,
+        out_shape=shape(GROUPS, FACES, NODES, CELLS),
+        in_specs=[HBM],
+        out_specs=HBM,
+        scratch_shapes=[
+            pltpu.VMEM((GROUPS, KEPT - ROW_FLUX, CELLS), jnp.float32), MOVED, TERMS, EACH, EACH,
+        ],
+        compiler_params=PARAMS,
+        cost_estimate=pl.CostEstimate(flops=4300000000, bytes_accessed=3000000, transcendentals=0),
+    )(kept)
 
     mine = jnp.sum(lax.all_to_all(sums, ("z", "c"), 0, 0, tiled=True), axis=0)
     params = pl.pallas_call(
@@ -463,13 +589,15 @@
     value, sums = pl.pallas_call(
         second_kernel,
         out_shape=(shape(GROUPS, NODES, CELLS), shape(TILES, 8, LANES)),
-        in_specs=[SMEM, VMEM, VMEM, VMEM, VMEM],
-        out_specs=(VMEM, VMEM),
-        scratch_shapes=[pltpu.VMEM((GROUPS, NODES, CELLS), jnp.float32), TERMS],
+        in_specs=[SMEM, VMEM, HBM, HBM, VMEM],
+        out_specs=(HBM, VMEM),
+        scratch_shapes=[
+            VALUES, pltpu.VMEM((GROUPS, 32, CELLS), jnp.bfloat16), KEEP, MOVED, VALUES, EACH, EACH, EACH,
+        ],
         compiler_params=PARAMS,
-    )(node, block, near, flux, params)
-
-    relaxed = lax.all_to_all(value, "z", 0, 0, tiled=True).reshape(GROUPS * NODES, CELLS)
+    )(node, block, kept, moved, params)
+
+    result = lax.all_to_all(value, "z", 0, 0, tiled=True).reshape(GROUPS * NODES, CELLS)
     mine = jnp.sum(lax.all_to_all(sums, ("z", "c"), 0, 0, tiled=True), axis=0)
     fields = pl.pallas_call(
         final_kernel,
@@ -482,7 +610,7 @@
     fields = jnp.where(
         c == 0, jnp.concatenate([fields, other], axis=1), jnp.concatenate([other, fields], axis=1)
     )
-    return relaxed, fields[:13]
+    return result, fields[:13]
 
 
 def solution(mesh):

time: 147 us -> 151 us (1.027)
  blocking collectives: 69.2 us -> 55.9 us
  Pallas kernels: 22 us -> 30.7 us
  starting transfers between devices: 18.4 us -> 24.1 us
  waiting for transfers between devices: 33 us -> 35.5 us
    all_to_all x3 -> x2, blocking collectives: 47.4 us -> 32.1 us  [spread(): return lax.all_to_all(copies, axes, 0, 0, tiled=True)]
    pallas_call x1 -> x2, Pallas kernels: 6.95 us -> 15.7 us  [the longest x1 7.88 us: per_device(): pl.pallas_call(between_kernel, out_shape=shape(GROUPS, FACES, NODES, CELL...]
    all_to_all x0 -> x1, starting transfers between devices: none -> 5.67 us  [spread(): return lax.all_to_all(copies, axes, 0, 0, tiled=True)]
    all_to_all x0 -> x1, waiting for transfers between devices: none -> 2.49 us  [spread(): return lax.all_to_all(copies, axes, 0, 0, tiled=True)]
    all_to_all x2, blocking collectives: 21.9 us -> 23.8 us  [per_device(): mine = jnp.sum(lax.all_to_all(sums, ('z', 'c'), 0, 0, tiled=True), axis=0)]
  transfers between devices with their start and end apart: 3 -> 4, of which waited for: 3 -> 4; matrix products, arithmetic and copies ran while one was open for 0% -> 0% of each run, Pallas kernels for 0% -> 5%
where the time goes in v6:
time: 151 us; the launch traced here: 149 us
  blocking collectives  55.9 us (37%)
  waiting for transfers between devices  35.5 us (24%)
  Pallas kernels  30.7 us (20%)
  starting transfers between devices  24.1 us (16%)
  local copies, waits for them, and re-layouts  1.53 us (1%)
    all_to_all x2, blocking collectives, spread(): return lax.all_to_all(copies, axes, 0, 0, tiled=True)  32.1 us
    all_to_all x2, blocking collectives, per_device(): mine = jnp.sum(lax.all_to_all(sums, ('z', 'c'), 0, 0, tiled=True), axis=0)  23.8 us
    all_to_all x1, waiting for transfers between devices, per_device(): block = lax.all_to_all(block, 'z', 0, 0, tiled=True)  22.1 us
    all_to_all x1, starting transfers between devices, per_device(): block = lax.all_to_all(block, 'z', 0, 0, tiled=True)  10.9 us
    all_to_all x1, waiting for transfers between devices, per_device(): lax.all_to_all(value, 'z', 0, 0, tiled=True).reshape(GROUPS * NODES, CELLS)  10.1 us
    pallas_call x1, Pallas kernels, per_device(): pl.pallas_call(second_kernel, out_shape=(shape(GROUPS, NODES, CELLS), sha...  7.98 us
    pallas_call x1, Pallas kernels, per_device(): pl.pallas_call(between_kernel, out_shape=shape(GROUPS, FACES, NODES, CELL...  7.88 us
    pallas_call x1, Pallas kernels, per_device(): pl.pallas_call(first_kernel, out_shape=(shape(GROUPS, KEPT, CELLS), shape...  7.83 us
  transfers between devices with their start and end apart: 4, of which 4 were waited for; matrix products, arithmetic and copies ran while one was open for 0% of the time, Pallas kernels for 5%

profile of v6, /device:TPU:1, one launch (start us, length us, event | category | flops | bytes accessed | tf_op | source)
XLA Modules:
  0.0 149.1 jit_solution(3702845438032717555)
XLA Ops:
  0.6 2.1 %shard_map.68 = f32[8,88,256]{2,1,0:T(8,128)} custom-call(f32[512,256]{1,0:T(8,128)} %value_hbm.1, s32[4,256]{1,0:T(4,128)} %adjacency_hbm.1, f32[3,4,256]{2,1,0:T(4,128)} %bitcast.7, s32[1,8,256]{2,1,0:T(8,128)} %send_hbm.1, s32[1,8]{1,0:T(1,128)} %bitcast.8), custom_call_target="tpu_custom_call" | custom-call | tf_op jit(solution)/shard_map/pallas_call | solution.py:538
  2.7 10.9 %all-to-all-start = ((f32[8,88,256]{2,1,0:T(8,128)}), f32[8,88,256]{2,1,0:T(8,128)S(1)}, u32[]{:S(2)}, u32[]{:S(2)}) async-start(f32[8,88,256]{2,1,0:T(8,128)} %shard_map.68), calls=%async_computation | async-start | bytes 1441792 | tf_op jit(solution)/shard_map/all_to_all | solution.py:553
  13.6 0.1 fusion.2.node_ref
  13.7 22.1 %all-to-all-done.block_ref = f32[8,88,256]{2,1,0:T(8,128)S(1)} async-done(((f32[8,88,256]{2,1,0:T(8,128)}), f32[8,88,256]{2,1,0:T(8,128)S(1)}, u32[]{:S(2)}, u32[]{:S(2)}) %all-to-all-start) | async-done | bytes 720928 | tf_op jit(solution)/shard_map/all_to_all | solution.py:553
  35.8 7.8 %shard_map.69 = (f32[8,328,256]{2,1,0:T(8,128)}, f32[16,4,384]{2,1,0:T(4,128)S(1)}) custom-call(f32[1,4]{1,0:T(1,128)S(1)} %fusion.2.node_ref, f32[8,88,256]{2,1,0:T(8,128)S(1)} %all-to-all-done.block_ref), custom_call_target="tpu_custom_call" | custom-call | tf_op jit(solution)/shard_map/pallas_call | solution.py:555
  43.6 11.4 %all_to_all.35 = f32[16,4,384]{2,1,0:T(4,128)S(1)} all-to-all(f32[16,4,384]{2,1,0:T(4,128)S(1)} %get-tuple-element.7), channel_id=1, replica_groups=mesh['z'=8,'x'=4,'y'=8,'c'=2] {'z','c'}, dimensions={0} | all-to-all | bytes 196608 | tf_op jit(solution)/shard_map/all_to_all | solution.py:578
  55.1 19.3 %all_to_all.36.parts_ref = f32[32,4,384]{2,1,0:T(4,128)S(1)} all-to-all(f32[32,4,384]{2,1,0:T(4,128)S(1)} %broadcast_in_dim.9), channel_id=1, replica_groups=mesh['z'=8,'x'=4,'y'=8,'c'=2] {'x','y'}, dimensions={0} | all-to-all | bytes 393216 | tf_op jit(solution)/shard_map/all_to_all | solution.py:528
  74.4 4.8 %shard_map.71 = f32[24,128]{1,0:T(8,128)S(1)} custom-call(f32[32,4,384]{2,1,0:T(4,128)S(1)} %all_to_all.36.parts_ref), custom_call_target="tpu_custom_call" | custom-call | tf_op jit(solution)/shard_map/pallas_call | solution.py:579
  79.2 0.7 broadcast_in_dim.10
  79.9 5.7 %all-to-all-start.3 = ((f32[16,24,128]{2,1,0:T(8,128)}), f32[16,24,128]{2,1,0:T(8,128)S(1)}, u32[]{:S(2)}, u32[]{:S(2)}) async-start(f32[16,24,128]{2,1,0:T(8,128)} %broadcast_in_dim.10), calls=%async_computation.3 | async-start | bytes 393216 | tf_op jit(solution)/shard_map/all_to_all | solution.py:528
  85.6 7.9 %shard_map.70.moved_hbm = f32[8,4,64,256]{3,2,1,0:T(8,128)} custom-call(f32[8,328,256]{2,1,0:T(8,128)} %get-tuple-element.6.kept_hbm), custom_call_target="tpu_custom_call" | custom-call | flops 4300000256 | bytes 3000000 | tf_op jit(solution)/shard_map/pallas_call | solution.py:566
  93.5 2.5 %all-to-all-done.3.params_ref = f32[16,24,128]{2,1,0:T(8,128)S(1)} async-done(((f32[16,24,128]{2,1,0:T(8,128)}), f32[16,24,128]{2,1,0:T(8,128)S(1)}, u32[]{:S(2)}, u32[]{:S(2)}) %all-to-all-start.3) | async-done | bytes 196640 | tf_op jit(solution)/shard_map/all_to_all | solution.py:528
  96.0 8.0 %shard_map.72 = (f32[8,64,256]{2,1,0:T(8,128)}, f32[16,8,128]{2,1,0:T(8,128)S(1)}) custom-call(f32[1,4]{1,0:T(1,128)S(1)} %fusion.2.node_ref, f32[8,88,256]{2,1,0:T(8,128)S(1)} %all-to-all-done.block_ref, f32[8,328,256]{2,1,0:T(8,128)} %get-tuple-element.6.kept_hbm, f32[8,4,64,256]{3,2,1,0:T(8,128)} %shard_map.70.moved_hbm, ...), custom_call_target="tpu_custom_call" | custom-call | tf_op jit(solution)/shard_map/pallas_call | solution.py:589
  104.0 12.4 %all_to_all.37 = f32[16,8,128]{2,1,0:T(8,128)S(1)} all-to-all(f32[16,8,128]{2,1,0:T(8,128)S(1)} %get-tuple-element.9), channel_id=1, replica_groups=mesh['z'=8,'x'=4,'y'=8,'c'=2] {'z','c'}, dimensions={0} | all-to-all | bytes 131072 | tf_op jit(solution)/shard_map/all_to_all | solution.py:601
  116.4 12.8 %all_to_all.38.parts_ref = f32[32,8,128]{2,1,0:T(8,128)S(1)} all-to-all(f32[32,8,128]{2,1,0:T(8,128)S(1)} %broadcast_in_dim.11), channel_id=1, replica_groups=mesh['z'=8,'x'=4,'y'=8,'c'=2] {'x','y'}, dimensions={0} | all-to-all | bytes 262144 | tf_op jit(solution)/shard_map/all_to_all | solution.py:528
  129.2 3.5 %all-to-all-start.4 = ((f32[8,64,256]{2,1,0:T(8,128)}), f32[8,64,256]{2,1,0:T(8,128)S(1)}, u32[]{:S(2)}, u32[]{:S(2)}) async-start(f32[8,64,256]{2,1,0:T(8,128)} %get-tuple-element.8), calls=%async_computation.4 | async-start | bytes 1048576 | tf_op jit(solution)/shard_map/all_to_all | solution.py:600
  132.7 0.1 shard_map.73
  132.8 4.0 %collective-permute-start = (f32[16,128]{1,0:T(8,128)S(1)}, f32[16,128]{1,0:T(8,128)S(1)}, u32[]{:S(2)}, u32[]{:S(2)}) collective-permute-start(f32[16,128]{1,0:T(8,128)S(1)} %shard_map.73), channel_id=1, source_target_pairs={{0,1},{1,0},{2,3},{3,2},{4,5},{5,4},{6,7},{7,6},{8,9},{9,8},{10,11... | collective-permute-start | bytes 24584 | tf_op jit(solution)/shard_map/ppermute | solution.py:609
  136.8 0.8 collective-permute-done
  137.6 0.6 fusion
  138.2 10.1 %all-to-all-done.4 = f32[8,64,256]{2,1,0:T(8,128)S(1)} async-done(((f32[8,64,256]{2,1,0:T(8,128)}), f32[8,64,256]{2,1,0:T(8,128)S(1)}, u32[]{:S(2)}, u32[]{:S(2)}) %all-to-all-start.4) | async-done | bytes 524320 | tf_op jit(solution)/shard_map/all_to_all | solution.py:600
  148.3 0.8 copy.8
  (4 shorter events, 0.1 us)
Async XLA Ops:
  2.7 33.0 %all-to-all-start = ((f32[8,88,256]{2,1,0:T(8,128)}), f32[8,88,256]{2,1,0:T(8,128)S(1)}, u32[]{:S(2)}, u32[]{:S(2)}) async-start(f32[8,88,256]{2,1,0:T(8,128)} %shard_map.68), calls=%async_computation | async-start | bytes 1441792 | tf_op jit(solution)/shard_map/all_to_all | solution.py:553
  79.9 16.1 %all-to-all-start.3 = ((f32[16,24,128]{2,1,0:T(8,128)}), f32[16,24,128]{2,1,0:T(8,128)S(1)}, u32[]{:S(2)}, u32[]{:S(2)}) async-start(f32[16,24,128]{2,1,0:T(8,128)} %broadcast_in_dim.10), calls=%async_computation.3 | async-start | bytes 393216 | tf_op jit(solution)/shard_map/all_to_all | solution.py:528
  129.2 19.1 %all-to-all-start.4 = ((f32[8,64,256]{2,1,0:T(8,128)}), f32[8,64,256]{2,1,0:T(8,128)S(1)}, u32[]{:S(2)}, u32[]{:S(2)}) async-start(f32[8,64,256]{2,1,0:T(8,128)} %get-tuple-element.8), calls=%async_computation.4 | async-start | bytes 1048576 | tf_op jit(solution)/shard_map/all_to_all | solution.py:600
  132.8 4.8 %collective-permute-start = (f32[16,128]{1,0:T(8,128)S(1)}, f32[16,128]{1,0:T(8,128)S(1)}, u32[]{:S(2)}, u32[]{:S(2)}) collective-permute-start(f32[16,128]{1,0:T(8,128)S(1)} %shard_map.73), channel_id=1, source_target_pairs={{0,1},{1,0},{2,3},{3,2},{4,5},{5,4},{6,7},{7,6},{8,9},{9,8},{10,11... | collective-permute-start | bytes 24584 | tf_op jit(solution)/shard_map/ppermute | solution.py:609

commit v7 on v5

--- a/solution.py
+++ b/solution.py
@@ -113,21 +113,44 @@
     terms_ref[g, NODES:, :] = (value - high.astype(jnp.float32)).astype(jnp.bfloat16)
 
 
+def look_up_lanes(value_ref, row):
+    blocks = NODES // 8
+    halves = []
+    for half in range(2):
+        near = jnp.broadcast_to(row[:, half * LANES : (half + 1) * LANES], (8, LANES))
+        lane = near & (LANES - 1)
+        tile = near >> 7
+        found = [None] * blocks
+        for t in range(TILES):
+            hit = tile == t
+            at = slice((t % 2) * LANES, (t % 2 + 1) * LANES)
+            for b in range(blocks):
+                got = take_lanes(value_ref[t // 2, b * 8 : b * 8 + 8, at], lane)
+                found[b] = got if t == 0 else jnp.where(hit, got, found[b])
+        halves.append(jnp.concatenate(found, axis=0))
+    return jnp.concatenate(halves, axis=1)
+
+
+def look_up(terms_ref, row):
+    place = lax.broadcasted_iota(jnp.int32, (CELLS, CELLS), 0)
+    chosen = jnp.where(place == (row & (CELLS - 1)), 1.0, 0.0).astype(jnp.bfloat16)
+    group = row >> 8
+    found = None
+    for s in range(GROUPS):
+        both = jnp.dot(terms_ref[s], chosen, preferred_element_type=jnp.float32)
+        got = both[:NODES] + both[NODES:]
+        found = got if s == 0 else jnp.where(group == s, got, found)
+    return found
+
+
 def transport(value_ref, terms_ref, normal_ref, near, node_ref, g):
     own = value_ref[g, :NODES, :]
     x = node_x(NODES, CELLS)
     second = lax.broadcasted_iota(jnp.int32, (NODES, CELLS), 0) >= VXY
-    place = lax.broadcasted_iota(jnp.int32, (CELLS, CELLS), 0)
     total = jnp.zeros((NODES, CELLS), jnp.float32)
     for face in range(FACES):
         row = near[face : face + 1, :]
-        chosen = jnp.where(place == (row & (CELLS - 1)), 1.0, 0.0).astype(jnp.bfloat16)
-        group = row >> 8
-        found = None
-        for s in range(GROUPS):
-            both = jnp.dot(terms_ref[s], chosen, preferred_element_type=jnp.float32)
-            got = both[:NODES] + both[NODES:]
-            found = got if s == 0 else jnp.where(group == s, got, found)
+        found = look_up(terms_ref, row) if face else look_up_lanes(value_ref, row)
         normal = [normal_ref[g, ROW_NORMAL + FACES * d + face : ROW_NORMAL + FACES * d + face + 1, :] for d in range(3)]
         fixed = [normal[1] * node_ref[0, y] + normal[2] * node_ref[0, 2] for y in range(2)]
         speed = normal[0] * x + jnp.where(second, fixed[1], fixed[0])
@@ -168,7 +191,7 @@
         for i, row in enumerate(rows):
             for half in range(2):
                 q = i // 4
-                sums_ref[g * 2 + half, i % 4 : i % 4 + 1, q * LANES : (q + 1) * LANES] = row[
+                sums_ref[half * GROUPS + g, i % 4 : i % 4 + 1, q * LANES : (q + 1) * LANES] = row[
                     :, half * LANES : (half + 1) * LANES
                 ]
         return carry
@@ -353,7 +376,7 @@
         for half in range(2):
             at = slice(half * LANES, (half + 1) * LANES)
             value_ref[g, :, at] = relaxed_tile(
-                block_ref[g, :NODES, at], flux_ref[g, :, at], params_ref, 0, g * 2 + half, node_ref
+                block_ref[g, :NODES, at], flux_ref[g, :, at], params_ref, 0, half * GROUPS + g, node_ref
             )
         split_terms(value_ref, terms_ref, g)
         return carry
@@ -364,10 +387,10 @@
         flux = transport(value_ref, terms_ref, block_ref, near_ref[g], node_ref, g)
         for half in range(2):
             at = slice(half * LANES, (half + 1) * LANES)
-            value = relaxed_tile(value_ref[g, :, at], flux[:, at], params_ref, 12, g * 2 + half, node_ref)
+            value = relaxed_tile(value_ref[g, :, at], flux[:, at], params_ref, 12, half * GROUPS + g, node_ref)
             out_ref[g, :, at] = value
             for i, row in enumerate(plane_sums(value, node_ref, True)):
-                sums_ref[g * 2 + half, i : i + 1, :] = row
+                sums_ref[half * GROUPS + g, i : i + 1, :] = row
         return carry
 
     lax.fori_loop(0, GROUPS, second_step, 0)
@@ -449,7 +472,7 @@
         compiler_params=PARAMS,
     )(node, block)
 
-    mine = jnp.sum(lax.all_to_all(sums, ("z", "c"), 0, 0, tiled=True), axis=0)
+    mine = jnp.sum(lax.all_to_all(sums, ("c", "z"), 0, 0, tiled=True), axis=0)
     params = pl.pallas_call(
         fields_kernel,
         out_shape=shape(24, LANES),
@@ -458,7 +481,7 @@
         scratch_shapes=TABLES,
         compiler_params=PARAMS,
     )(spread(mine, ("x", "y"), LEVELS))
-    params = spread(params, ("z", "c"), TILES)
+    params = spread(params, ("c", "z"), TILES)
 
     value, sums = pl.pallas_call(
         second_kernel,
@@ -470,7 +493,7 @@
     )(node, block, near, flux, params)
 
     relaxed = lax.all_to_all(value, "z", 0, 0, tiled=True).reshape(GROUPS * NODES, CELLS)
-    mine = jnp.sum(lax.all_to_all(sums, ("z", "c"), 0, 0, tiled=True), axis=0)
+    mine = jnp.sum(lax.all_to_all(sums, ("c", "z"), 0, 0, tiled=True), axis=0)
     fields = pl.pallas_call(
         final_kernel,
         out_shape=shape(16, LANES),

time: 147 us -> 143 us (0.973)
  Pallas kernels: 22 us -> 20.2 us
    all_to_all x3, blocking collectives: 47.4 us -> 45.8 us  [spread(): return lax.all_to_all(copies, axes, 0, 0, tiled=True)]
where the time goes in v7:
time: 143 us; the launch traced here: 141 us
  blocking collectives  67.9 us (47%)
  waiting for transfers between devices  32.3 us (23%)
  Pallas kernels  20.2 us (14%)
  starting transfers between devices  18.6 us (13%)
    all_to_all x3, blocking collectives, spread(): return lax.all_to_all(copies, axes, 0, 0, tiled=True)  45.8 us
    all_to_all x2, blocking collectives, per_device(): mine = jnp.sum(lax.all_to_all(sums, ('c', 'z'), 0, 0, tiled=True), axis=0)  22.1 us
    all_to_all x1, waiting for transfers between devices, per_device(): block = lax.all_to_all(block, 'z', 0, 0, tiled=True)  22.1 us
    all_to_all x1, starting transfers between devices, per_device(): block = lax.all_to_all(block, 'z', 0, 0, tiled=True)  10.9 us
    all_to_all x1, waiting for transfers between devices, per_device(): lax.all_to_all(value, 'z', 0, 0, tiled=True).reshape(GROUPS * NODES, CELLS)  9.38 us
    pallas_call x1, Pallas kernels, per_device(): pl.pallas_call(second_kernel, out_shape=(shape(GROUPS, NODES, CELLS), sha...  7.14 us
    pallas_call x1, Pallas kernels, per_device(): pl.pallas_call(first_kernel, out_shape=(shape(GROUPS, FACES, CELLS, dtype...  6.03 us
    pallas_call x1, Pallas kernels, per_device(): pl.pallas_call(fields_kernel, out_shape=shape(24, LANES), in_specs=[VMEM]...  4.84 us
  transfers between devices with their start and end apart: 3, of which 3 were waited for; matrix products, arithmetic and copies ran while one was open for 0% of the time, Pallas kernels for 0%

profile of v7, /device:TPU:1, one launch (start us, length us, event | category | flops | bytes accessed | tf_op | source)
XLA Modules:
  0.0 141.2 jit_solution(10362420693848172324)
XLA Ops:
  0.6 2.1 %shard_map.68 = f32[8,88,256]{2,1,0:T(8,128)} custom-call(f32[512,256]{1,0:T(8,128)} %value_hbm.1, s32[4,256]{1,0:T(4,128)} %adjacency_hbm.1, f32[3,4,256]{2,1,0:T(4,128)} %bitcast.7, s32[1,8,256]{2,1,0:T(8,128)} %send_hbm.1, s32[1,8]{1,0:T(1,128)} %bitcast.8), custom_call_target="tpu_custom_call" | custom-call | tf_op jit(solution)/shard_map/pallas_call | solution.py:445
  2.7 10.9 %all-to-all-start = ((f32[8,88,256]{2,1,0:T(8,128)}), f32[8,88,256]{2,1,0:T(8,128)S(1)}, u32[]{:S(2)}, u32[]{:S(2)}) async-start(f32[8,88,256]{2,1,0:T(8,128)} %shard_map.68), calls=%async_computation | async-start | bytes 1441792 | tf_op jit(solution)/shard_map/all_to_all | solution.py:460
  13.6 0.1 fusion.2.node_ref
  13.7 22.1 %all-to-all-done.block_ref = f32[8,88,256]{2,1,0:T(8,128)S(1)} async-done(((f32[8,88,256]{2,1,0:T(8,128)}), f32[8,88,256]{2,1,0:T(8,128)S(1)}, u32[]{:S(2)}, u32[]{:S(2)}) %all-to-all-start) | async-done | bytes 720928 | tf_op jit(solution)/shard_map/all_to_all | solution.py:460
  35.8 6.0 %shard_map.69 = (s32[8,4,256]{2,1,0:T(4,128)S(1)}, f32[8,64,256]{2,1,0:T(8,128)S(1)}, f32[16,4,384]{2,1,0:T(4,128)S(1)}) custom-call(f32[1,4]{1,0:T(1,128)S(1)} %fusion.2.node_ref, f32[8,88,256]{2,1,0:T(8,128)S(1)} %all-to-all-done.block_ref), custom_call_target="tpu_custom_call" | custom-call | tf_op jit(solution)/shard_map/pallas_call | solution.py:462
  41.8 10.2 %all_to_all.35 = f32[16,4,384]{2,1,0:T(4,128)S(1)} all-to-all(f32[16,4,384]{2,1,0:T(4,128)S(1)} %get-tuple-element.9), channel_id=1, replica_groups=mesh['z'=8,'x'=4,'y'=8,'c'=2] {'c','z'}, dimensions={0} | all-to-all | bytes 196608 | tf_op jit(solution)/shard_map/all_to_all | solution.py:475
  52.1 18.8 %all_to_all.36.parts_ref = f32[32,4,384]{2,1,0:T(4,128)S(1)} all-to-all(f32[32,4,384]{2,1,0:T(4,128)S(1)} %broadcast_in_dim.9), channel_id=1, replica_groups=mesh['z'=8,'x'=4,'y'=8,'c'=2] {'x','y'}, dimensions={0} | all-to-all | bytes 393216 | tf_op jit(solution)/shard_map/all_to_all | solution.py:435
  71.0 4.8 %shard_map.70 = f32[24,128]{1,0:T(8,128)S(1)} custom-call(f32[32,4,384]{2,1,0:T(4,128)S(1)} %all_to_all.36.parts_ref), custom_call_target="tpu_custom_call" | custom-call | tf_op jit(solution)/shard_map/pallas_call | solution.py:476
  75.8 14.1 %all_to_all.37.params_ref = f32[16,24,128]{2,1,0:T(8,128)S(1)} all-to-all(f32[16,24,128]{2,1,0:T(8,128)S(1)} %broadcast_in_dim.10), channel_id=1, replica_groups=mesh['z'=8,'x'=4,'y'=8,'c'=2] {'c','z'}, dimensions={0} | all-to-all | bytes 393216 | tf_op jit(solution)/shard_map/all_to_all | solution.py:435
  90.0 7.1 %shard_map.71 = (f32[8,64,256]{2,1,0:T(8,128)}, f32[16,8,128]{2,1,0:T(8,128)S(1)}) custom-call(f32[1,4]{1,0:T(1,128)S(1)} %fusion.2.node_ref, f32[8,88,256]{2,1,0:T(8,128)S(1)} %all-to-all-done.block_ref, s32[8,4,256]{2,1,0:T(4,128)S(1)} %get-tuple-element.7.near_ref, f32[8,64,256]{2,1,0:T(8,128)S(1)} %get-tuple-element.8.flux_ref, ...), custom_call_target="tpu_custom_call" | custom-call | tf_op jit(solution)/shard_map/pallas_call | solution.py:486
  97.1 11.9 %all_to_all.38 = f32[16,8,128]{2,1,0:T(8,128)S(1)} all-to-all(f32[16,8,128]{2,1,0:T(8,128)S(1)} %get-tuple-element.11), channel_id=1, replica_groups=mesh['z'=8,'x'=4,'y'=8,'c'=2] {'c','z'}, dimensions={0} | all-to-all | bytes 131072 | tf_op jit(solution)/shard_map/all_to_all | solution.py:496
  109.0 12.8 %all_to_all.39.parts_ref = f32[32,8,128]{2,1,0:T(8,128)S(1)} all-to-all(f32[32,8,128]{2,1,0:T(8,128)S(1)} %broadcast_in_dim.11), channel_id=1, replica_groups=mesh['z'=8,'x'=4,'y'=8,'c'=2] {'x','y'}, dimensions={0} | all-to-all | bytes 262144 | tf_op jit(solution)/shard_map/all_to_all | solution.py:435
  121.9 3.5 %all-to-all-start.4 = ((f32[8,64,256]{2,1,0:T(8,128)}), f32[8,64,256]{2,1,0:T(8,128)S(1)}, u32[]{:S(2)}, u32[]{:S(2)}) async-start(f32[8,64,256]{2,1,0:T(8,128)} %get-tuple-element.10), calls=%async_computation.4 | async-start | bytes 1048576 | tf_op jit(solution)/shard_map/all_to_all | solution.py:495
  125.4 0.1 shard_map.72
  125.4 4.2 %collective-permute-start = (f32[16,128]{1,0:T(8,128)S(1)}, f32[16,128]{1,0:T(8,128)S(1)}, u32[]{:S(2)}, u32[]{:S(2)}) collective-permute-start(f32[16,128]{1,0:T(8,128)S(1)} %shard_map.72), channel_id=1, source_target_pairs={{0,1},{1,0},{2,3},{3,2},{4,5},{5,4},{6,7},{7,6},{8,9},{9,8},{10,11... | collective-permute-start | bytes 24584 | tf_op jit(solution)/shard_map/ppermute | solution.py:504
  129.7 0.8 collective-permute-done
  130.5 0.6 fusion
  131.1 9.4 %all-to-all-done.4 = f32[8,64,256]{2,1,0:T(8,128)S(1)} async-done(((f32[8,64,256]{2,1,0:T(8,128)}), f32[8,64,256]{2,1,0:T(8,128)S(1)}, u32[]{:S(2)}, u32[]{:S(2)}) %all-to-all-start.4) | async-done | bytes 524320 | tf_op jit(solution)/shard_map/all_to_all | solution.py:495
  140.4 0.8 copy.8
  (5 shorter events, 0.1 us)
Async XLA Ops:
  2.7 33.0 %all-to-all-start = ((f32[8,88,256]{2,1,0:T(8,128)}), f32[8,88,256]{2,1,0:T(8,128)S(1)}, u32[]{:S(2)}, u32[]{:S(2)}) async-start(f32[8,88,256]{2,1,0:T(8,128)} %shard_map.68), calls=%async_computation | async-start | bytes 1441792 | tf_op jit(solution)/shard_map/all_to_all | solution.py:460
  121.9 18.6 %all-to-all-start.4 = ((f32[8,64,256]{2,1,0:T(8,128)}), f32[8,64,256]{2,1,0:T(8,128)S(1)}, u32[]{:S(2)}, u32[]{:S(2)}) async-start(f32[8,64,256]{2,1,0:T(8,128)} %get-tuple-element.10), calls=%async_computation.4 | async-start | bytes 1048576 | tf_op jit(solution)/shard_map/all_to_all | solution.py:495
  125.4 5.0 %collective-permute-start = (f32[16,128]{1,0:T(8,128)S(1)}, f32[16,128]{1,0:T(8,128)S(1)}, u32[]{:S(2)}, u32[]{:S(2)}) collective-permute-start(f32[16,128]{1,0:T(8,128)S(1)} %shard_map.72), channel_id=1, source_target_pairs={{0,1},{1,0},{2,3},{3,2},{4,5},{5,4},{6,7},{7,6},{8,9},{9,8},{10,11... | collective-permute-start | bytes 24584 | tf_op jit(solution)/shard_map/ppermute | solution.py:504

commit v8 on v7

--- a/solution.py
+++ b/solution.py
@@ -396,13 +396,30 @@
     lax.fori_loop(0, GROUPS, second_step, 0)
 
 
-def final_kernel(parts_ref, out_ref):
+def partial_kernel(node_ref, parts_ref, out_ref):
+    sums = [jnp.zeros((8, LANES), jnp.float32) for _ in range(4)]
+    for i in range(parts_ref.shape[0]):
+        part = parts_ref[i]
+        z = node_ref[0, 3] + i * spacing
+        for order in range(4):
+            sums[order] = sums[order] + part
+            part = z * part
+
     def of(a):
         return lambda i: a[i : i + 1, :] / TOTAL
 
-    row0, row1, row2, row3 = (of(a) for a in level_sums(parts_ref, 4))
-    density, (ux, uy, uz), b, theta, _ = macroscopic(ten(row0, row1, row2))
-    third = [row0(6) + row2(1), row0(7) + row2(2), row1(3) + row1(4) + row3(0)]
+    row0, row1, row2, row3 = (of(a) for a in sums)
+    rows = ten(row0, row1, row2)
+    rows += [row0(6) + row2(1), row0(7) + row2(2), row1(3) + row1(4) + row3(0)]
+    for i, row in enumerate(rows):
+        out_ref[i : i + 1, :] = row
+    out_ref[13:16, :] = jnp.zeros((3, LANES), jnp.float32)
+
+
+def final_kernel(moments_ref, out_ref):
+    rows = [moments_ref[i : i + 1, :] for i in range(13)]
+    density, (ux, uy, uz), b, theta, _ = macroscopic(rows[:10])
+    third = rows[10:]
     trace = b[0] + b[1] + b[2]
     square = ux * ux + uy * uy + uz * uz
     stress = (
@@ -439,7 +456,7 @@
     z, x, y, c = (lax.axis_index(a) for a in ("z", "x", "y", "c"))
     vel = (x * 8 + y) * 2 + c
     row = (vel * 16 + z * 2) & (VXY - 1)
-    node = jnp.stack([row, row + 1, vel // 2, vel // 2]).astype(jnp.float32)
+    node = jnp.stack([row, row + 1, vel // 2, x * 8]).astype(jnp.float32)
     node = ((node - (VXY - 1) / 2.0) * spacing).reshape(1, 4)
 
     block = pl.pallas_call(
@@ -494,13 +511,22 @@
 
     relaxed = lax.all_to_all(value, "z", 0, 0, tiled=True).reshape(GROUPS * NODES, CELLS)
     mine = jnp.sum(lax.all_to_all(sums, ("c", "z"), 0, 0, tiled=True), axis=0)
+    moments = pl.pallas_call(
+        partial_kernel,
+        out_shape=shape(16, LANES),
+        in_specs=[SMEM, VMEM],
+        out_specs=VMEM,
+        compiler_params=PARAMS,
+    )(node, spread(mine, "y", 8))
+    for step in (1, 2):
+        moments = moments + lax.ppermute(moments, "x", [(i, i ^ step) for i in range(4)])
     fields = pl.pallas_call(
         final_kernel,
         out_shape=shape(16, LANES),
         in_specs=[VMEM],
         out_specs=VMEM,
         compiler_params=PARAMS,
-    )(spread(mine, ("x", "y"), LEVELS))
+    )(moments)
     other = lax.ppermute(fields, "c", [(0, 1), (1, 0)])
     fields = jnp.where(
         c == 0, jnp.concatenate([fields, other], axis=1), jnp.concatenate([other, fields], axis=1)

time: 143 us -> 142 us (level)
  starting transfers between devices: 18.6 us -> 25.8 us
  waiting for transfers between devices: 32.3 us -> 28.2 us
  blocking collectives: 67.9 us -> 64.5 us
    all_to_all x1, waiting for transfers between devices: 9.38 us -> 0.01 us  [per_device(): lax.all_to_all(value, 'z', 0, 0, tiled=True).reshape(GROUPS * NODES, CELLS)]
    ppermute x0 -> x2, waiting for transfers between devices: none -> 5.33 us  [per_device(): lax.ppermute(moments, 'x', [(i, i ^ step) for i in range(4)])]
    ppermute x0 -> x2, starting transfers between devices: none -> 5.23 us  [per_device(): lax.ppermute(moments, 'x', [(i, i ^ step) for i in range(4)])]
    all_to_all x3, blocking collectives: 45.8 us -> 42.4 us  [spread(): return lax.all_to_all(copies, axes, 0, 0, tiled=True)]
    ppermute x1, starting transfers between devices: 4.22 us -> 6.24 us  [per_device(): other = lax.ppermute(fields, 'c', [(0, 1), (1, 0)])]
  transfers between devices with their start and end apart: 3 -> 5, of which waited for: 3 -> 4; matrix products, arithmetic and copies ran while one was open for 0% -> 0% of each run, Pallas kernels for 0% -> 0%
where the time goes in v8:
time: 142 us
  blocking collectives  64.5 us (45%)
  waiting for transfers between devices  28.2 us (20%)
  starting transfers between devices  25.8 us (18%)
  Pallas kernels  20.7 us (15%)
    all_to_all x3, blocking collectives, spread(): return lax.all_to_all(copies, axes, 0, 0, tiled=True)  42.4 us
    all_to_all x2, blocking collectives, per_device(): mine = jnp.sum(lax.all_to_all(sums, ('c', 'z'), 0, 0, tiled=True), axis=0)  22.1 us
    all_to_all x1, waiting for transfers between devices, per_device(): block = lax.all_to_all(block, 'z', 0, 0, tiled=True)  22.1 us
    all_to_all x1, starting transfers between devices, per_device(): block = lax.all_to_all(block, 'z', 0, 0, tiled=True)  10.9 us
    pallas_call x1, Pallas kernels, per_device(): pl.pallas_call(second_kernel, out_shape=(shape(GROUPS, NODES, CELLS), sha...  7.13 us
    ppermute x1, starting transfers between devices, per_device(): other = lax.ppermute(fields, 'c', [(0, 1), (1, 0)])  6.24 us
    pallas_call x1, Pallas kernels, per_device(): pl.pallas_call(first_kernel, out_shape=(shape(GROUPS, FACES, CELLS, dtype...  6.02 us
    ppermute x2, waiting for transfers between devices, per_device(): lax.ppermute(moments, 'x', [(i, i ^ step) for i in range(4)])  5.33 us
  transfers between devices with their start and end apart: 5, of which 4 were waited for; matrix products, arithmetic and copies ran while one was open for 0% of the time, Pallas kernels for 0%

profile of v8, /device:TPU:1, one launch (start us, length us, event | category | flops | bytes accessed | tf_op | source)
XLA Modules:
  0.0 141.6 jit_solution(16879698688614390289)
XLA Ops:
  0.6 2.1 %shard_map.68 = f32[8,88,256]{2,1,0:T(8,128)} custom-call(f32[512,256]{1,0:T(8,128)} %value_hbm.1, s32[4,256]{1,0:T(4,128)} %adjacency_hbm.1, f32[3,4,256]{2,1,0:T(4,128)} %bitcast.8, s32[1,8,256]{2,1,0:T(8,128)} %send_hbm.1, s32[1,8]{1,0:T(1,128)} %bitcast.9), custom_call_target="tpu_custom_call" | custom-call | tf_op jit(solution)/shard_map/pallas_call | solution.py:462
  2.7 10.9 %all-to-all-start = ((f32[8,88,256]{2,1,0:T(8,128)}), f32[8,88,256]{2,1,0:T(8,128)S(1)}, u32[]{:S(2)}, u32[]{:S(2)}) async-start(f32[8,88,256]{2,1,0:T(8,128)} %shard_map.68), calls=%async_computation | async-start | bytes 1441792 | tf_op jit(solution)/shard_map/all_to_all | solution.py:477
  13.6 0.1 fusion.2.node_ref
  13.7 22.1 %all-to-all-done.block_ref = f32[8,88,256]{2,1,0:T(8,128)S(1)} async-done(((f32[8,88,256]{2,1,0:T(8,128)}), f32[8,88,256]{2,1,0:T(8,128)S(1)}, u32[]{:S(2)}, u32[]{:S(2)}) %all-to-all-start) | async-done | bytes 720928 | tf_op jit(solution)/shard_map/all_to_all | solution.py:477
  35.8 6.0 %shard_map.69 = (s32[8,4,256]{2,1,0:T(4,128)S(1)}, f32[8,64,256]{2,1,0:T(8,128)S(1)}, f32[16,4,384]{2,1,0:T(4,128)S(1)}) custom-call(f32[1,4]{1,0:T(1,128)S(1)} %fusion.2.node_ref, f32[8,88,256]{2,1,0:T(8,128)S(1)} %all-to-all-done.block_ref), custom_call_target="tpu_custom_call" | custom-call | tf_op jit(solution)/shard_map/pallas_call | solution.py:479
  41.8 10.2 %all_to_all.35 = f32[16,4,384]{2,1,0:T(4,128)S(1)} all-to-all(f32[16,4,384]{2,1,0:T(4,128)S(1)} %get-tuple-element.9), channel_id=1, replica_groups=mesh['z'=8,'x'=4,'y'=8,'c'=2] {'c','z'}, dimensions={0} | all-to-all | bytes 196608 | tf_op jit(solution)/shard_map/all_to_all | solution.py:492
  52.1 18.9 %all_to_all.36.parts_ref = f32[32,4,384]{2,1,0:T(4,128)S(1)} all-to-all(f32[32,4,384]{2,1,0:T(4,128)S(1)} %broadcast_in_dim.9), channel_id=1, replica_groups=mesh['z'=8,'x'=4,'y'=8,'c'=2] {'x','y'}, dimensions={0} | all-to-all | bytes 393216 | tf_op jit(solution)/shard_map/all_to_all | solution.py:452
  71.0 4.8 %shard_map.70 = f32[24,128]{1,0:T(8,128)S(1)} custom-call(f32[32,4,384]{2,1,0:T(4,128)S(1)} %all_to_all.36.parts_ref), custom_call_target="tpu_custom_call" | custom-call | tf_op jit(solution)/shard_map/pallas_call | solution.py:493
  75.9 14.1 %all_to_all.37.params_ref = f32[16,24,128]{2,1,0:T(8,128)S(1)} all-to-all(f32[16,24,128]{2,1,0:T(8,128)S(1)} %broadcast_in_dim.10), channel_id=1, replica_groups=mesh['z'=8,'x'=4,'y'=8,'c'=2] {'c','z'}, dimensions={0} | all-to-all | bytes 393216 | tf_op jit(solution)/shard_map/all_to_all | solution.py:452
  90.0 7.1 %shard_map.71 = (f32[8,64,256]{2,1,0:T(8,128)}, f32[16,8,128]{2,1,0:T(8,128)S(1)}) custom-call(f32[1,4]{1,0:T(1,128)S(1)} %fusion.2.node_ref, f32[8,88,256]{2,1,0:T(8,128)S(1)} %all-to-all-done.block_ref, s32[8,4,256]{2,1,0:T(4,128)S(1)} %get-tuple-element.7.near_ref, f32[8,64,256]{2,1,0:T(8,128)S(1)} %get-tuple-element.8.flux_ref, ...), custom_call_target="tpu_custom_call" | custom-call | tf_op jit(solution)/shard_map/pallas_call | solution.py:503
  97.1 11.9 %all_to_all.38 = f32[16,8,128]{2,1,0:T(8,128)S(1)} all-to-all(f32[16,8,128]{2,1,0:T(8,128)S(1)} %get-tuple-element.11), channel_id=1, replica_groups=mesh['z'=8,'x'=4,'y'=8,'c'=2] {'c','z'}, dimensions={0} | all-to-all | bytes 131072 | tf_op jit(solution)/shard_map/all_to_all | solution.py:513
  109.0 9.4 %all_to_all.39.parts_ref = f32[8,8,128]{2,1,0:T(8,128)S(1)} all-to-all(f32[8,8,128]{2,1,0:T(8,128)S(1)} %broadcast_in_dim.11), channel_id=1, replica_groups=mesh['z'=8,'x'=4,'y'=8,'c'=2] {'y'}, dimensions={0} | all-to-all | bytes 65536 | tf_op jit(solution)/shard_map/all_to_all | solution.py:452
  118.4 3.5 %all-to-all-start.4 = ((f32[8,64,256]{2,1,0:T(8,128)}), f32[8,64,256]{2,1,0:T(8,128)S(1)}, u32[]{:S(2)}, u32[]{:S(2)}) async-start(f32[8,64,256]{2,1,0:T(8,128)} %get-tuple-element.10), calls=%async_computation.4 | async-start | bytes 1048576 | tf_op jit(solution)/shard_map/all_to_all | solution.py:512
  121.9 0.6 shard_map.72
  122.5 2.2 %collective-permute-start = (f32[16,128]{1,0:T(8,128)S(1)}, f32[16,128]{1,0:T(8,128)S(1)}, u32[]{:S(2)}, u32[]{:S(2)}) collective-permute-start(f32[16,128]{1,0:T(8,128)S(1)} %shard_map.72), channel_id=1, source_target_pairs={{0,16},{16,0},{32,48},{48,32},{1,17},{17,1},{33,49},{49,33},{2,18}... | collective-permute-start | bytes 24584 | tf_op jit(solution)/shard_map/ppermute | solution.py:522
  124.7 2.2 %collective-permute-done = f32[16,128]{1,0:T(8,128)S(1)} collective-permute-done((f32[16,128]{1,0:T(8,128)S(1)}, f32[16,128]{1,0:T(8,128)S(1)}, u32[]{:S(2)}, u32[]{:S(2)}) %collective-permute-start) | collective-permute-done | bytes 8224 | tf_op jit(solution)/shard_map/ppermute | solution.py:522
  126.9 3.0 %collective-permute-start.1 = (f32[16,128]{1,0:T(8,128)S(1)}, f32[16,128]{1,0:T(8,128)S(1)}, u32[]{:S(2)}, u32[]{:S(2)}) collective-permute-start(f32[16,128]{1,0:T(8,128)S(1)} %add.31), channel_id=1, source_target_pairs={{0,32},{16,48},{32,0},{48,16},{1,33},{17,49},{33,1},{49,17},{2,34}... | collective-permute-start | bytes 24584 | tf_op jit(solution)/shard_map/ppermute | solution.py:522
  130.0 3.1 %collective-permute-done.1 = f32[16,128]{1,0:T(8,128)S(1)} collective-permute-done((f32[16,128]{1,0:T(8,128)S(1)}, f32[16,128]{1,0:T(8,128)S(1)}, u32[]{:S(2)}, u32[]{:S(2)}) %collective-permute-start.1) | collective-permute-done | bytes 8224 | tf_op jit(solution)/shard_map/ppermute | solution.py:522
  133.1 6.2 %collective-permute-start.2 = (f32[16,128]{1,0:T(8,128)S(1)}, f32[16,128]{1,0:T(8,128)S(1)}, u32[]{:S(2)}, u32[]{:S(2)}) collective-permute-start(f32[16,128]{1,0:T(8,128)S(1)} %shard_map.73), channel_id=1, source_target_pairs={{0,1},{1,0},{2,3},{3,2},{4,5},{5,4},{6,7},{7,6},{8,9},{9,8},{10,11... | collective-permute-start | bytes 24584 | tf_op jit(solution)/shard_map/ppermute | solution.py:530
  139.4 0.8 collective-permute-done.2
  140.2 0.6 fusion
  140.8 0.0 all-to-all-done.4
  140.8 0.8 copy.8
  (8 shorter events, 0.1 us)
Async XLA Ops:
  2.7 33.0 %all-to-all-start = ((f32[8,88,256]{2,1,0:T(8,128)}), f32[8,88,256]{2,1,0:T(8,128)S(1)}, u32[]{:S(2)}, u32[]{:S(2)}) async-start(f32[8,88,256]{2,1,0:T(8,128)} %shard_map.68), calls=%async_computation | async-start | bytes 1441792 | tf_op jit(solution)/shard_map/all_to_all | solution.py:477
  118.4 22.4 %all-to-all-start.4 = ((f32[8,64,256]{2,1,0:T(8,128)}), f32[8,64,256]{2,1,0:T(8,128)S(1)}, u32[]{:S(2)}, u32[]{:S(2)}) async-start(f32[8,64,256]{2,1,0:T(8,128)} %get-tuple-element.10), calls=%async_computation.4 | async-start | bytes 1048576 | tf_op jit(solution)/shard_map/all_to_all | solution.py:512
  122.5 4.4 %collective-permute-start = (f32[16,128]{1,0:T(8,128)S(1)}, f32[16,128]{1,0:T(8,128)S(1)}, u32[]{:S(2)}, u32[]{:S(2)}) collective-permute-start(f32[16,128]{1,0:T(8,128)S(1)} %shard_map.72), channel_id=1, source_target_pairs={{0,16},{16,0},{32,48},{48,32},{1,17},{17,1},{33,49},{49,33},{2,18}... | collective-permute-start | bytes 24584 | tf_op jit(solution)/shard_map/ppermute | solution.py:522
  126.9 6.2 %collective-permute-start.1 = (f32[16,128]{1,0:T(8,128)S(1)}, f32[16,128]{1,0:T(8,128)S(1)}, u32[]{:S(2)}, u32[]{:S(2)}) collective-permute-start(f32[16,128]{1,0:T(8,128)S(1)} %add.31), channel_id=1, source_target_pairs={{0,32},{16,48},{32,0},{48,16},{1,33},{17,49},{33,1},{49,17},{2,34}... | collective-permute-start | bytes 24584 | tf_op jit(solution)/shard_map/ppermute | solution.py:522
  133.1 7.1 %collective-permute-start.2 = (f32[16,128]{1,0:T(8,128)S(1)}, f32[16,128]{1,0:T(8,128)S(1)}, u32[]{:S(2)}, u32[]{:S(2)}) collective-permute-start(f32[16,128]{1,0:T(8,128)S(1)} %shard_map.73), channel_id=1, source_target_pairs={{0,1},{1,0},{2,3},{3,2},{4,5},{5,4},{6,7},{7,6},{8,9},{9,8},{10,11... | collective-permute-start | bytes 24584 | tf_op jit(solution)/shard_map/ppermute | solution.py:530

commit v9 on v8

--- a/solution.py
+++ b/solution.py
@@ -400,7 +400,7 @@
     sums = [jnp.zeros((8, LANES), jnp.float32) for _ in range(4)]
     for i in range(parts_ref.shape[0]):
         part = parts_ref[i]
-        z = node_ref[0, 3] + i * spacing
+        z = node_ref[0, 3] + (i // 8 * 16 + i % 8) * spacing
         for order in range(4):
             sums[order] = sums[order] + part
             part = z * part
@@ -453,10 +453,10 @@
 
 
 def per_device(distribution, normals, adjacency, send_list, block_counts):
-    z, x, y, c = (lax.axis_index(a) for a in ("z", "x", "y", "c"))
-    vel = (x * 8 + y) * 2 + c
+    z, x, w, y, c = (lax.axis_index(a) for a in ("z", "x", "w", "y", "c"))
+    vel = ((x * 2 + w) * 8 + y) * 2 + c
     row = (vel * 16 + z * 2) & (VXY - 1)
-    node = jnp.stack([row, row + 1, vel // 2, x * 8]).astype(jnp.float32)
+    node = jnp.stack([row, row + 1, vel // 2, w * 8]).astype(jnp.float32)
     node = ((node - (VXY - 1) / 2.0) * spacing).reshape(1, 4)
 
     block = pl.pallas_call(
@@ -497,7 +497,7 @@
         out_specs=VMEM,
         scratch_shapes=TABLES,
         compiler_params=PARAMS,
-    )(spread(mine, ("x", "y"), LEVELS))
+    )(spread(mine, ("x", "w", "y"), LEVELS))
     params = spread(params, ("c", "z"), TILES)
 
     value, sums = pl.pallas_call(
@@ -517,9 +517,8 @@
         in_specs=[SMEM, VMEM],
         out_specs=VMEM,
         compiler_params=PARAMS,
-    )(node, spread(mine, "y", 8))
-    for step in (1, 2):
-        moments = moments + lax.ppermute(moments, "x", [(i, i ^ step) for i in range(4)])
+    )(node, spread(mine, ("x", "y"), 16))
+    moments = moments + lax.ppermute(moments, "w", [(0, 1), (1, 0)])
     fields = pl.pallas_call(
         final_kernel,
         out_shape=shape(16, LANES),
@@ -535,8 +534,8 @@
 
 
 def solution(mesh):
-    split = Mesh(mesh.devices.reshape(8, 4, 8, 2), ("z", "x", "y", "c"))
-    vel = ("x", "y", "c")
+    split = Mesh(mesh.devices.reshape(8, 2, 2, 8, 2), ("z", "x", "w", "y", "c"))
+    vel = ("x", "w", "y", "c")
     placed = (P(vel, "z"), P(None, None, "z"), P(None, "z"), P("z", None, None), P(None, "z"))
     return jax.shard_map(
         per_device,

time: 142 us -> 142 us (level)
  starting transfers between devices: 25.8 us -> 22 us
  blocking collectives: 64.5 us -> 67.5 us
    all_to_all x1, waiting for transfers between devices: 0.01 us -> 3.58 us  [per_device(): lax.all_to_all(value, 'z', 0, 0, tiled=True).reshape(GROUPS * NODES, CELLS)]
    ppermute x2 -> x1, waiting for transfers between devices: 5.33 us -> 2.04 us  [per_device(): moments = moments + lax.ppermute(moments, 'w', [(0, 1), (1, 0)])]
    all_to_all x3, blocking collectives: 42.4 us -> 45.4 us  [spread(): return lax.all_to_all(copies, axes, 0, 0, tiled=True)]
    ppermute x2 -> x1, starting transfers between devices: 5.23 us -> 2.35 us  [per_device(): moments = moments + lax.ppermute(moments, 'w', [(0, 1), (1, 0)])]
  transfers between devices with their start and end apart: 5 -> 4, of which waited for: 4 -> 4; matrix products, arithmetic and copies ran while one was open for 0% -> 0% of each run, Pallas kernels for 0% -> 0%
where the time goes in v9:
time: 142 us; the launch traced here: 141 us
  blocking collectives  67.5 us (48%)
  waiting for transfers between devices  28.5 us (20%)
  starting transfers between devices  22 us (15%)
  Pallas kernels  20.7 us (15%)
    all_to_all x3, blocking collectives, spread(): return lax.all_to_all(copies, axes, 0, 0, tiled=True)  45.4 us
    all_to_all x2, blocking collectives, per_device(): mine = jnp.sum(lax.all_to_all(sums, ('c', 'z'), 0, 0, tiled=True), axis=0)  22.1 us
    all_to_all x1, waiting for transfers between devices, per_device(): block = lax.all_to_all(block, 'z', 0, 0, tiled=True)  22.1 us
    all_to_all x1, starting transfers between devices, per_device(): block = lax.all_to_all(block, 'z', 0, 0, tiled=True)  10.9 us
    pallas_call x1, Pallas kernels, per_device(): pl.pallas_call(second_kernel, out_shape=(shape(GROUPS, NODES, CELLS), sha...  7.14 us
    pallas_call x1, Pallas kernels, per_device(): pl.pallas_call(first_kernel, out_shape=(shape(GROUPS, FACES, CELLS, dtype...  6.02 us
    ppermute x1, starting transfers between devices, per_device(): other = lax.ppermute(fields, 'c', [(0, 1), (1, 0)])  5.29 us
    pallas_call x1, Pallas kernels, per_device(): pl.pallas_call(fields_kernel, out_shape=shape(24, LANES), in_specs=[VMEM]...  4.84 us
  transfers between devices with their start and end apart: 4, of which 4 were waited for; matrix products, arithmetic and copies ran while one was open for 0% of the time, Pallas kernels for 0%

profile of v9, /device:TPU:1, one launch (start us, length us, event | category | flops | bytes accessed | tf_op | source)
XLA Modules:
  0.0 141.0 jit_solution(10555886419917769014)
XLA Ops:
  0.6 2.1 %shard_map.68 = f32[8,88,256]{2,1,0:T(8,128)} custom-call(f32[512,256]{1,0:T(8,128)} %value_hbm.1, s32[4,256]{1,0:T(4,128)} %adjacency_hbm.1, f32[3,4,256]{2,1,0:T(4,128)} %bitcast.8, s32[1,8,256]{2,1,0:T(8,128)} %send_hbm.1, s32[1,8]{1,0:T(1,128)} %bitcast.9), custom_call_target="tpu_custom_call" | custom-call | tf_op jit(solution)/shard_map/pallas_call | solution.py:462
  2.7 10.9 %all-to-all-start = ((f32[8,88,256]{2,1,0:T(8,128)}), f32[8,88,256]{2,1,0:T(8,128)S(1)}, u32[]{:S(2)}, u32[]{:S(2)}) async-start(f32[8,88,256]{2,1,0:T(8,128)} %shard_map.68), calls=%async_computation | async-start | bytes 1441792 | tf_op jit(solution)/shard_map/all_to_all | solution.py:477
  13.6 0.1 fusion.2.node_ref
  13.7 22.1 %all-to-all-done.block_ref = f32[8,88,256]{2,1,0:T(8,128)S(1)} async-done(((f32[8,88,256]{2,1,0:T(8,128)}), f32[8,88,256]{2,1,0:T(8,128)S(1)}, u32[]{:S(2)}, u32[]{:S(2)}) %all-to-all-start) | async-done | bytes 720928 | tf_op jit(solution)/shard_map/all_to_all | solution.py:477
  35.8 6.0 %shard_map.69 = (s32[8,4,256]{2,1,0:T(4,128)S(1)}, f32[8,64,256]{2,1,0:T(8,128)S(1)}, f32[16,4,384]{2,1,0:T(4,128)S(1)}) custom-call(f32[1,4]{1,0:T(1,128)S(1)} %fusion.2.node_ref, f32[8,88,256]{2,1,0:T(8,128)S(1)} %all-to-all-done.block_ref), custom_call_target="tpu_custom_call" | custom-call | tf_op jit(solution)/shard_map/pallas_call | solution.py:479
  41.8 10.3 %all_to_all.35 = f32[16,4,384]{2,1,0:T(4,128)S(1)} all-to-all(f32[16,4,384]{2,1,0:T(4,128)S(1)} %get-tuple-element.9), channel_id=1, replica_groups=mesh['z'=8,'x'=2,'w'=2,'y'=8,'c'=2] {'c','z'}, dimensions={0} | all-to-all | bytes 196608 | tf_op jit(solution)/shard_map/all_to_all | solution.py:492
  52.1 18.9 %all_to_all.36.parts_ref = f32[32,4,384]{2,1,0:T(4,128)S(1)} all-to-all(f32[32,4,384]{2,1,0:T(4,128)S(1)} %broadcast_in_dim.9), channel_id=1, replica_groups=mesh['z'=8,'x'=2,'w'=2,'y'=8,'c'=2] {'x','w','y'}, dimensions={0} | all-to-all | bytes 393216 | tf_op jit(solution)/shard_map/all_to_all | solution.py:452
  71.0 4.8 %shard_map.70 = f32[24,128]{1,0:T(8,128)S(1)} custom-call(f32[32,4,384]{2,1,0:T(4,128)S(1)} %all_to_all.36.parts_ref), custom_call_target="tpu_custom_call" | custom-call | tf_op jit(solution)/shard_map/pallas_call | solution.py:493
  75.9 14.1 %all_to_all.37.params_ref = f32[16,24,128]{2,1,0:T(8,128)S(1)} all-to-all(f32[16,24,128]{2,1,0:T(8,128)S(1)} %broadcast_in_dim.10), channel_id=1, replica_groups=mesh['z'=8,'x'=2,'w'=2,'y'=8,'c'=2] {'c','z'}, dimensions={0} | all-to-all | bytes 393216 | tf_op jit(solution)/shard_map/all_to_all | solution.py:452
  90.0 7.1 %shard_map.71 = (f32[8,64,256]{2,1,0:T(8,128)}, f32[16,8,128]{2,1,0:T(8,128)S(1)}) custom-call(f32[1,4]{1,0:T(1,128)S(1)} %fusion.2.node_ref, f32[8,88,256]{2,1,0:T(8,128)S(1)} %all-to-all-done.block_ref, s32[8,4,256]{2,1,0:T(4,128)S(1)} %get-tuple-element.7.near_ref, f32[8,64,256]{2,1,0:T(8,128)S(1)} %get-tuple-element.8.flux_ref, ...), custom_call_target="tpu_custom_call" | custom-call | tf_op jit(solution)/shard_map/pallas_call | solution.py:503
  97.1 11.8 %all_to_all.38 = f32[16,8,128]{2,1,0:T(8,128)S(1)} all-to-all(f32[16,8,128]{2,1,0:T(8,128)S(1)} %get-tuple-element.11), channel_id=1, replica_groups=mesh['z'=8,'x'=2,'w'=2,'y'=8,'c'=2] {'c','z'}, dimensions={0} | all-to-all | bytes 131072 | tf_op jit(solution)/shard_map/all_to_all | solution.py:513
  109.0 12.4 %all_to_all.39.parts_ref = f32[16,8,128]{2,1,0:T(8,128)S(1)} all-to-all(f32[16,8,128]{2,1,0:T(8,128)S(1)} %broadcast_in_dim.11), channel_id=1, replica_groups=mesh['z'=8,'x'=2,'w'=2,'y'=8,'c'=2] {'x','y'}, dimensions={0} | all-to-all | bytes 131072 | tf_op jit(solution)/shard_map/all_to_all | solution.py:452
  121.4 3.5 %all-to-all-start.4 = ((f32[8,64,256]{2,1,0:T(8,128)}), f32[8,64,256]{2,1,0:T(8,128)S(1)}, u32[]{:S(2)}, u32[]{:S(2)}) async-start(f32[8,64,256]{2,1,0:T(8,128)} %get-tuple-element.10), calls=%async_computation.4 | async-start | bytes 1048576 | tf_op jit(solution)/shard_map/all_to_all | solution.py:512
  124.9 0.6 shard_map.72
  125.5 2.3 %collective-permute-start = (f32[16,128]{1,0:T(8,128)S(1)}, f32[16,128]{1,0:T(8,128)S(1)}, u32[]{:S(2)}, u32[]{:S(2)}) collective-permute-start(f32[16,128]{1,0:T(8,128)S(1)} %shard_map.72), channel_id=1, source_target_pairs={{0,16},{16,0},{1,17},{17,1},{2,18},{18,2},{3,19},{19,3},{4,20},{20... | collective-permute-start | bytes 24584 | tf_op jit(solution)/shard_map/ppermute | solution.py:521
  127.8 2.0 %collective-permute-done = f32[16,128]{1,0:T(8,128)S(1)} collective-permute-done((f32[16,128]{1,0:T(8,128)S(1)}, f32[16,128]{1,0:T(8,128)S(1)}, u32[]{:S(2)}, u32[]{:S(2)}) %collective-permute-start) | collective-permute-done | bytes 8224 | tf_op jit(solution)/shard_map/ppermute | solution.py:521
  129.9 5.3 %collective-permute-start.1 = (f32[16,128]{1,0:T(8,128)S(1)}, f32[16,128]{1,0:T(8,128)S(1)}, u32[]{:S(2)}, u32[]{:S(2)}) collective-permute-start(f32[16,128]{1,0:T(8,128)S(1)} %shard_map.73), channel_id=1, source_target_pairs={{0,1},{1,0},{2,3},{3,2},{4,5},{5,4},{6,7},{7,6},{8,9},{9,8},{10,11... | collective-permute-start | bytes 24584 | tf_op jit(solution)/shard_map/ppermute | solution.py:529
  135.2 0.8 collective-permute-done.1
  136.0 0.6 fusion
  136.6 3.6 %all-to-all-done.4 = f32[8,64,256]{2,1,0:T(8,128)S(1)} async-done(((f32[8,64,256]{2,1,0:T(8,128)}), f32[8,64,256]{2,1,0:T(8,128)S(1)}, u32[]{:S(2)}, u32[]{:S(2)}) %all-to-all-start.4) | async-done | bytes 524320 | tf_op jit(solution)/shard_map/all_to_all | solution.py:512
  140.2 0.8 copy.8
  (7 shorter events, 0.1 us)
Async XLA Ops:
  2.7 33.0 %all-to-all-start = ((f32[8,88,256]{2,1,0:T(8,128)}), f32[8,88,256]{2,1,0:T(8,128)S(1)}, u32[]{:S(2)}, u32[]{:S(2)}) async-start(f32[8,88,256]{2,1,0:T(8,128)} %shard_map.68), calls=%async_computation | async-start | bytes 1441792 | tf_op jit(solution)/shard_map/all_to_all | solution.py:477
  121.4 18.8 %all-to-all-start.4 = ((f32[8,64,256]{2,1,0:T(8,128)}), f32[8,64,256]{2,1,0:T(8,128)S(1)}, u32[]{:S(2)}, u32[]{:S(2)}) async-start(f32[8,64,256]{2,1,0:T(8,128)} %get-tuple-element.10), calls=%async_computation.4 | async-start | bytes 1048576 | tf_op jit(solution)/shard_map/all_to_all | solution.py:512
  125.5 4.4 %collective-permute-start = (f32[16,128]{1,0:T(8,128)S(1)}, f32[16,128]{1,0:T(8,128)S(1)}, u32[]{:S(2)}, u32[]{:S(2)}) collective-permute-start(f32[16,128]{1,0:T(8,128)S(1)} %shard_map.72), channel_id=1, source_target_pairs={{0,16},{16,0},{1,17},{17,1},{2,18},{18,2},{3,19},{19,3},{4,20},{20... | collective-permute-start | bytes 24584 | tf_op jit(solution)/shard_map/ppermute | solution.py:521
  129.9 6.1 %collective-permute-start.1 = (f32[16,128]{1,0:T(8,128)S(1)}, f32[16,128]{1,0:T(8,128)S(1)}, u32[]{:S(2)}, u32[]{:S(2)}) collective-permute-start(f32[16,128]{1,0:T(8,128)S(1)} %shard_map.73), channel_id=1, source_target_pairs={{0,1},{1,0},{2,3},{3,2},{4,5},{5,4},{6,7},{7,6},{8,9},{9,8},{10,11... | collective-permute-start | bytes 24584 | tf_op jit(solution)/shard_map/ppermute | solution.py:529
